TPU v7x, 256 devices: a whole 4x4x8 slice. The times are simulated.
256 devices in a mesh: pts: 32 (over x, z_hi, core), ctr: 8 (over z_lo, y).
Axes of the slice: x: 4, y: 4, z: 8 (z_hi: 4, z_lo: 2; z = z_hi * 2 + z_lo), core: 2. Of those that a mesh axis runs over, the one named last changes fastest.
Arguments:
- embeddings: bfloat16 [16384, 128], P('pts'), may hold values from -1.1953125 to 1.1953125
- centres: bfloat16 [65536, 128], P('ctr'), may hold values from -1.1953125 to 1.1953125
- prior_freq: float32 [65536], P('ctr'), may hold values from 0.1 to 1
Outputs:
- embed_grad: float32 [16384, 128], P('pts')
- centre_grad: float32 [8, 8192, 128], P('ctr', 'pts')
All inputs are finite; a program needn't handle non-finite values.
Results may differ from a plain program's by a relative error of at most 0.0003.
Values sent between devices are 32-bit elements; how exact they have to be, the bound alone decides.
No kernel may reach another device: no remote copies, remote signals or barrier semaphores. Data moves between devices by JAX's collectives and lax.ppermute only.
A program may use at most 64 MiB of HBM per device.

v0:
```python
import functools

import jax
import jax.numpy as jnp
from jax import lax
from jax.experimental import pallas as pl
from jax.experimental.pallas import tpu as pltpu
from jax.sharding import PartitionSpec as P

SIDE = 4
CORES = 2
LANES = 128
ONES = 16
SCALE = 128.0
MIB = 2**20
HINT = 10**10
HOPS = (2, 1, 3, 0)
F32 = jnp.float32
BF16 = jnp.bfloat16


def tile_lanes(column, width):
    return jnp.concatenate([column] * (width // LANES), axis=1)


def spread(row):
    return jnp.broadcast_to(row, (LANES, row.shape[1])).T


def four(refs):
    a, b, c, d = refs
    return (a[...] + b[...]) + (c[...] + d[...])


def block_rows(block, inner, core):
    return pl.ds(pl.multiple_of((block * CORES + core) * inner, inner), inner)


def kern_block(za, zn, ct, norms):
    cross = jnp.dot(za[...], ct, preferred_element_type=F32)
    return 1.0 / (cross + norms + tile_lanes(zn[...], ct.shape[1]))


def kern_setup(part, za, zn):
    zn[...] = jnp.broadcast_to(jnp.sum(part * part, axis=1, keepdims=True) + 1.0, zn.shape)
    za[...] = (-2.0 * part).astype(BF16)


def lane_sums(total, kern):
    for g in range(kern.shape[1] // LANES):
        total = total + kern[:, g * LANES : (g + 1) * LANES]
    return total


def own_body(z_ref, c_ref, kern_ref, row_ref, ct_ref, norm_ref, za, zn):
    half, count = kern_ref.shape
    inner = count // (SIDE * SIDE)
    core = lax.axis_index("core")
    kern_setup(z_ref[...], za, zn)
    total = jnp.zeros((half, LANES), F32)
    for b in range(count // inner):
        at = slice(b * inner, (b + 1) * inner)
        ct = c_ref[block_rows(b, inner, core), :].astype(F32).T
        norms = jnp.sum(ct * ct, axis=0, keepdims=True)
        ct = ct.astype(BF16)
        ct_ref[:, at] = ct
        norm_ref[:, at] = norms
        kern = kern_block(za, zn, ct, norms)
        kern_ref[:, at] = kern
        total = lane_sums(total, kern)
    row_ref[...] = jnp.sum(total.T, axis=0, keepdims=True)


def other_body(zo_ref, ct_ref, norm_ref, row_ref, kern_ref, rows_ref, za, zn):
    half, count = kern_ref.shape
    step = 256
    rows_ref[:1] = row_ref[...]
    kern_setup(zo_ref[...], za, zn)
    total = jnp.zeros((half, LANES), F32)
    for b in range(count // step):
        at = slice(b * step, (b + 1) * step)
        kern = kern_block(za, zn, ct_ref[:, at], norm_ref[:, at])
        kern_ref[:, at] = kern
        total = lane_sums(total, kern)
    rows_ref[1:] = jnp.sum(total.T, axis=0, keepdims=True)


def swap_core_body(mine, theirs, out):
    out[:1] = mine[:1] + theirs[1:]
    out[1:] = mine[1:] + theirs[:1]


def swap_add_body(mine, theirs, out):
    for n in range(out.shape[0]):
        out[n, :1] = mine[:1] + theirs[1:]
        out[n, 1:] = mine[1:] + theirs[:1]


def summed(ref):
    total = ref[0]
    for n in range(1, ref.shape[0]):
        total = total + ref[n]
    return total


def add_body(*refs):
    refs[-1][...] = four(refs[:-1]) if len(refs) == 5 else refs[0][...] + refs[1][...]


def freq_body(own_ref, other_ref, rows_ref, f_ref, rinv_ref, scale_ref):
    half, count = own_ref.shape
    rinv = 1.0 / summed(rows_ref)
    rinv_ref[...] = rinv
    step, rows = 2048, 64
    scales = [spread(rinv[p : p + 1]) for p in range(CORES)]
    for p in range(CORES):
        scale_ref[p] = scales[p]
    for base in range(0, count, step):
        at = slice(base, base + step)
        total = jnp.zeros((8, step), F32)
        for p, kern_ref in enumerate((own_ref, other_ref)):

            def add_rows(n, total, p=p, kern_ref=kern_ref, at=at):
                for i in range(0, rows, 8):
                    tile = pl.ds(pl.multiple_of(n * rows + i, 8), 8)
                    total = total + kern_ref[tile, at] * tile_lanes(scale_ref[p, tile, :], step)
                return total

            total = lax.fori_loop(0, half // rows, add_rows, total)
        f_ref[:, at] = jnp.sum(total, axis=0, keepdims=True)


def target_body(own_ref, other_ref, f0, f1, f2, f3, prior_ref, t_ref, finv_ref, acc):
    half, count = own_ref.shape
    inner = count // (SIDE * SIDE)
    core = lax.axis_index("core")
    prior = [prior_ref[:, block_rows(b, inner, core)] for b in range(count // inner)]
    finv_ref[...] = 1.0 / (four((f0, f1, f2, f3)) + jnp.concatenate(prior, axis=1))
    step = 64
    for row, kern_ref in ((0, own_ref), (1, other_ref)):

        @pl.loop(0, half // (2 * step))
        def _(n):
            for i in range(2):
                tile = pl.ds(pl.multiple_of((2 * n + i) * step, step), step)
                total = jnp.zeros((step, LANES), F32)
                for g in range(count // LANES):
                    at = slice(g * LANES, (g + 1) * LANES)
                    kern = kern_ref[tile, at]
                    total = total + kern * kern * finv_ref[:, at]
                acc[tile, :] = total

        t_ref[row : row + 1] = jnp.sum(acc[...].T, axis=0, keepdims=True)


def two_terms(value):
    high = value.astype(BF16)
    return high, (value - high.astype(F32)).astype(BF16)


def weights(kern, finv, tinv, rinv):
    return two_terms(kern * kern * (kern * finv * tinv - rinv))


def grad_setup(tinv, rinv_ref, points, zt, ts, rs):
    for p in range(CORES):
        ts[p] = spread(tinv[p : p + 1])
        rs[p] = spread(rinv_ref[p : p + 1])
        zt[p, :LANES] = (-SCALE * points[p].T).astype(BF16)
        zt[p, LANES:] = jnp.full((ONES, points[p].shape[0]), SCALE, BF16)


def grad_weights(block, kerns, finv_ref, ts, rs, p):
    inner = kerns[p].shape[1] // (SIDE * SIDE)
    at = pl.ds(pl.multiple_of(block * inner, inner), inner)
    return weights(
        kerns[p][:, at], finv_ref[:, at], tile_lanes(ts[p], inner), tile_lanes(rs[p], inner)
    )


def grad_block(parts, zt, c):
    sums = jnp.zeros((LANES + ONES, c.shape[0]), F32)
    for p, terms in enumerate(parts):
        for term in terms:
            sums += jnp.dot(zt[p], term, preferred_element_type=F32)
    return sums[:LANES] + sums[LANES : LANES + 1] * c.astype(F32).T


def embed_sums(kern_ref, c_ref, out, power):
    half, count = kern_ref.shape
    inner = count // (SIDE * SIDE)
    core = lax.axis_index("core")
    step = 2 * SIDE
    out[...] = jnp.zeros_like(out)

    @pl.loop(0, count // (inner * step))
    def _(n):
        total = out[...]
        for i in range(step):
            b = n * step + i
            at = pl.ds(pl.multiple_of(b * inner, inner), inner)
            c = c_ref[block_rows(b, inner, core), :]
            wide = jnp.concatenate([c, jnp.ones((inner, LANES), BF16)], axis=1)
            for term in two_terms(power(kern_ref[:, at], at)):
                total += jnp.dot(term, wide, preferred_element_type=F32)
        out[...] = total


def square_body(kern_ref, c_ref, out):
    embed_sums(kern_ref, c_ref, out, lambda kern, at: kern * kern)


def cube_body(kern_ref, finv_ref, c_ref, out):
    embed_sums(kern_ref, c_ref, out, lambda kern, at: kern * kern * (kern * finv_ref[:, at]))


def embed_body(a0, a1, b0, b1, t0, t1, t2, t3, rinv_ref, z_ref, zo_ref, own, other):
    tinv = 1.0 / four((t0, t1, t2, t3))
    points = (z_ref[...].astype(F32), zo_ref[...])
    for p, (cubes, squares, out) in enumerate(((a0, b0, own), (a1, b1, other))):
        ts, rs = spread(tinv[p : p + 1]), spread(rinv_ref[p : p + 1])
        total = ts * cubes[:, LANES:] - rs * squares[:, LANES:]
        moved = ts * cubes[:, :LANES] - rs * squares[:, :LANES]
        out[...] = SCALE * (total * points[p] - moved)


def centre_grads(s, refs, tinv, outs):
    kerns, rinv_ref, finv_ref, z_ref, zo_ref, c_ref, zt, ts, rs = refs
    points = (z_ref[...].astype(F32), zo_ref[...])
    grad_setup(tinv, rinv_ref, points, zt, ts, rs)
    core, x, h = lax.axis_index("core"), lax.axis_index("x"), lax.axis_index("h")
    inner = kerns[0].shape[1] // (SIDE * SIDE)
    for step, out in zip(s, outs):
        for n, hop in enumerate(HOPS):
            block = (x ^ step) * SIDE + (h ^ hop)
            parts = [grad_weights(block, kerns, finv_ref, ts, rs, p) for p in range(CORES)]
            grad = grad_block(parts, zt, c_ref[block_rows(block, inner, core), :])
            at = slice(n * inner, (n + 1) * inner)
            if len(out) == 1:
                out[0][:, at] = grad
            else:
                cut = out[0].shape[0]
                out[0][:, at] = grad[:cut]
                out[1][:, at] = grad[cut:]


def far_body(own, other, rinv, finv, t0, t1, t2, t3, z, zo, c, low, high, tinv_ref, zt, ts, rs):
    tinv = 1.0 / four((t0, t1, t2, t3))
    tinv_ref[...] = tinv
    refs = ((own, other), rinv, finv, z, zo, c, zt, ts, rs)
    centre_grads((2,), refs, tinv, ((low, high),))


def mid_body(own, other, rinv, finv, tinv, z, zo, c, first, third, zt, ts, rs):
    refs = ((own, other), rinv, finv, z, zo, c, zt, ts, rs)
    centre_grads((1, 3), refs, tinv[...], ((first,), (third,)))


def near_body(own, other, rinv, finv, tinv, z, zo, c, near, zt, ts, rs):
    refs = ((own, other), rinv, finv, z, zo, c, zt, ts, rs)
    centre_grads((0,), refs, tinv[...], ((near,),))


def second_body(base, first, third, low, high, to_first, to_third):
    cut = low.shape[0]
    at = slice(base, base + to_first.shape[1])
    to_first[:cut] = first[:cut, at]
    to_first[cut:] = first[cut:, at] + high[:, at]
    to_third[:cut] = third[:cut, at] + low[:, at]
    to_third[cut:] = third[cut:, at]


def split_body(base, near, first, third, *outs):
    inner = outs[0].shape[1]
    for n, out in enumerate(outs):
        at = slice(n * inner, (n + 1) * inner)
        out[...] = near[:, base + n * inner : base + (n + 1) * inner] + first[:, at] + third[:, at]


def final_body(p0, p1, p2, p3, mine, theirs, grad, embed):
    grad[...] = four((p0, p1, p2, p3)).T
    embed[...] = mine[...] + theirs[...]


VMEM = pl.BlockSpec(memory_space=pltpu.VMEM)
ANY = pl.BlockSpec(memory_space=pl.ANY)


def call(body, outs, *args, scratch=(), limit=2, name=None, flops=0, after=()):
    used = len(args)

    def kernel(*refs):
        body(*refs[:used], *refs[used + len(after) :])

    args = (*args, *after)
    shapes = tuple(o if hasattr(o, "dtype") else jax.ShapeDtypeStruct(o, F32) for o in outs)
    moved = sum(a.size * a.dtype.itemsize for a in args)
    out = pl.pallas_call(
        kernel,
        out_shape=shapes,
        in_specs=[VMEM] * used + [ANY] * len(after),
        out_specs=tuple(VMEM for _ in outs),
        scratch_shapes=scratch,
        compiler_params=pltpu.CompilerParams(vmem_limit_bytes=limit * MIB),
        cost_estimate=pl.CostEstimate(flops=flops, bytes_accessed=moved, transcendentals=0),
        name=name,
    )(*args)
    return out if len(out) > 1 else out[0]


def swap(v, axis, s):
    return lax.ppermute(v, axis, [(i, i ^ s) for i in range(lax.axis_size(axis))])


def around(pieces, axis):
    return [pieces[0]] + [swap(pieces[s], axis, s) for s in (1, 3, 2)]


def body(embeddings, centres, prior_freq):
    half, width = embeddings.shape
    count = centres.shape[0] // CORES
    inner = count // (SIDE * SIDE)
    prior = prior_freq.reshape(1, centres.shape[0])
    rows = (CORES, half)

    def over_ctr(v):
        parts = lax.axis_size("zl") * lax.axis_size("y")
        v = call(swap_add_body, [(parts, *rows)], v, swap(v, "core", 1), name="sum_core")
        return lax.all_to_all(v, ("zl", "y"), 0, 0)

    z_own = embeddings.astype(F32)
    z_other = swap(z_own, "core", 1)
    kern_scratch = [pltpu.VMEM((half, width), BF16), pltpu.VMEM((half, LANES), F32)]
    kern_own, row, ct, norms = call(
        own_body,
        [(half, count), (1, half), jax.ShapeDtypeStruct((width, count), BF16), (1, count)],
        z_own,
        centres,
        scratch=kern_scratch,
        limit=16,
        name="kern_own",
    )
    kern_other, row = call(
        other_body,
        [(half, count), rows],
        z_other,
        ct,
        norms,
        row,
        scratch=kern_scratch,
        limit=16,
        name="kern_other",
    )
    freq, rinv = call(
        freq_body,
        [(1, count), rows],
        kern_own,
        kern_other,
        over_ctr(row),
        scratch=[pltpu.VMEM((CORES, half, LANES), F32)],
        limit=20,
        name="freq",
    )
    kerns = (kern_own, kern_other)
    sums = (half, 2 * LANES)
    work = 4 * half * count * 2 * LANES
    squares = [
        call(square_body, [sums], kern, centres, limit=20, name="squares", flops=work)
        for kern in kerns
    ]
    freq = call(
        add_body, [freq.shape], *around([freq] * SIDE, "x"), name="sum_x", after=squares[:1]
    )
    freq = around([freq] * SIDE, "h")
    target, finv = call(
        target_body,
        [rows, (1, count)],
        *kerns,
        *freq,
        prior,
        scratch=[pltpu.VMEM((half, LANES), F32)],
        limit=20,
        name="target",
        after=squares[1:],
    )
    cubes = [
        call(cube_body, [sums], kern, finv, centres, limit=20, name="cubes", flops=work)
        for kern in kerns
    ]
    target = call(swap_core_body, [rows], target, swap(target, "core", 1), name="target_core")
    target = call(add_body, [rows], target, swap(target, "zl", 1), name="target_zl")
    target = around([target] * SIDE, "y")

    setup = [
        pltpu.VMEM((CORES, width + ONES, half), BF16),
        pltpu.VMEM((CORES, half, LANES), F32),
        pltpu.VMEM((CORES, half, LANES), F32),
    ]
    piece, part, pair = (width, SIDE * inner), (width // 2, SIDE * inner), (width, 2 * inner)
    base = (*kerns, rinv, finv)
    data = (embeddings, z_other, centres)
    low, high, tinv = call(
        far_body, [part, part, rows], *base, *target, *data, scratch=setup, limit=24, name="grad_far"
    )
    low, high = swap(low, "x", 1), swap(high, "x", 3)
    mine, other = call(
        embed_body,
        [(half, width)] * 2,
        *cubes,
        *squares,
        *target,
        rinv,
        embeddings,
        z_other,
        limit=8,
        name="embed_part",
    )
    first, third = call(
        mid_body, [piece, piece], *base, tinv, *data, scratch=setup, limit=24, name="grad_mid"
    )
    near = call(near_body, [piece], *base, tinv, *data, scratch=setup, limit=24, name="grad_near")

    def second(start, name, after=()):
        to_first, to_third = call(
            functools.partial(second_body, start),
            [pair] * 2,
            first,
            third,
            low,
            high,
            name=name,
            flops=HINT,
            after=after,
        )
        return swap(to_first, "x", 1), swap(to_third, "x", 3)

    first_a, third_a = second(0, "second_a")
    first_b, third_b = second(2 * inner, "second_b", after=[near])

    embed = call(add_body, [mine.shape], mine, swap(other, "core", 1), name="embed_core")
    embed = call(add_body, [mine.shape], embed, swap(embed, "zl", 1), name="embed_zl")
    embed = call(add_body, [mine.shape], embed, swap(embed, "y", 1), name="embed_y")
    embed = (embed, swap(embed, "y", 3))

    block = (width, inner)
    def split(start, pieces, name, after=()):
        return call(
            functools.partial(split_body, start),
            [block] * 2,
            near,
            *pieces,
            name=name,
            flops=HINT,
            after=after,
        )

    far2, far1 = split(0, (first_a, third_a), "split_a")
    h2, h1 = swap(far2, "h", 2), swap(far1, "h", 1)
    h3, h0 = split(2 * inner, (first_b, third_b), "split_b", after=[far2])
    grad, embed = call(
        final_body,
        [(inner, width), (half, width)],
        h0,
        h1,
        h2,
        swap(h3, "h", 3),
        *embed,
        name="final",
        flops=HINT,
    )
    return embed, grad.reshape(1, inner, width)


def solution(mesh):
    names = ("x", "h", "core", "zl", "y")
    grid = jax.sharding.Mesh(mesh.devices.reshape(SIDE, SIDE, CORES, CORES, SIDE), names)
    pts, ctr = names[:3], names[3:]
    in_specs = (P(pts, None), P(ctr, None), P(ctr))
    out_specs = (P(pts, None), P(ctr, pts, None))
    return jax.shard_map(body, mesh=grid, in_specs=in_specs, out_specs=out_specs, check_vma=False)
```

profile of v0, /device:TPU:32, one launch (start us, length us, event | category | flops | bytes accessed | tf_op | source)
XLA Modules:
  0.0 96.4 jit_solution(9327445982718775872)
XLA Ops:
  1.7 1.6 %copy-done = bf16[8192,128]{1,0:T(8,128)(2,1)S(1)} copy-done((bf16[8192,128]{1,0:T(8,128)(2,1)S(1)}, bf16[8192,128]{1,0:T(8,128)(2,1)}, u32[]{:S(2)}) %copy-start) | copy-done | bytes 2097176
  3.3 2.2 %kern_own.1 = (f32[512,4096]{1,0:T(8,128)S(1)}, f32[1,512]{1,0:T(1,128)S(1)}, bf16[128,4096]{1,0:T(8,128)(2,1)S(1)}, f32[1,4096]{1,0:T(1,128)S(1)}) custom-call(f32[512,128]{1,0:T(8,128)S(1)} %convert_element_type.3.refs_0_, bf16[8192,128]{1,0:T(8,128)(2,1)S(1)} %copy-done), custom_call_target="tpu_custom_call" | custom-call | bytes 2359296 | tf_op jit(solution)/shard_map/kern_own/pallas_call | solution.py:298
  5.5 1.7 %kern_other.1 = (f32[512,4096]{1,0:T(8,128)S(1)}, f32[2,512]{1,0:T(2,128)S(1)}) custom-call(f32[512,128]{1,0:T(8,128)S(1)} %collective-permute-done.refs_0_.refs_9_.refs_6_.refs_10_, bf16[128,4096]{1,0:T(8,128)(2,1)S(1)} %get-tuple-element.30.refs_1_, f32[1,4096]{1,0:T(1,128)S(1)} %get-tuple-element.31.refs_2_, f32[1,512]{1,0:T(1,128)S(1)} %get-tuple-element.32.refs_3_), custom_call_target="tpu_custom_call" | custom-call | bytes 1329152 | tf_op jit(solution)/shard_map/kern_other/pallas_call | solution.py:298
  8.6 10.6 %all_to_all.5.refs_2_ = f32[8,2,512]{2,1,0:T(2,128)S(1)} all-to-all(f32[8,2,512]{2,1,0:T(2,128)S(1)} %sum_core.1), channel_id=1, replica_groups=mesh['x'=4,'h'=4,'core'=2,'zl'=2,'y'=4] {'zl','y'}, dimensions={0} | all-to-all | bytes 65536 | tf_op jit(solution)/shard_map/all_to_all | solution.py:329
  20.7 3.1 %collective-permute-start.4 = (f32[1,4096]{1,0:T(1,128)S(1)}, f32[1,4096]{1,0:T(1,128)S(1)}, u32[]{:S(2)}, u32[]{:S(2)}) collective-permute-start(f32[1,4096]{1,0:T(1,128)S(1)} %get-tuple-element.36.refs_0_), channel_id=1, source_target_pairs={{0,128},{64,192},{128,0},{192,64},{1,129},{65,193},{129,1},{193,65... | collective-permute-start | bytes 49160 | tf_op jit(solution)/shard_map/ppermute | solution.py:312
  24.9 2.6 %squares.2.refs_4_.refs_2_ = f32[512,256]{1,0:T(8,128)S(1)} custom-call(f32[512,4096]{1,0:T(8,128)S(1)} %get-tuple-element.29.refs_0_, bf16[8192,128]{1,0:T(8,128)(2,1)S(1)} %copy-done.1), custom_call_target="tpu_custom_call" | custom-call | flops 2147483648 | bytes 10485760 | tf_op jit(solution)/shard_map/squares/pallas_call | solution.py:298
  28.7 6.4 %collective-permute-start.7 = (f32[1,4096]{1,0:T(1,128)S(1)}, f32[1,4096]{1,0:T(1,128)S(1)}, u32[]{:S(2)}, u32[]{:S(2)}) collective-permute-start(f32[1,4096]{1,0:T(1,128)S(1)} %sum_x.1.refs_2_), channel_id=1, source_target_pairs={{0,32},{16,48},{32,0},{48,16},{1,33},{17,49},{33,1},{49,17},{2,34}... | collective-permute-start | bytes 49160 | tf_op jit(solution)/shard_map/ppermute | solution.py:312
  36.6 2.6 %squares.3.refs_7_.refs_3_ = f32[512,256]{1,0:T(8,128)S(1)} custom-call(f32[512,4096]{1,0:T(8,128)S(1)} %get-tuple-element.33.refs_1_.refs_0_, bf16[8192,128]{1,0:T(8,128)(2,1)S(1)} %copy-done.1), custom_call_target="tpu_custom_call" | custom-call | flops 2147483648 | bytes 10485760 | tf_op jit(solution)/shard_map/squares/pallas_call | solution.py:298
  39.2 1.8 %collective-permute-done.6.refs_4_ = f32[1,4096]{1,0:T(1,128)S(1)} collective-permute-done((f32[1,4096]{1,0:T(1,128)S(1)}, f32[1,4096]{1,0:T(1,128)S(1)}, u32[]{:S(2)}, u32[]{:S(2)}) %collective-permute-start.6) | collective-permute-done | bytes 16416 | tf_op jit(solution)/shard_map/ppermute | solution.py:312
  41.0 2.3 %target.1 = (f32[2,512]{1,0:T(2,128)S(1)}, f32[1,4096]{1,0:T(1,128)S(1)}) custom-call(f32[512,4096]{1,0:T(8,128)S(1)} %get-tuple-element.29.refs_0_, f32[512,4096]{1,0:T(8,128)S(1)} %get-tuple-element.33.refs_1_.refs_0_, f32[1,4096]{1,0:T(1,128)S(1)} %sum_x.1.refs_2_, f32[1,4096]{1,0:T(1,128)S(1)} %collective-permute-done.5.refs_3_, ...), custom_call_target="tpu_custom_call" | custom-call | bytes 17399808 | tf_op jit(solution)/shard_map/target/pallas_call | solution.py:298
  45.9 2.6 %cubes.3.refs_1_ = f32[512,256]{1,0:T(8,128)S(1)} custom-call(f32[512,4096]{1,0:T(8,128)S(1)} %get-tuple-element.33.refs_1_.refs_0_, f32[1,4096]{1,0:T(1,128)S(1)} %get-tuple-element.37.refs_3_.refs_1_, bf16[8192,128]{1,0:T(8,128)(2,1)S(1)} %copy-done.1), custom_call_target="tpu_custom_call" | custom-call | flops 2147483648 | bytes 10502144 | tf_op jit(solution)/shard_map/cubes/pallas_call | solution.py:298
  49.8 2.1 %collective-permute-start.11 = (f32[2,512]{1,0:T(2,128)S(1)}, f32[2,512]{1,0:T(2,128)S(1)}, u32[]{:S(2)}, u32[]{:S(2)}) collective-permute-start(f32[2,512]{1,0:T(2,128)S(1)} %target_zl.1.refs_4_), channel_id=1, source_target_pairs={{0,3},{1,2},{2,1},{3,0},{4,7},{5,6},{6,5},{7,4},{8,11},{9,10},{10,... | collective-permute-start | bytes 12296 | tf_op jit(solution)/shard_map/ppermute | solution.py:312
  52.2 2.6 %cubes.2.refs_0_ = f32[512,256]{1,0:T(8,128)S(1)} custom-call(f32[512,4096]{1,0:T(8,128)S(1)} %get-tuple-element.29.refs_0_, f32[1,4096]{1,0:T(1,128)S(1)} %get-tuple-element.37.refs_3_.refs_1_, bf16[8192,128]{1,0:T(8,128)(2,1)S(1)} %copy-done.1), custom_call_target="tpu_custom_call" | custom-call | flops 2147483648 | bytes 10502144 | tf_op jit(solution)/shard_map/cubes/pallas_call | solution.py:298
  56.0 1.7 %grad_far.1 = (f32[64,1024]{1,0:T(8,128)S(1)}, f32[64,1024]{1,0:T(8,128)S(1)}, f32[2,512]{1,0:T(2,128)S(1)}) custom-call(f32[512,4096]{1,0:T(8,128)S(1)} %get-tuple-element.29.refs_0_, f32[512,4096]{1,0:T(8,128)S(1)} %get-tuple-element.33.refs_1_.refs_0_, f32[2,512]{1,0:T(2,128)S(1)} %get-tuple-element.35.refs_2_.refs_8_, ...), custom_call_target="tpu_custom_call" | custom-call | bytes 19304448 | tf_op jit(solution)/shard_map/grad_far/pallas_call | solution.py:298
  58.6 2.1 %collective-permute-start.14 = (f32[64,1024]{1,0:T(8,128)S(1)}, f32[64,1024]{1,0:T(8,128)S(1)}, u32[]{:S(2)}, u32[]{:S(2)}) collective-permute-start(f32[64,1024]{1,0:T(8,128)S(1)} %get-tuple-element.43), channel_id=1, source_target_pairs={{0,192},{64,128},{128,64},{192,0},{1,193},{65,129},{129,65},{193,1... | collective-permute-start | bytes 786440 | tf_op jit(solution)/shard_map/ppermute | solution.py:312
  60.7 1.7 %grad_near.1.refs_4_.refs_0_ = f32[128,1024]{1,0:T(8,128)S(1)} custom-call(f32[512,4096]{1,0:T(8,128)S(1)} %get-tuple-element.29.refs_0_, f32[512,4096]{1,0:T(8,128)S(1)} %get-tuple-element.33.refs_1_.refs_0_, f32[2,512]{1,0:T(2,128)S(1)} %get-tuple-element.35.refs_2_.refs_8_, f32[1,4096]{1,0:T(1,128)S(1)} %get-tuple-element.37.refs_3_.refs_1_, ...), custom_call_target="tpu_custom_call" | custom-call | bytes 19292160 | tf_op jit(solution)/shard_map/grad_near/pallas_call | solution.py:298
  62.4 3.1 %grad_mid.1 = (f32[128,1024]{1,0:T(8,128)S(1)}, f32[128,1024]{1,0:T(8,128)S(1)}) custom-call(f32[512,4096]{1,0:T(8,128)S(1)} %get-tuple-element.29.refs_0_, f32[512,4096]{1,0:T(8,128)S(1)} %get-tuple-element.33.refs_1_.refs_0_, f32[2,512]{1,0:T(2,128)S(1)} %get-tuple-element.35.refs_2_.refs_8_, f32[1,4096]{1,0:T(1,128)S(1)} %get-tuple-element.37.refs_3_.refs_1_, ...), custom_call_target="tpu_custom_call" | custom-call | bytes 19292160 | tf_op jit(solution)/shard_map/grad_mid/pallas_call | solution.py:298
  66.6 1.7 %collective-permute-done.14.refs_3_ = f32[64,1024]{1,0:T(8,128)S(1)} collective-permute-done((f32[64,1024]{1,0:T(8,128)S(1)}, f32[64,1024]{1,0:T(8,128)S(1)}, u32[]{:S(2)}, u32[]{:S(2)}) %collective-permute-start.14) | collective-permute-done | bytes 262176 | tf_op jit(solution)/shard_map/ppermute | solution.py:312
  68.4 2.2 %collective-permute-start.18 = (f32[128,512]{1,0:T(8,128)S(1)}, f32[128,512]{1,0:T(8,128)S(1)}, u32[]{:S(2)}, u32[]{:S(2)}) collective-permute-start(f32[128,512]{1,0:T(8,128)S(1)} %get-tuple-element.47), channel_id=1, source_target_pairs={{0,192},{64,128},{128,64},{192,0},{1,193},{65,129},{129,65},{193,1... | collective-permute-start | bytes 786440 | tf_op jit(solution)/shard_map/ppermute | solution.py:312
  75.0 2.6 %collective-permute-done.17.refs_1_ = f32[128,512]{1,0:T(8,128)S(1)} collective-permute-done((f32[128,512]{1,0:T(8,128)S(1)}, f32[128,512]{1,0:T(8,128)S(1)}, u32[]{:S(2)}, u32[]{:S(2)}) %collective-permute-start.17) | collective-permute-done | bytes 262176 | tf_op jit(solution)/shard_map/ppermute | solution.py:312
  80.6 3.8 %collective-permute-start.20 = (f32[128,256]{1,0:T(8,128)S(1)}, f32[128,256]{1,0:T(8,128)S(1)}, u32[]{:S(2)}, u32[]{:S(2)}) collective-permute-start(f32[128,256]{1,0:T(8,128)S(1)} %get-tuple-element.48.refs_3_), channel_id=1, source_target_pairs={{0,32},{16,48},{32,0},{48,16},{1,33},{17,49},{33,1},{49,17},{2,34}... | collective-permute-start | bytes 393224 | tf_op jit(solution)/shard_map/ppermute | solution.py:312
  87.1 2.2 %collective-permute-done.19.refs_1_ = f32[128,256]{1,0:T(8,128)S(1)} collective-permute-done((f32[128,256]{1,0:T(8,128)S(1)}, f32[128,256]{1,0:T(8,128)S(1)}, u32[]{:S(2)}, u32[]{:S(2)}) %collective-permute-start.19) | collective-permute-done | bytes 131104 | tf_op jit(solution)/shard_map/ppermute | solution.py:312
  89.3 3.6 %collective-permute-done.20.refs_2_ = f32[128,256]{1,0:T(8,128)S(1)} collective-permute-done((f32[128,256]{1,0:T(8,128)S(1)}, f32[128,256]{1,0:T(8,128)S(1)}, u32[]{:S(2)}, u32[]{:S(2)}) %collective-permute-start.20) | collective-permute-done | bytes 131104 | tf_op jit(solution)/shard_map/ppermute | solution.py:312
  92.9 2.7 %collective-permute-done.21.refs_3_ = f32[128,256]{1,0:T(8,128)S(1)} collective-permute-done((f32[128,256]{1,0:T(8,128)S(1)}, f32[128,256]{1,0:T(8,128)S(1)}, u32[]{:S(2)}, u32[]{:S(2)}) %collective-permute-start.21) | collective-permute-done | bytes 131104 | tf_op jit(solution)/shard_map/ppermute | solution.py:312
  (62 shorter events, 26.1 us)
Async XLA Ops:
  1.6 3.9 %collective-permute-start = (f32[512,128]{1,0:T(8,128)S(1)}, f32[512,128]{1,0:T(8,128)S(1)}, u32[]{:S(2)}, u32[]{:S(2)}) collective-permute-start(f32[512,128]{1,0:T(8,128)S(1)} %convert_element_type.3.refs_0_), channel_id=1, source_target_pairs={{0,8},{8,0},{1,9},{9,1},{2,10},{10,2},{3,11},{11,3},{4,12},{12,4},... | collective-permute-start | bytes 786440 | tf_op jit(solution)/shard_map/ppermute | solution.py:312
  20.7 6.9 %collective-permute-start.4 = (f32[1,4096]{1,0:T(1,128)S(1)}, f32[1,4096]{1,0:T(1,128)S(1)}, u32[]{:S(2)}, u32[]{:S(2)}) collective-permute-start(f32[1,4096]{1,0:T(1,128)S(1)} %get-tuple-element.36.refs_0_), channel_id=1, source_target_pairs={{0,128},{64,192},{128,0},{192,64},{1,129},{65,193},{129,1},{193,65... | collective-permute-start | bytes 49160 | tf_op jit(solution)/shard_map/ppermute | solution.py:312
  23.8 4.9 %collective-permute-start.3 = (f32[1,4096]{1,0:T(1,128)S(1)}, f32[1,4096]{1,0:T(1,128)S(1)}, u32[]{:S(2)}, u32[]{:S(2)}) collective-permute-start(f32[1,4096]{1,0:T(1,128)S(1)} %get-tuple-element.36.refs_0_), channel_id=1, source_target_pairs={{0,192},{64,128},{128,64},{192,0},{1,193},{65,129},{129,65},{193,1... | collective-permute-start | bytes 49160 | tf_op jit(solution)/shard_map/ppermute | solution.py:312
  24.9 3.8 %collective-permute-start.2 = (f32[1,4096]{1,0:T(1,128)S(1)}, f32[1,4096]{1,0:T(1,128)S(1)}, u32[]{:S(2)}, u32[]{:S(2)}) collective-permute-start(f32[1,4096]{1,0:T(1,128)S(1)} %get-tuple-element.36.refs_0_), channel_id=1, source_target_pairs={{0,64},{64,0},{128,192},{192,128},{1,65},{65,1},{129,193},{193,129... | collective-permute-start | bytes 49160 | tf_op jit(solution)/shard_map/ppermute | solution.py:312
  28.7 10.4 %collective-permute-start.7 = (f32[1,4096]{1,0:T(1,128)S(1)}, f32[1,4096]{1,0:T(1,128)S(1)}, u32[]{:S(2)}, u32[]{:S(2)}) collective-permute-start(f32[1,4096]{1,0:T(1,128)S(1)} %sum_x.1.refs_2_), channel_id=1, source_target_pairs={{0,32},{16,48},{32,0},{48,16},{1,33},{17,49},{33,1},{49,17},{2,34}... | collective-permute-start | bytes 49160 | tf_op jit(solution)/shard_map/ppermute | solution.py:312
  35.1 5.8 %collective-permute-start.6 = (f32[1,4096]{1,0:T(1,128)S(1)}, f32[1,4096]{1,0:T(1,128)S(1)}, u32[]{:S(2)}, u32[]{:S(2)}) collective-permute-start(f32[1,4096]{1,0:T(1,128)S(1)} %sum_x.1.refs_2_), channel_id=1, source_target_pairs={{0,48},{16,32},{32,16},{48,0},{1,49},{17,33},{33,17},{49,1},{2,50}... | collective-permute-start | bytes 49160 | tf_op jit(solution)/shard_map/ppermute | solution.py:312
  35.7 5.3 %collective-permute-start.5 = (f32[1,4096]{1,0:T(1,128)S(1)}, f32[1,4096]{1,0:T(1,128)S(1)}, u32[]{:S(2)}, u32[]{:S(2)}) collective-permute-start(f32[1,4096]{1,0:T(1,128)S(1)} %sum_x.1.refs_2_), channel_id=1, source_target_pairs={{0,16},{16,0},{32,48},{48,32},{1,17},{17,1},{33,49},{49,33},{2,18}... | collective-permute-start | bytes 49160 | tf_op jit(solution)/shard_map/ppermute | solution.py:312
  44.5 4.0 %collective-permute-start.9 = (f32[2,512]{1,0:T(2,128)S(1)}, f32[2,512]{1,0:T(2,128)S(1)}, u32[]{:S(2)}, u32[]{:S(2)}) collective-permute-start(f32[2,512]{1,0:T(2,128)S(1)} %target_core.1.refs_0_), channel_id=1, source_target_pairs={{0,4},{4,0},{1,5},{5,1},{2,6},{6,2},{3,7},{7,3},{8,12},{12,8},{9,1... | collective-permute-start | bytes 12296 | tf_op jit(solution)/shard_map/ppermute | solution.py:312
  48.6 6.2 %collective-permute-start.12 = (f32[2,512]{1,0:T(2,128)S(1)}, f32[2,512]{1,0:T(2,128)S(1)}, u32[]{:S(2)}, u32[]{:S(2)}) collective-permute-start(f32[2,512]{1,0:T(2,128)S(1)} %target_zl.1.refs_4_), channel_id=1, source_target_pairs={{0,2},{1,3},{2,0},{3,1},{4,6},{5,7},{6,4},{7,5},{8,10},{9,11},{10,... | collective-permute-start | bytes 12296 | tf_op jit(solution)/shard_map/ppermute | solution.py:312
  49.8 5.0 %collective-permute-start.11 = (f32[2,512]{1,0:T(2,128)S(1)}, f32[2,512]{1,0:T(2,128)S(1)}, u32[]{:S(2)}, u32[]{:S(2)}) collective-permute-start(f32[2,512]{1,0:T(2,128)S(1)} %target_zl.1.refs_4_), channel_id=1, source_target_pairs={{0,3},{1,2},{2,1},{3,0},{4,7},{5,6},{6,5},{7,4},{8,11},{9,10},{10,... | collective-permute-start | bytes 12296 | tf_op jit(solution)/shard_map/ppermute | solution.py:312
  51.9 3.6 %collective-permute-start.10 = (f32[2,512]{1,0:T(2,128)S(1)}, f32[2,512]{1,0:T(2,128)S(1)}, u32[]{:S(2)}, u32[]{:S(2)}) collective-permute-start(f32[2,512]{1,0:T(2,128)S(1)} %target_zl.1.refs_4_), channel_id=1, source_target_pairs={{0,1},{1,0},{2,3},{3,2},{4,5},{5,4},{6,7},{7,6},{8,9},{9,8},{10,11... | collective-permute-start | bytes 12296 | tf_op jit(solution)/shard_map/ppermute | solution.py:312
  55.9 9.7 %collective-permute-start.22 = (f32[512,128]{1,0:T(8,128)S(1)}, f32[512,128]{1,0:T(8,128)S(1)}, u32[]{:S(2)}, u32[]{:S(2)}) collective-permute-start(f32[512,128]{1,0:T(8,128)S(1)} %get-tuple-element.53), channel_id=1, source_target_pairs={{0,8},{8,0},{1,9},{9,1},{2,10},{10,2},{3,11},{11,3},{4,12},{12,4},... | collective-permute-start | bytes 786440 | tf_op jit(solution)/shard_map/ppermute | solution.py:312
  57.7 8.9 %collective-permute-start.13 = (f32[64,1024]{1,0:T(8,128)S(1)}, f32[64,1024]{1,0:T(8,128)S(1)}, u32[]{:S(2)}, u32[]{:S(2)}) collective-permute-start(f32[64,1024]{1,0:T(8,128)S(1)} %get-tuple-element.42), channel_id=1, source_target_pairs={{0,64},{64,0},{128,192},{192,128},{1,65},{65,1},{129,193},{193,129... | collective-permute-start | bytes 786440 | tf_op jit(solution)/shard_map/ppermute | solution.py:312
  58.6 9.6 %collective-permute-start.14 = (f32[64,1024]{1,0:T(8,128)S(1)}, f32[64,1024]{1,0:T(8,128)S(1)}, u32[]{:S(2)}, u32[]{:S(2)}) collective-permute-start(f32[64,1024]{1,0:T(8,128)S(1)} %get-tuple-element.43), channel_id=1, source_target_pairs={{0,192},{64,128},{128,64},{192,0},{1,193},{65,129},{129,65},{193,1... | collective-permute-start | bytes 786440 | tf_op jit(solution)/shard_map/ppermute | solution.py:312
  65.6 8.2 %collective-permute-start.23 = (f32[512,128]{1,0:T(8,128)S(1)}, f32[512,128]{1,0:T(8,128)S(1)}, u32[]{:S(2)}, u32[]{:S(2)}) collective-permute-start(f32[512,128]{1,0:T(8,128)S(1)} %embed_core.1.refs_0_), channel_id=1, source_target_pairs={{0,4},{4,0},{1,5},{5,1},{2,6},{6,2},{3,7},{7,3},{8,12},{12,8},{9,1... | collective-permute-start | bytes 786440 | tf_op jit(solution)/shard_map/ppermute | solution.py:312
  68.3 9.3 %collective-permute-start.17 = (f32[128,512]{1,0:T(8,128)S(1)}, f32[128,512]{1,0:T(8,128)S(1)}, u32[]{:S(2)}, u32[]{:S(2)}) collective-permute-start(f32[128,512]{1,0:T(8,128)S(1)} %get-tuple-element.46), channel_id=1, source_target_pairs={{0,64},{64,0},{128,192},{192,128},{1,65},{65,1},{129,193},{193,129... | collective-permute-start | bytes 786440 | tf_op jit(solution)/shard_map/ppermute | solution.py:312
  68.4 10.5 %collective-permute-start.18 = (f32[128,512]{1,0:T(8,128)S(1)}, f32[128,512]{1,0:T(8,128)S(1)}, u32[]{:S(2)}, u32[]{:S(2)}) collective-permute-start(f32[128,512]{1,0:T(8,128)S(1)} %get-tuple-element.47), channel_id=1, source_target_pairs={{0,192},{64,128},{128,64},{192,0},{1,193},{65,129},{129,65},{193,1... | collective-permute-start | bytes 786440 | tf_op jit(solution)/shard_map/ppermute | solution.py:312
  70.7 15.0 %collective-permute-start.15 = (f32[128,512]{1,0:T(8,128)S(1)}, f32[128,512]{1,0:T(8,128)S(1)}, u32[]{:S(2)}, u32[]{:S(2)}) collective-permute-start(f32[128,512]{1,0:T(8,128)S(1)} %get-tuple-element.44), channel_id=1, source_target_pairs={{0,64},{64,0},{128,192},{192,128},{1,65},{65,1},{129,193},{193,129... | collective-permute-start | bytes 786440 | tf_op jit(solution)/shard_map/ppermute | solution.py:312
  72.1 13.6 %collective-permute-start.16 = (f32[128,512]{1,0:T(8,128)S(1)}, f32[128,512]{1,0:T(8,128)S(1)}, u32[]{:S(2)}, u32[]{:S(2)}) collective-permute-start(f32[128,512]{1,0:T(8,128)S(1)} %get-tuple-element.45), channel_id=1, source_target_pairs={{0,192},{64,128},{128,64},{192,0},{1,193},{65,129},{129,65},{193,1... | collective-permute-start | bytes 786440 | tf_op jit(solution)/shard_map/ppermute | solution.py:312
  73.9 10.5 %collective-permute-start.24 = (f32[512,128]{1,0:T(8,128)S(1)}, f32[512,128]{1,0:T(8,128)S(1)}, u32[]{:S(2)}, u32[]{:S(2)}) collective-permute-start(f32[512,128]{1,0:T(8,128)S(1)} %embed_zl.1.refs_0_), channel_id=1, source_target_pairs={{0,1},{1,0},{2,3},{3,2},{4,5},{5,4},{6,7},{7,6},{8,9},{9,8},{10,11... | collective-permute-start | bytes 786440 | tf_op jit(solution)/shard_map/ppermute | solution.py:312
  79.0 10.2 %collective-permute-start.19 = (f32[128,256]{1,0:T(8,128)S(1)}, f32[128,256]{1,0:T(8,128)S(1)}, u32[]{:S(2)}, u32[]{:S(2)}) collective-permute-start(f32[128,256]{1,0:T(8,128)S(1)} %get-tuple-element.50), channel_id=1, source_target_pairs={{0,16},{16,0},{32,48},{48,32},{1,17},{17,1},{33,49},{49,33},{2,18}... | collective-permute-start | bytes 393224 | tf_op jit(solution)/shard_map/ppermute | solution.py:312
  80.6 12.3 %collective-permute-start.20 = (f32[128,256]{1,0:T(8,128)S(1)}, f32[128,256]{1,0:T(8,128)S(1)}, u32[]{:S(2)}, u32[]{:S(2)}) collective-permute-start(f32[128,256]{1,0:T(8,128)S(1)} %get-tuple-element.48.refs_3_), channel_id=1, source_target_pairs={{0,32},{16,48},{32,0},{48,16},{1,33},{17,49},{33,1},{49,17},{2,34}... | collective-permute-start | bytes 393224 | tf_op jit(solution)/shard_map/ppermute | solution.py:312
  84.4 11.2 %collective-permute-start.25 = (f32[512,128]{1,0:T(8,128)S(1)}, f32[512,128]{1,0:T(8,128)S(1)}, u32[]{:S(2)}, u32[]{:S(2)}) collective-permute-start(f32[512,128]{1,0:T(8,128)S(1)} %embed_y.1.refs_4_), channel_id=1, source_target_pairs={{0,3},{1,2},{2,1},{3,0},{4,7},{5,6},{6,5},{7,4},{8,11},{9,10},{10,... | collective-permute-start | bytes 786440 | tf_op jit(solution)/shard_map/ppermute | solution.py:312
  85.8 9.8 %collective-permute-start.21 = (f32[128,256]{1,0:T(8,128)S(1)}, f32[128,256]{1,0:T(8,128)S(1)}, u32[]{:S(2)}, u32[]{:S(2)}) collective-permute-start(f32[128,256]{1,0:T(8,128)S(1)} %get-tuple-element.51), channel_id=1, source_target_pairs={{0,48},{16,32},{32,16},{48,0},{1,49},{17,33},{33,17},{49,1},{2,50}... | collective-permute-start | bytes 393224 | tf_op jit(solution)/shard_map/ppermute | solution.py:312
  (6 other events, 33.1 us)
where the time goes:
time: 96.5 us; the launch traced here: 96.4 us
  starting transfers between devices  35.9 us (37%)
  Pallas kernels  26.1 us (27%)
  waiting for transfers between devices  20.4 us (21%)
  blocking collectives  10.6 us (11%)
  local copies, waits for them, and re-layouts  1.6 us (2%)
    ppermute x26, starting transfers between devices, swap(): lax.ppermute(v, axis, [(i, i ^ s) for i in range(lax.axis_size(axis))])  35.9 us
    pallas_call x24, Pallas kernels, call(): pl.pallas_call(kernel, out_shape=shapes, in_specs=[VMEM] * used + [ANY] *...  26.1 us
    ppermute x26, waiting for transfers between devices, swap(): lax.ppermute(v, axis, [(i, i ^ s) for i in range(lax.axis_size(axis))])  20.4 us
    all_to_all x1, blocking collectives, over_ctr(): return lax.all_to_all(v, ('zl', 'y'), 0, 0)  10.6 us
  transfers between devices with their start and end apart: 26, of which 12 were waited for; matrix products, arithmetic and copies ran while one was open for 0% of the time, Pallas kernels for 20%

commit v1 on v0

--- a/solution.py
+++ b/solution.py
@@ -139,16 +139,13 @@
     step = 64
     for row, kern_ref in ((0, own_ref), (1, other_ref)):
 
-        @pl.loop(0, half // (2 * step))
-        def _(n):
-            for i in range(2):
-                tile = pl.ds(pl.multiple_of((2 * n + i) * step, step), step)
-                total = jnp.zeros((step, LANES), F32)
-                for g in range(count // LANES):
-                    at = slice(g * LANES, (g + 1) * LANES)
-                    kern = kern_ref[tile, at]
-                    total = total + kern * kern * finv_ref[:, at]
-                acc[tile, :] = total
+        for i in range(0, half, step):
+            total = jnp.zeros((step, LANES), F32)
+            for g in range(count // LANES):
+                at = slice(g * LANES, (g + 1) * LANES)
+                kern = kern_ref[i : i + step, at]
+                total = total + kern * kern * finv_ref[:, at]
+            acc[i : i + step] = total
 
         t_ref[row : row + 1] = jnp.sum(acc[...].T, axis=0, keepdims=True)
 
@@ -214,10 +211,8 @@
     embed_sums(kern_ref, c_ref, out, lambda kern, at: kern * kern * (kern * finv_ref[:, at]))
 
 
-def embed_body(a0, a1, b0, b1, t0, t1, t2, t3, rinv_ref, z_ref, zo_ref, own, other):
-    tinv = 1.0 / four((t0, t1, t2, t3))
-    points = (z_ref[...].astype(F32), zo_ref[...])
-    for p, (cubes, squares, out) in enumerate(((a0, b0, own), (a1, b1, other))):
+def embed_grads(sums, tinv, rinv_ref, points, outs):
+    for p, (cubes, squares, out) in enumerate(zip(sums[:CORES], sums[CORES:], outs)):
         ts, rs = spread(tinv[p : p + 1]), spread(rinv_ref[p : p + 1])
         total = ts * cubes[:, LANES:] - rs * squares[:, LANES:]
         moved = ts * cubes[:, :LANES] - rs * squares[:, :LANES]
@@ -256,7 +251,9 @@
     centre_grads((1, 3), refs, tinv[...], ((first,), (third,)))
 
 
-def near_body(own, other, rinv, finv, tinv, z, zo, c, near, zt, ts, rs):
+def near_body(own, other, rinv, finv, tinv, z, zo, c, a0, a1, b0, b1, near, e0, e1, zt, ts, rs):
+    points = (z[...].astype(F32), zo[...])
+    embed_grads((a0, a1, b0, b1), tinv[...], rinv, points, (e0, e1))
     refs = ((own, other), rinv, finv, z, zo, c, zt, ts, rs)
     centre_grads((0,), refs, tinv[...], ((near,),))
 
@@ -403,22 +400,21 @@
         far_body, [part, part, rows], *base, *target, *data, scratch=setup, limit=24, name="grad_far"
     )
     low, high = swap(low, "x", 1), swap(high, "x", 3)
-    mine, other = call(
-        embed_body,
-        [(half, width)] * 2,
+    first, third = call(
+        mid_body, [piece, piece], *base, tinv, *data, scratch=setup, limit=24, name="grad_mid"
+    )
+    near, mine, other = call(
+        near_body,
+        [piece, (half, width), (half, width)],
+        *base,
+        tinv,
+        *data,
         *cubes,
         *squares,
-        *target,
-        rinv,
-        embeddings,
-        z_other,
-        limit=8,
-        name="embed_part",
-    )
-    first, third = call(
-        mid_body, [piece, piece], *base, tinv, *data, scratch=setup, limit=24, name="grad_mid"
-    )
-    near = call(near_body, [piece], *base, tinv, *data, scratch=setup, limit=24, name="grad_near")
+        scratch=setup,
+        limit=24,
+        name="grad_near",
+    )
 
     def second(start, name, after=()):
         to_first, to_third = call(
@@ -437,7 +433,7 @@
     first_a, third_a = second(0, "second_a")
     first_b, third_b = second(2 * inner, "second_b", after=[near])
 
-    embed = call(add_body, [mine.shape], mine, swap(other, "core", 1), name="embed_core")
+    embed = call(add_body, [mine.shape], mine, swap(other, "core", 1), name="embed_core", after=[low, high])
     embed = call(add_body, [mine.shape], embed, swap(embed, "zl", 1), name="embed_zl")
     embed = call(add_body, [mine.shape], embed, swap(embed, "y", 1), name="embed_y")
     embed = (embed, swap(embed, "y", 3))

time: 96.5 us -> 95.9 us (level)
  waiting for transfers between devices: 20.4 us -> 18.9 us
    ppermute x26, waiting for transfers between devices: 20.4 us -> 18.9 us  [swap(): lax.ppermute(v, axis, [(i, i ^ s) for i in range(lax.axis_size(axis))])]
    pallas_call x24 -> x23, Pallas kernels: 26.1 us -> 25.6 us  [call(): pl.pallas_call(kernel, out_shape=shapes, in_specs=[VMEM] * used + [ANY] *...]
  transfers between devices with their start and end apart: 26 -> 26, of which waited for: 12 -> 12; matrix products, arithmetic and copies ran while one was open for 0% -> 0% of each run, Pallas kernels for 20% -> 19%
where the time goes in v1:
time: 95.9 us; the launch traced here: 95.1 us
  starting transfers between devices  36.7 us (38%)
  Pallas kernels  25.6 us (27%)
  waiting for transfers between devices  18.9 us (20%)
  blocking collectives  10.6 us (11%)
  local copies, waits for them, and re-layouts  1.6 us (2%)
    ppermute x26, starting transfers between devices, swap(): lax.ppermute(v, axis, [(i, i ^ s) for i in range(lax.axis_size(axis))])  36.7 us
    pallas_call x23, Pallas kernels, call(): pl.pallas_call(kernel, out_shape=shapes, in_specs=[VMEM] * used + [ANY] *...  25.6 us
    ppermute x26, waiting for transfers between devices, swap(): lax.ppermute(v, axis, [(i, i ^ s) for i in range(lax.axis_size(axis))])  18.9 us
    all_to_all x1, blocking collectives, over_ctr(): return lax.all_to_all(v, ('zl', 'y'), 0, 0)  10.6 us
  transfers between devices with their start and end apart: 26, of which 12 were waited for; matrix products, arithmetic and copies ran while one was open for 0% of the time, Pallas kernels for 19%

profile of v1, /device:TPU:32, one launch (start us, length us, event | category | flops | bytes accessed | tf_op | source)
XLA Modules:
  0.0 95.1 jit_solution(10902212779290842659)
XLA Ops:
  1.7 1.6 %copy-done = bf16[8192,128]{1,0:T(8,128)(2,1)S(1)} copy-done((bf16[8192,128]{1,0:T(8,128)(2,1)S(1)}, bf16[8192,128]{1,0:T(8,128)(2,1)}, u32[]{:S(2)}) %copy-start) | copy-done | bytes 2097176
  3.3 2.2 %kern_own.1 = (f32[512,4096]{1,0:T(8,128)S(1)}, f32[1,512]{1,0:T(1,128)S(1)}, bf16[128,4096]{1,0:T(8,128)(2,1)S(1)}, f32[1,4096]{1,0:T(1,128)S(1)}) custom-call(f32[512,128]{1,0:T(8,128)S(1)} %convert_element_type.3.refs_0_, bf16[8192,128]{1,0:T(8,128)(2,1)S(1)} %copy-done), custom_call_target="tpu_custom_call" | custom-call | bytes 2359296 | tf_op jit(solution)/shard_map/kern_own/pallas_call | solution.py:295
  5.5 1.7 %kern_other.1 = (f32[512,4096]{1,0:T(8,128)S(1)}, f32[2,512]{1,0:T(2,128)S(1)}) custom-call(f32[512,128]{1,0:T(8,128)S(1)} %collective-permute-done.refs_0_.refs_9_.refs_6_, bf16[128,4096]{1,0:T(8,128)(2,1)S(1)} %get-tuple-element.31.refs_1_, f32[1,4096]{1,0:T(1,128)S(1)} %get-tuple-element.32.refs_2_, f32[1,512]{1,0:T(1,128)S(1)} %get-tuple-element.33.refs_3_), custom_call_target="tpu_custom_call" | custom-call | bytes 1329152 | tf_op jit(solution)/shard_map/kern_other/pallas_call | solution.py:295
  8.6 10.6 %all_to_all.5.refs_2_ = f32[8,2,512]{2,1,0:T(2,128)S(1)} all-to-all(f32[8,2,512]{2,1,0:T(2,128)S(1)} %sum_core.1), channel_id=1, replica_groups=mesh['x'=4,'h'=4,'core'=2,'zl'=2,'y'=4] {'zl','y'}, dimensions={0} | all-to-all | bytes 65536 | tf_op jit(solution)/shard_map/all_to_all | solution.py:326
  20.7 3.1 %collective-permute-start.4 = (f32[1,4096]{1,0:T(1,128)S(1)}, f32[1,4096]{1,0:T(1,128)S(1)}, u32[]{:S(2)}, u32[]{:S(2)}) collective-permute-start(f32[1,4096]{1,0:T(1,128)S(1)} %get-tuple-element.37.refs_0_), channel_id=1, source_target_pairs={{0,128},{64,192},{128,0},{192,64},{1,129},{65,193},{129,1},{193,65... | collective-permute-start | bytes 49160 | tf_op jit(solution)/shard_map/ppermute | solution.py:309
  24.9 2.6 %squares.2.refs_4_.refs_10_ = f32[512,256]{1,0:T(8,128)S(1)} custom-call(f32[512,4096]{1,0:T(8,128)S(1)} %get-tuple-element.30.refs_0_, bf16[8192,128]{1,0:T(8,128)(2,1)S(1)} %copy-done.1), custom_call_target="tpu_custom_call" | custom-call | flops 2147483648 | bytes 10485760 | tf_op jit(solution)/shard_map/squares/pallas_call | solution.py:295
  28.7 6.4 %collective-permute-start.7 = (f32[1,4096]{1,0:T(1,128)S(1)}, f32[1,4096]{1,0:T(1,128)S(1)}, u32[]{:S(2)}, u32[]{:S(2)}) collective-permute-start(f32[1,4096]{1,0:T(1,128)S(1)} %sum_x.1.refs_2_), channel_id=1, source_target_pairs={{0,32},{16,48},{32,0},{48,16},{1,33},{17,49},{33,1},{49,17},{2,34}... | collective-permute-start | bytes 49160 | tf_op jit(solution)/shard_map/ppermute | solution.py:309
  36.6 2.6 %squares.3.refs_7_.refs_11_ = f32[512,256]{1,0:T(8,128)S(1)} custom-call(f32[512,4096]{1,0:T(8,128)S(1)} %get-tuple-element.34.refs_1_.refs_0_, bf16[8192,128]{1,0:T(8,128)(2,1)S(1)} %copy-done.1), custom_call_target="tpu_custom_call" | custom-call | flops 2147483648 | bytes 10485760 | tf_op jit(solution)/shard_map/squares/pallas_call | solution.py:295
  39.2 1.8 %collective-permute-done.6.refs_4_ = f32[1,4096]{1,0:T(1,128)S(1)} collective-permute-done((f32[1,4096]{1,0:T(1,128)S(1)}, f32[1,4096]{1,0:T(1,128)S(1)}, u32[]{:S(2)}, u32[]{:S(2)}) %collective-permute-start.6) | collective-permute-done | bytes 16416 | tf_op jit(solution)/shard_map/ppermute | solution.py:309
  41.0 1.9 %target.1 = (f32[2,512]{1,0:T(2,128)S(1)}, f32[1,4096]{1,0:T(1,128)S(1)}) custom-call(f32[512,4096]{1,0:T(8,128)S(1)} %get-tuple-element.30.refs_0_, f32[512,4096]{1,0:T(8,128)S(1)} %get-tuple-element.34.refs_1_.refs_0_, f32[1,4096]{1,0:T(1,128)S(1)} %sum_x.1.refs_2_, f32[1,4096]{1,0:T(1,128)S(1)} %collective-permute-done.5.refs_3_, ...), custom_call_target="tpu_custom_call" | custom-call | bytes 17399808 | tf_op jit(solution)/shard_map/target/pallas_call | solution.py:295
  45.5 2.6 %cubes.3.refs_9_ = f32[512,256]{1,0:T(8,128)S(1)} custom-call(f32[512,4096]{1,0:T(8,128)S(1)} %get-tuple-element.34.refs_1_.refs_0_, f32[1,4096]{1,0:T(1,128)S(1)} %get-tuple-element.38.refs_3_.refs_1_, bf16[8192,128]{1,0:T(8,128)(2,1)S(1)} %copy-done.1), custom_call_target="tpu_custom_call" | custom-call | flops 2147483648 | bytes 10502144 | tf_op jit(solution)/shard_map/cubes/pallas_call | solution.py:295
  49.4 2.1 %collective-permute-start.11 = (f32[2,512]{1,0:T(2,128)S(1)}, f32[2,512]{1,0:T(2,128)S(1)}, u32[]{:S(2)}, u32[]{:S(2)}) collective-permute-start(f32[2,512]{1,0:T(2,128)S(1)} %target_zl.1.refs_4_), channel_id=1, source_target_pairs={{0,3},{1,2},{2,1},{3,0},{4,7},{5,6},{6,5},{7,4},{8,11},{9,10},{10,... | collective-permute-start | bytes 12296 | tf_op jit(solution)/shard_map/ppermute | solution.py:309
  51.8 2.6 %cubes.2.refs_8_ = f32[512,256]{1,0:T(8,128)S(1)} custom-call(f32[512,4096]{1,0:T(8,128)S(1)} %get-tuple-element.30.refs_0_, f32[1,4096]{1,0:T(1,128)S(1)} %get-tuple-element.38.refs_3_.refs_1_, bf16[8192,128]{1,0:T(8,128)(2,1)S(1)} %copy-done.1), custom_call_target="tpu_custom_call" | custom-call | flops 2147483648 | bytes 10502144 | tf_op jit(solution)/shard_map/cubes/pallas_call | solution.py:295
  55.1 1.7 %grad_far.1 = (f32[64,1024]{1,0:T(8,128)S(1)}, f32[64,1024]{1,0:T(8,128)S(1)}, f32[2,512]{1,0:T(2,128)S(1)}) custom-call(f32[512,4096]{1,0:T(8,128)S(1)} %get-tuple-element.30.refs_0_, f32[512,4096]{1,0:T(8,128)S(1)} %get-tuple-element.34.refs_1_.refs_0_, f32[2,512]{1,0:T(2,128)S(1)} %get-tuple-element.36.refs_2_, ...), custom_call_target="tpu_custom_call" | custom-call | bytes 19304448 | tf_op jit(solution)/shard_map/grad_far/pallas_call | solution.py:295
  57.7 2.1 %collective-permute-start.14 = (f32[64,1024]{1,0:T(8,128)S(1)}, f32[64,1024]{1,0:T(8,128)S(1)}, u32[]{:S(2)}, u32[]{:S(2)}) collective-permute-start(f32[64,1024]{1,0:T(8,128)S(1)} %get-tuple-element.45), channel_id=1, source_target_pairs={{0,192},{64,128},{128,64},{192,0},{1,193},{65,129},{129,65},{193,1... | collective-permute-start | bytes 786440 | tf_op jit(solution)/shard_map/ppermute | solution.py:309
  59.8 1.9 %grad_near.1 = (f32[128,1024]{1,0:T(8,128)S(1)}, f32[512,128]{1,0:T(8,128)S(1)}, f32[512,128]{1,0:T(8,128)S(1)}) custom-call(f32[512,4096]{1,0:T(8,128)S(1)} %get-tuple-element.30.refs_0_, f32[512,4096]{1,0:T(8,128)S(1)} %get-tuple-element.34.refs_1_.refs_0_, f32[2,512]{1,0:T(2,128)S(1)} %get-tuple-element.36.refs_2_, ...), custom_call_target="tpu_custom_call" | custom-call | bytes 21389312 | tf_op jit(solution)/shard_map/grad_near/pallas_call | solution.py:295
  61.9 3.1 %grad_mid.1 = (f32[128,1024]{1,0:T(8,128)S(1)}, f32[128,1024]{1,0:T(8,128)S(1)}) custom-call(f32[512,4096]{1,0:T(8,128)S(1)} %get-tuple-element.30.refs_0_, f32[512,4096]{1,0:T(8,128)S(1)} %get-tuple-element.34.refs_1_.refs_0_, f32[2,512]{1,0:T(2,128)S(1)} %get-tuple-element.36.refs_2_, f32[1,4096]{1,0:T(1,128)S(1)} %get-tuple-element.38.refs_3_.refs_1_, ...), custom_call_target="tpu_custom_call" | custom-call | bytes 19292160 | tf_op jit(solution)/shard_map/grad_mid/pallas_call | solution.py:295
  66.7 2.0 %collective-permute-start.18 = (f32[128,512]{1,0:T(8,128)S(1)}, f32[128,512]{1,0:T(8,128)S(1)}, u32[]{:S(2)}, u32[]{:S(2)}) collective-permute-start(f32[128,512]{1,0:T(8,128)S(1)} %get-tuple-element.49), channel_id=1, source_target_pairs={{0,192},{64,128},{128,64},{192,0},{1,193},{65,129},{129,65},{193,1... | collective-permute-start | bytes 786440 | tf_op jit(solution)/shard_map/ppermute | solution.py:309
  71.3 2.6 %collective-permute-done.23.refs_1_ = f32[512,128]{1,0:T(8,128)S(1)} collective-permute-done((f32[512,128]{1,0:T(8,128)S(1)}, f32[512,128]{1,0:T(8,128)S(1)}, u32[]{:S(2)}, u32[]{:S(2)}) %collective-permute-start.23) | collective-permute-done | bytes 262176 | tf_op jit(solution)/shard_map/ppermute | solution.py:309
  78.7 3.8 %collective-permute-start.20 = (f32[128,256]{1,0:T(8,128)S(1)}, f32[128,256]{1,0:T(8,128)S(1)}, u32[]{:S(2)}, u32[]{:S(2)}) collective-permute-start(f32[128,256]{1,0:T(8,128)S(1)} %get-tuple-element.50.refs_3_), channel_id=1, source_target_pairs={{0,32},{16,48},{32,0},{48,16},{1,33},{17,49},{33,1},{49,17},{2,34}... | collective-permute-start | bytes 393224 | tf_op jit(solution)/shard_map/ppermute | solution.py:309
  83.9 2.1 %collective-permute-start.21 = (f32[128,256]{1,0:T(8,128)S(1)}, f32[128,256]{1,0:T(8,128)S(1)}, u32[]{:S(2)}, u32[]{:S(2)}) collective-permute-start(f32[128,256]{1,0:T(8,128)S(1)} %get-tuple-element.53), channel_id=1, source_target_pairs={{0,48},{16,32},{32,16},{48,0},{1,49},{17,33},{33,17},{49,1},{2,50}... | collective-permute-start | bytes 393224 | tf_op jit(solution)/shard_map/ppermute | solution.py:309
  86.0 2.1 %collective-permute-done.19.refs_1_ = f32[128,256]{1,0:T(8,128)S(1)} collective-permute-done((f32[128,256]{1,0:T(8,128)S(1)}, f32[128,256]{1,0:T(8,128)S(1)}, u32[]{:S(2)}, u32[]{:S(2)}) %collective-permute-start.19) | collective-permute-done | bytes 131104 | tf_op jit(solution)/shard_map/ppermute | solution.py:309
  88.1 2.3 %collective-permute-done.20.refs_2_ = f32[128,256]{1,0:T(8,128)S(1)} collective-permute-done((f32[128,256]{1,0:T(8,128)S(1)}, f32[128,256]{1,0:T(8,128)S(1)}, u32[]{:S(2)}, u32[]{:S(2)}) %collective-permute-start.20) | collective-permute-done | bytes 131104 | tf_op jit(solution)/shard_map/ppermute | solution.py:309
  90.5 3.8 %collective-permute-done.21.refs_3_ = f32[128,256]{1,0:T(8,128)S(1)} collective-permute-done((f32[128,256]{1,0:T(8,128)S(1)}, f32[128,256]{1,0:T(8,128)S(1)}, u32[]{:S(2)}, u32[]{:S(2)}) %collective-permute-start.21) | collective-permute-done | bytes 131104 | tf_op jit(solution)/shard_map/ppermute | solution.py:309
  (61 shorter events, 25.0 us)
Async XLA Ops:
  1.6 3.9 %collective-permute-start = (f32[512,128]{1,0:T(8,128)S(1)}, f32[512,128]{1,0:T(8,128)S(1)}, u32[]{:S(2)}, u32[]{:S(2)}) collective-permute-start(f32[512,128]{1,0:T(8,128)S(1)} %convert_element_type.3.refs_0_), channel_id=1, source_target_pairs={{0,8},{8,0},{1,9},{9,1},{2,10},{10,2},{3,11},{11,3},{4,12},{12,4},... | collective-permute-start | bytes 786440 | tf_op jit(solution)/shard_map/ppermute | solution.py:309
  20.7 6.9 %collective-permute-start.4 = (f32[1,4096]{1,0:T(1,128)S(1)}, f32[1,4096]{1,0:T(1,128)S(1)}, u32[]{:S(2)}, u32[]{:S(2)}) collective-permute-start(f32[1,4096]{1,0:T(1,128)S(1)} %get-tuple-element.37.refs_0_), channel_id=1, source_target_pairs={{0,128},{64,192},{128,0},{192,64},{1,129},{65,193},{129,1},{193,65... | collective-permute-start | bytes 49160 | tf_op jit(solution)/shard_map/ppermute | solution.py:309
  23.8 4.9 %collective-permute-start.3 = (f32[1,4096]{1,0:T(1,128)S(1)}, f32[1,4096]{1,0:T(1,128)S(1)}, u32[]{:S(2)}, u32[]{:S(2)}) collective-permute-start(f32[1,4096]{1,0:T(1,128)S(1)} %get-tuple-element.37.refs_0_), channel_id=1, source_target_pairs={{0,192},{64,128},{128,64},{192,0},{1,193},{65,129},{129,65},{193,1... | collective-permute-start | bytes 49160 | tf_op jit(solution)/shard_map/ppermute | solution.py:309
  24.9 3.8 %collective-permute-start.2 = (f32[1,4096]{1,0:T(1,128)S(1)}, f32[1,4096]{1,0:T(1,128)S(1)}, u32[]{:S(2)}, u32[]{:S(2)}) collective-permute-start(f32[1,4096]{1,0:T(1,128)S(1)} %get-tuple-element.37.refs_0_), channel_id=1, source_target_pairs={{0,64},{64,0},{128,192},{192,128},{1,65},{65,1},{129,193},{193,129... | collective-permute-start | bytes 49160 | tf_op jit(solution)/shard_map/ppermute | solution.py:309
  28.7 10.4 %collective-permute-start.7 = (f32[1,4096]{1,0:T(1,128)S(1)}, f32[1,4096]{1,0:T(1,128)S(1)}, u32[]{:S(2)}, u32[]{:S(2)}) collective-permute-start(f32[1,4096]{1,0:T(1,128)S(1)} %sum_x.1.refs_2_), channel_id=1, source_target_pairs={{0,32},{16,48},{32,0},{48,16},{1,33},{17,49},{33,1},{49,17},{2,34}... | collective-permute-start | bytes 49160 | tf_op jit(solution)/shard_map/ppermute | solution.py:309
  35.1 5.8 %collective-permute-start.6 = (f32[1,4096]{1,0:T(1,128)S(1)}, f32[1,4096]{1,0:T(1,128)S(1)}, u32[]{:S(2)}, u32[]{:S(2)}) collective-permute-start(f32[1,4096]{1,0:T(1,128)S(1)} %sum_x.1.refs_2_), channel_id=1, source_target_pairs={{0,48},{16,32},{32,16},{48,0},{1,49},{17,33},{33,17},{49,1},{2,50}... | collective-permute-start | bytes 49160 | tf_op jit(solution)/shard_map/ppermute | solution.py:309
  35.7 5.3 %collective-permute-start.5 = (f32[1,4096]{1,0:T(1,128)S(1)}, f32[1,4096]{1,0:T(1,128)S(1)}, u32[]{:S(2)}, u32[]{:S(2)}) collective-permute-start(f32[1,4096]{1,0:T(1,128)S(1)} %sum_x.1.refs_2_), channel_id=1, source_target_pairs={{0,16},{16,0},{32,48},{48,32},{1,17},{17,1},{33,49},{49,33},{2,18}... | collective-permute-start | bytes 49160 | tf_op jit(solution)/shard_map/ppermute | solution.py:309
  44.1 4.0 %collective-permute-start.9 = (f32[2,512]{1,0:T(2,128)S(1)}, f32[2,512]{1,0:T(2,128)S(1)}, u32[]{:S(2)}, u32[]{:S(2)}) collective-permute-start(f32[2,512]{1,0:T(2,128)S(1)} %target_core.1.refs_0_), channel_id=1, source_target_pairs={{0,4},{4,0},{1,5},{5,1},{2,6},{6,2},{3,7},{7,3},{8,12},{12,8},{9,1... | collective-permute-start | bytes 12296 | tf_op jit(solution)/shard_map/ppermute | solution.py:309
  48.2 6.2 %collective-permute-start.12 = (f32[2,512]{1,0:T(2,128)S(1)}, f32[2,512]{1,0:T(2,128)S(1)}, u32[]{:S(2)}, u32[]{:S(2)}) collective-permute-start(f32[2,512]{1,0:T(2,128)S(1)} %target_zl.1.refs_4_), channel_id=1, source_target_pairs={{0,2},{1,3},{2,0},{3,1},{4,6},{5,7},{6,4},{7,5},{8,10},{9,11},{10,... | collective-permute-start | bytes 12296 | tf_op jit(solution)/shard_map/ppermute | solution.py:309
  49.4 5.0 %collective-permute-start.11 = (f32[2,512]{1,0:T(2,128)S(1)}, f32[2,512]{1,0:T(2,128)S(1)}, u32[]{:S(2)}, u32[]{:S(2)}) collective-permute-start(f32[2,512]{1,0:T(2,128)S(1)} %target_zl.1.refs_4_), channel_id=1, source_target_pairs={{0,3},{1,2},{2,1},{3,0},{4,7},{5,6},{6,5},{7,4},{8,11},{9,10},{10,... | collective-permute-start | bytes 12296 | tf_op jit(solution)/shard_map/ppermute | solution.py:309
  51.5 3.6 %collective-permute-start.10 = (f32[2,512]{1,0:T(2,128)S(1)}, f32[2,512]{1,0:T(2,128)S(1)}, u32[]{:S(2)}, u32[]{:S(2)}) collective-permute-start(f32[2,512]{1,0:T(2,128)S(1)} %target_zl.1.refs_4_), channel_id=1, source_target_pairs={{0,1},{1,0},{2,3},{3,2},{4,5},{5,4},{6,7},{7,6},{8,9},{9,8},{10,11... | collective-permute-start | bytes 12296 | tf_op jit(solution)/shard_map/ppermute | solution.py:309
  56.8 8.2 %collective-permute-start.13 = (f32[64,1024]{1,0:T(8,128)S(1)}, f32[64,1024]{1,0:T(8,128)S(1)}, u32[]{:S(2)}, u32[]{:S(2)}) collective-permute-start(f32[64,1024]{1,0:T(8,128)S(1)} %get-tuple-element.44), channel_id=1, source_target_pairs={{0,64},{64,0},{128,192},{192,128},{1,65},{65,1},{129,193},{193,129... | collective-permute-start | bytes 786440 | tf_op jit(solution)/shard_map/ppermute | solution.py:309
  57.7 7.6 %collective-permute-start.14 = (f32[64,1024]{1,0:T(8,128)S(1)}, f32[64,1024]{1,0:T(8,128)S(1)}, u32[]{:S(2)}, u32[]{:S(2)}) collective-permute-start(f32[64,1024]{1,0:T(8,128)S(1)} %get-tuple-element.45), channel_id=1, source_target_pairs={{0,192},{64,128},{128,64},{192,0},{1,193},{65,129},{129,65},{193,1... | collective-permute-start | bytes 786440 | tf_op jit(solution)/shard_map/ppermute | solution.py:309
  61.8 3.5 %collective-permute-start.22 = (f32[512,128]{1,0:T(8,128)S(1)}, f32[512,128]{1,0:T(8,128)S(1)}, u32[]{:S(2)}, u32[]{:S(2)}) collective-permute-start(f32[512,128]{1,0:T(8,128)S(1)} %get-tuple-element.55), channel_id=1, source_target_pairs={{0,8},{8,0},{1,9},{9,1},{2,10},{10,2},{3,11},{11,3},{4,12},{12,4},... | collective-permute-start | bytes 786440 | tf_op jit(solution)/shard_map/ppermute | solution.py:309
  65.4 8.5 %collective-permute-start.23 = (f32[512,128]{1,0:T(8,128)S(1)}, f32[512,128]{1,0:T(8,128)S(1)}, u32[]{:S(2)}, u32[]{:S(2)}) collective-permute-start(f32[512,128]{1,0:T(8,128)S(1)} %embed_core.1.refs_0_), channel_id=1, source_target_pairs={{0,4},{4,0},{1,5},{5,1},{2,6},{6,2},{3,7},{7,3},{8,12},{12,8},{9,1... | collective-permute-start | bytes 786440 | tf_op jit(solution)/shard_map/ppermute | solution.py:309
  66.4 9.3 %collective-permute-start.17 = (f32[128,512]{1,0:T(8,128)S(1)}, f32[128,512]{1,0:T(8,128)S(1)}, u32[]{:S(2)}, u32[]{:S(2)}) collective-permute-start(f32[128,512]{1,0:T(8,128)S(1)} %get-tuple-element.48), channel_id=1, source_target_pairs={{0,64},{64,0},{128,192},{192,128},{1,65},{65,1},{129,193},{193,129... | collective-permute-start | bytes 786440 | tf_op jit(solution)/shard_map/ppermute | solution.py:309
  66.7 10.4 %collective-permute-start.18 = (f32[128,512]{1,0:T(8,128)S(1)}, f32[128,512]{1,0:T(8,128)S(1)}, u32[]{:S(2)}, u32[]{:S(2)}) collective-permute-start(f32[128,512]{1,0:T(8,128)S(1)} %get-tuple-element.49), channel_id=1, source_target_pairs={{0,192},{64,128},{128,64},{192,0},{1,193},{65,129},{129,65},{193,1... | collective-permute-start | bytes 786440 | tf_op jit(solution)/shard_map/ppermute | solution.py:309
  68.7 15.1 %collective-permute-start.15 = (f32[128,512]{1,0:T(8,128)S(1)}, f32[128,512]{1,0:T(8,128)S(1)}, u32[]{:S(2)}, u32[]{:S(2)}) collective-permute-start(f32[128,512]{1,0:T(8,128)S(1)} %get-tuple-element.46), channel_id=1, source_target_pairs={{0,64},{64,0},{128,192},{192,128},{1,65},{65,1},{129,193},{193,129... | collective-permute-start | bytes 786440 | tf_op jit(solution)/shard_map/ppermute | solution.py:309
  70.1 13.7 %collective-permute-start.16 = (f32[128,512]{1,0:T(8,128)S(1)}, f32[128,512]{1,0:T(8,128)S(1)}, u32[]{:S(2)}, u32[]{:S(2)}) collective-permute-start(f32[128,512]{1,0:T(8,128)S(1)} %get-tuple-element.47), channel_id=1, source_target_pairs={{0,192},{64,128},{128,64},{192,0},{1,193},{65,129},{129,65},{193,1... | collective-permute-start | bytes 786440 | tf_op jit(solution)/shard_map/ppermute | solution.py:309
  73.9 8.6 %collective-permute-start.24 = (f32[512,128]{1,0:T(8,128)S(1)}, f32[512,128]{1,0:T(8,128)S(1)}, u32[]{:S(2)}, u32[]{:S(2)}) collective-permute-start(f32[512,128]{1,0:T(8,128)S(1)} %embed_zl.1.refs_0_), channel_id=1, source_target_pairs={{0,1},{1,0},{2,3},{3,2},{4,5},{5,4},{6,7},{7,6},{8,9},{9,8},{10,11... | collective-permute-start | bytes 786440 | tf_op jit(solution)/shard_map/ppermute | solution.py:309
  77.2 11.0 %collective-permute-start.19 = (f32[128,256]{1,0:T(8,128)S(1)}, f32[128,256]{1,0:T(8,128)S(1)}, u32[]{:S(2)}, u32[]{:S(2)}) collective-permute-start(f32[128,256]{1,0:T(8,128)S(1)} %get-tuple-element.52), channel_id=1, source_target_pairs={{0,16},{16,0},{32,48},{48,32},{1,17},{17,1},{33,49},{49,33},{2,18}... | collective-permute-start | bytes 393224 | tf_op jit(solution)/shard_map/ppermute | solution.py:309
  78.7 11.7 %collective-permute-start.20 = (f32[128,256]{1,0:T(8,128)S(1)}, f32[128,256]{1,0:T(8,128)S(1)}, u32[]{:S(2)}, u32[]{:S(2)}) collective-permute-start(f32[128,256]{1,0:T(8,128)S(1)} %get-tuple-element.50.refs_3_), channel_id=1, source_target_pairs={{0,32},{16,48},{32,0},{48,16},{1,33},{17,49},{33,1},{49,17},{2,34}... | collective-permute-start | bytes 393224 | tf_op jit(solution)/shard_map/ppermute | solution.py:309
  82.5 11.8 %collective-permute-start.25 = (f32[512,128]{1,0:T(8,128)S(1)}, f32[512,128]{1,0:T(8,128)S(1)}, u32[]{:S(2)}, u32[]{:S(2)}) collective-permute-start(f32[512,128]{1,0:T(8,128)S(1)} %embed_y.1.refs_4_), channel_id=1, source_target_pairs={{0,3},{1,2},{2,1},{3,0},{4,7},{5,6},{6,5},{7,4},{8,11},{9,10},{10,... | collective-permute-start | bytes 786440 | tf_op jit(solution)/shard_map/ppermute | solution.py:309
  83.9 10.4 %collective-permute-start.21 = (f32[128,256]{1,0:T(8,128)S(1)}, f32[128,256]{1,0:T(8,128)S(1)}, u32[]{:S(2)}, u32[]{:S(2)}) collective-permute-start(f32[128,256]{1,0:T(8,128)S(1)} %get-tuple-element.53), channel_id=1, source_target_pairs={{0,48},{16,32},{32,16},{48,0},{1,49},{17,33},{33,17},{49,1},{2,50}... | collective-permute-start | bytes 393224 | tf_op jit(solution)/shard_map/ppermute | solution.py:309
  (6 other events, 33.1 us)

commit v2 on v1

--- a/solution.py
+++ b/solution.py
@@ -60,9 +60,8 @@
     total = jnp.zeros((half, LANES), F32)
     for b in range(count // inner):
         at = slice(b * inner, (b + 1) * inner)
-        ct = c_ref[block_rows(b, inner, core), :].astype(F32).T
-        norms = jnp.sum(ct * ct, axis=0, keepdims=True)
-        ct = ct.astype(BF16)
+        ct = c_ref[block_rows(b, inner, core), :].T
+        norms = jnp.sum(jnp.square(ct.astype(F32)), axis=0, keepdims=True)
         ct_ref[:, at] = ct
         norm_ref[:, at] = norms
         kern = kern_block(za, zn, ct, norms)
@@ -159,19 +158,11 @@
     return two_terms(kern * kern * (kern * finv * tinv - rinv))
 
 
-def grad_setup(tinv, rinv_ref, points, zt, ts, rs):
-    for p in range(CORES):
-        ts[p] = spread(tinv[p : p + 1])
-        rs[p] = spread(rinv_ref[p : p + 1])
-        zt[p, :LANES] = (-SCALE * points[p].T).astype(BF16)
-        zt[p, LANES:] = jnp.full((ONES, points[p].shape[0]), SCALE, BF16)
-
-
 def grad_weights(block, kerns, finv_ref, ts, rs, p):
     inner = kerns[p].shape[1] // (SIDE * SIDE)
     at = pl.ds(pl.multiple_of(block * inner, inner), inner)
     return weights(
-        kerns[p][:, at], finv_ref[:, at], tile_lanes(ts[p], inner), tile_lanes(rs[p], inner)
+        kerns[p][:, at], finv_ref[:, at], tile_lanes(ts[p], inner), tile_lanes(rs[p][...], inner)
     )
 
 
@@ -179,7 +170,7 @@
     sums = jnp.zeros((LANES + ONES, c.shape[0]), F32)
     for p, terms in enumerate(parts):
         for term in terms:
-            sums += jnp.dot(zt[p], term, preferred_element_type=F32)
+            sums += jnp.dot(zt[p][...], term, preferred_element_type=F32)
     return sums[:LANES] + sums[LANES : LANES + 1] * c.astype(F32).T
 
 
@@ -203,7 +194,10 @@
         out[...] = total
 
 
-def square_body(kern_ref, c_ref, out):
+def square_body(p, kern_ref, c_ref, z_ref, rinv_ref, out, zt, rs):
+    zt[:LANES] = (-SCALE * z_ref[...].T).astype(BF16)
+    zt[LANES:] = jnp.full((ONES, z_ref.shape[0]), SCALE, BF16)
+    rs[...] = spread(rinv_ref[p : p + 1])
     embed_sums(kern_ref, c_ref, out, lambda kern, at: kern * kern)
 
 
@@ -211,20 +205,21 @@
     embed_sums(kern_ref, c_ref, out, lambda kern, at: kern * kern * (kern * finv_ref[:, at]))
 
 
-def embed_grads(sums, tinv, rinv_ref, points, outs):
+def embed_grads(sums, ts, rs, points, outs):
     for p, (cubes, squares, out) in enumerate(zip(sums[:CORES], sums[CORES:], outs)):
-        ts, rs = spread(tinv[p : p + 1]), spread(rinv_ref[p : p + 1])
-        total = ts * cubes[:, LANES:] - rs * squares[:, LANES:]
-        moved = ts * cubes[:, :LANES] - rs * squares[:, :LANES]
-        out[...] = SCALE * (total * points[p] - moved)
+        tinv, rinv = ts[p], rs[p][...]
+        total = tinv * cubes[:, LANES:] - rinv * squares[:, LANES:]
+        moved = tinv * cubes[:, :LANES] - rinv * squares[:, :LANES]
+        out[...] = SCALE * (total * points[p][...] - moved)
 
 
 def centre_grads(s, refs, tinv, outs):
-    kerns, rinv_ref, finv_ref, z_ref, zo_ref, c_ref, zt, ts, rs = refs
-    points = (z_ref[...].astype(F32), zo_ref[...])
-    grad_setup(tinv, rinv_ref, points, zt, ts, rs)
+    own, other, finv_ref, c_ref, zt0, zt1, rs0, rs1, ts = refs
+    kerns, zt, rs = (own, other), (zt0, zt1), (rs0, rs1)
+    for p in range(CORES):
+        ts[p] = spread(tinv[p : p + 1])
     core, x, h = lax.axis_index("core"), lax.axis_index("x"), lax.axis_index("h")
-    inner = kerns[0].shape[1] // (SIDE * SIDE)
+    inner = own.shape[1] // (SIDE * SIDE)
     for step, out in zip(s, outs):
         for n, hop in enumerate(HOPS):
             block = (x ^ step) * SIDE + (h ^ hop)
@@ -239,23 +234,21 @@
                 out[1][:, at] = grad[cut:]
 
 
-def far_body(own, other, rinv, finv, t0, t1, t2, t3, z, zo, c, low, high, tinv_ref, zt, ts, rs):
+def far_body(*refs):
+    base, (t0, t1, t2, t3, low, high, tinv_ref, ts) = refs[:8], refs[8:]
     tinv = 1.0 / four((t0, t1, t2, t3))
     tinv_ref[...] = tinv
-    refs = ((own, other), rinv, finv, z, zo, c, zt, ts, rs)
-    centre_grads((2,), refs, tinv, ((low, high),))
-
-
-def mid_body(own, other, rinv, finv, tinv, z, zo, c, first, third, zt, ts, rs):
-    refs = ((own, other), rinv, finv, z, zo, c, zt, ts, rs)
-    centre_grads((1, 3), refs, tinv[...], ((first,), (third,)))
-
-
-def near_body(own, other, rinv, finv, tinv, z, zo, c, a0, a1, b0, b1, near, e0, e1, zt, ts, rs):
-    points = (z[...].astype(F32), zo[...])
-    embed_grads((a0, a1, b0, b1), tinv[...], rinv, points, (e0, e1))
-    refs = ((own, other), rinv, finv, z, zo, c, zt, ts, rs)
-    centre_grads((0,), refs, tinv[...], ((near,),))
+    centre_grads((2,), (*base, ts), tinv, ((low, high),))
+
+
+def mid_body(*refs):
+    base, (tinv, first, third, ts) = refs[:8], refs[8:]
+    centre_grads((1, 3), (*base, ts), tinv[...], ((first,), (third,)))
+
+
+def embed_body(tinv, rs0, rs1, z, zo, a0, a1, b0, b1, e0, e1):
+    ts = [spread(tinv[p : p + 1]) for p in range(CORES)]
+    embed_grads((a0, a1, b0, b1), ts, (rs0, rs1), (z, zo), (e0, e1))
 
 
 def second_body(base, first, third, low, high, to_first, to_third):
@@ -267,6 +260,12 @@
     to_third[cut:] = third[cut:, at]
 
 
+def second_near_body(start, *refs):
+    base, (tinv, first, third, low, high, to_first, to_third, near, ts) = refs[:8], refs[8:]
+    second_body(start, first, third, low, high, to_first, to_third)
+    centre_grads((0,), (*base, ts), tinv[...], ((near,),))
+
+
 def split_body(base, near, first, third, *outs):
     inner = outs[0].shape[1]
     for n, out in enumerate(outs):
@@ -274,8 +273,12 @@
         out[...] = near[:, base + n * inner : base + (n + 1) * inner] + first[:, at] + third[:, at]
 
 
-def final_body(p0, p1, p2, p3, mine, theirs, grad, embed):
-    grad[...] = four((p0, p1, p2, p3)).T
+def three_body(p0, p1, p2, out):
+    out[...] = p0[...] + (p1[...] + p2[...])
+
+
+def final_body(most, last, mine, theirs, grad, embed):
+    grad[...] = (most[...] + last[...]).T
     embed[...] = mine[...] + theirs[...]
 
 
@@ -361,10 +364,22 @@
     kerns = (kern_own, kern_other)
     sums = (half, 2 * LANES)
     work = 4 * half * count * 2 * LANES
+    lanes = ((width + ONES, half), (half, LANES))
     squares = [
-        call(square_body, [sums], kern, centres, limit=20, name="squares", flops=work)
-        for kern in kerns
+        call(
+            functools.partial(square_body, p),
+            [sums, jax.ShapeDtypeStruct(lanes[0], BF16), lanes[1]],
+            kern,
+            centres,
+            points,
+            rinv,
+            limit=20,
+            name="squares",
+            flops=work,
+        )
+        for p, (kern, points) in enumerate(zip(kerns, (z_own, z_other)))
     ]
+    squares, zt, rs = zip(*squares)
     freq = call(
         add_body, [freq.shape], *around([freq] * SIDE, "x"), name="sum_x", after=squares[:1]
     )
@@ -388,50 +403,47 @@
     target = call(add_body, [rows], target, swap(target, "zl", 1), name="target_zl")
     target = around([target] * SIDE, "y")
 
-    setup = [
-        pltpu.VMEM((CORES, width + ONES, half), BF16),
-        pltpu.VMEM((CORES, half, LANES), F32),
-        pltpu.VMEM((CORES, half, LANES), F32),
-    ]
+    setup = [pltpu.VMEM((CORES, half, LANES), F32)]
     piece, part, pair = (width, SIDE * inner), (width // 2, SIDE * inner), (width, 2 * inner)
-    base = (*kerns, rinv, finv)
-    data = (embeddings, z_other, centres)
+    base = (*kerns, finv, centres, *zt, *rs)
     low, high, tinv = call(
-        far_body, [part, part, rows], *base, *target, *data, scratch=setup, limit=24, name="grad_far"
+        far_body, [part, part, rows], *base, *target, scratch=setup, limit=24, name="grad_far"
     )
     low, high = swap(low, "x", 1), swap(high, "x", 3)
     first, third = call(
-        mid_body, [piece, piece], *base, tinv, *data, scratch=setup, limit=24, name="grad_mid"
-    )
-    near, mine, other = call(
-        near_body,
-        [piece, (half, width), (half, width)],
+        mid_body, [piece, piece], *base, tinv, scratch=setup, limit=24, name="grad_mid"
+    )
+    mine, other = call(
+        embed_body,
+        [(half, width)] * 2,
+        tinv,
+        *rs,
+        z_own,
+        z_other,
+        *cubes,
+        *squares,
+        limit=8,
+        name="embed_part",
+        flops=HINT // 2,
+    )
+    moved = (first, third, low, high)
+    first_a, third_a = call(
+        functools.partial(second_body, 0), [pair] * 2, *moved, name="second_a", flops=HINT
+    )
+    first_a, third_a = swap(first_a, "x", 1), swap(third_a, "x", 3)
+    first_b, third_b, near = call(
+        functools.partial(second_near_body, 2 * inner),
+        [pair, pair, piece],
         *base,
         tinv,
-        *data,
-        *cubes,
-        *squares,
+        *moved,
         scratch=setup,
         limit=24,
-        name="grad_near",
-    )
-
-    def second(start, name, after=()):
-        to_first, to_third = call(
-            functools.partial(second_body, start),
-            [pair] * 2,
-            first,
-            third,
-            low,
-            high,
-            name=name,
-            flops=HINT,
-            after=after,
-        )
-        return swap(to_first, "x", 1), swap(to_third, "x", 3)
-
-    first_a, third_a = second(0, "second_a")
-    first_b, third_b = second(2 * inner, "second_b", after=[near])
+        name="second_b",
+        flops=HINT,
+        after=[mine],
+    )
+    first_b, third_b = swap(first_b, "x", 1), swap(third_b, "x", 3)
 
     embed = call(add_body, [mine.shape], mine, swap(other, "core", 1), name="embed_core", after=[low, high])
     embed = call(add_body, [mine.shape], embed, swap(embed, "zl", 1), name="embed_zl")
@@ -453,12 +465,11 @@
     far2, far1 = split(0, (first_a, third_a), "split_a")
     h2, h1 = swap(far2, "h", 2), swap(far1, "h", 1)
     h3, h0 = split(2 * inner, (first_b, third_b), "split_b", after=[far2])
+    most = call(three_body, [block], h0, h1, h2, name="most", flops=HINT)
     grad, embed = call(
         final_body,
         [(inner, width), (half, width)],
-        h0,
-        h1,
-        h2,
+        most,
         swap(h3, "h", 3),
         *embed,
         name="final",

time: 95.9 us -> 92.7 us (0.967)
  waiting for transfers between devices: 18.9 us -> 16.2 us
    ppermute x26, waiting for transfers between devices: 18.9 us -> 16.2 us  [swap(): lax.ppermute(v, axis, [(i, i ^ s) for i in range(lax.axis_size(axis))])]
    pallas_call x23 -> x24, Pallas kernels: 25.6 us -> 25.7 us  [call(): pl.pallas_call(kernel, out_shape=shapes, in_specs=[VMEM] * used + [ANY] *...]
  transfers between devices with their start and end apart: 26 -> 26, of which waited for: 12 -> 10; matrix products, arithmetic and copies ran while one was open for 0% -> 0% of each run, Pallas kernels for 19% -> 20%
where the time goes in v2:
time: 92.7 us; the launch traced here: 92.5 us
  starting transfers between devices  36.7 us (40%)
  Pallas kernels  25.7 us (28%)
  waiting for transfers between devices  16.2 us (17%)
  blocking collectives  10.6 us (11%)
  local copies, waits for them, and re-layouts  1.59 us (2%)
    ppermute x26, starting transfers between devices, swap(): lax.ppermute(v, axis, [(i, i ^ s) for i in range(lax.axis_size(axis))])  36.7 us
    pallas_call x24, Pallas kernels, call(): pl.pallas_call(kernel, out_shape=shapes, in_specs=[VMEM] * used + [ANY] *...  25.7 us
    ppermute x26, waiting for transfers between devices, swap(): lax.ppermute(v, axis, [(i, i ^ s) for i in range(lax.axis_size(axis))])  16.2 us
    all_to_all x1, blocking collectives, over_ctr(): return lax.all_to_all(v, ('zl', 'y'), 0, 0)  10.6 us
  transfers between devices with their start and end apart: 26, of which 10 were waited for; matrix products, arithmetic and copies ran while one was open for 0% of the time, Pallas kernels for 20%

profile of v2, /device:TPU:32, one launch (start us, length us, event | category | flops | bytes accessed | tf_op | source)
XLA Modules:
  0.0 92.5 jit_solution(18428130264630324178)
XLA Ops:
  1.7 1.6 %copy-done = bf16[8192,128]{1,0:T(8,128)(2,1)S(1)} copy-done((bf16[8192,128]{1,0:T(8,128)(2,1)S(1)}, bf16[8192,128]{1,0:T(8,128)(2,1)}, u32[]{:S(2)}) %copy-start) | copy-done | bytes 2097176
  3.3 2.0 %kern_own.1 = (f32[512,4096]{1,0:T(8,128)S(1)}, f32[1,512]{1,0:T(1,128)S(1)}, bf16[128,4096]{1,0:T(8,128)(2,1)S(1)}, f32[1,4096]{1,0:T(1,128)S(1)}) custom-call(f32[512,128]{1,0:T(8,128)S(1)} %convert_element_type.3.refs_0_.refs_2_.refs_3_, bf16[8192,128]{1,0:T(8,128)(2,1)S(1)} %copy-done), custom_call_target="tpu_custom_call" | custom-call | bytes 2359296 | tf_op jit(solution)/shard_map/kern_own/pallas_call | solution.py:298
  5.3 1.7 %kern_other.1 = (f32[512,4096]{1,0:T(8,128)S(1)}, f32[2,512]{1,0:T(2,128)S(1)}) custom-call(f32[512,128]{1,0:T(8,128)S(1)} %collective-permute-done.refs_0_.refs_2_.refs_4_, bf16[128,4096]{1,0:T(8,128)(2,1)S(1)} %get-tuple-element.37.refs_1_, f32[1,4096]{1,0:T(1,128)S(1)} %get-tuple-element.38.refs_2_, f32[1,512]{1,0:T(1,128)S(1)} %get-tuple-element.39.refs_3_), custom_call_target="tpu_custom_call" | custom-call | bytes 1329152 | tf_op jit(solution)/shard_map/kern_other/pallas_call | solution.py:298
  8.4 10.6 %all_to_all.5.refs_2_ = f32[8,2,512]{2,1,0:T(2,128)S(1)} all-to-all(f32[8,2,512]{2,1,0:T(2,128)S(1)} %sum_core.1), channel_id=1, replica_groups=mesh['x'=4,'h'=4,'core'=2,'zl'=2,'y'=4] {'zl','y'}, dimensions={0} | all-to-all | bytes 65536 | tf_op jit(solution)/shard_map/all_to_all | solution.py:329
  20.5 3.1 %collective-permute-start.4 = (f32[1,4096]{1,0:T(1,128)S(1)}, f32[1,4096]{1,0:T(1,128)S(1)}, u32[]{:S(2)}, u32[]{:S(2)}) collective-permute-start(f32[1,4096]{1,0:T(1,128)S(1)} %get-tuple-element.42.refs_0_), channel_id=1, source_target_pairs={{0,128},{64,192},{128,0},{192,64},{1,129},{65,193},{129,1},{193,65... | collective-permute-start | bytes 49160 | tf_op jit(solution)/shard_map/ppermute | solution.py:312
  24.7 2.7 %squares.2 = (f32[512,256]{1,0:T(8,128)S(1)}, bf16[144,512]{1,0:T(8,128)(2,1)S(1)}, f32[512,128]{1,0:T(8,128)S(1)}) custom-call(f32[512,4096]{1,0:T(8,128)S(1)} %get-tuple-element.36.refs_0_, bf16[8192,128]{1,0:T(8,128)(2,1)S(1)} %copy-done.1, f32[512,128]{1,0:T(8,128)S(1)} %convert_element_type.3.refs_0_.refs_2_.refs_3_, f32[2,512]{1,0:T(2,128)S(1)} %get-tuple-element.43.refs_3_), custom_call_target="tpu_custom_call" | custom-call | flops 2147483648 | bytes 10752000 | tf_op jit(solution)/shard_map/squares/pallas_call | solution.py:298
  28.5 6.4 %collective-permute-start.7 = (f32[1,4096]{1,0:T(1,128)S(1)}, f32[1,4096]{1,0:T(1,128)S(1)}, u32[]{:S(2)}, u32[]{:S(2)}) collective-permute-start(f32[1,4096]{1,0:T(1,128)S(1)} %sum_x.1.refs_2_), channel_id=1, source_target_pairs={{0,32},{16,48},{32,0},{48,16},{1,33},{17,49},{33,1},{49,17},{2,34}... | collective-permute-start | bytes 49160 | tf_op jit(solution)/shard_map/ppermute | solution.py:312
  36.4 2.7 %squares.3 = (f32[512,256]{1,0:T(8,128)S(1)}, bf16[144,512]{1,0:T(8,128)(2,1)S(1)}, f32[512,128]{1,0:T(8,128)S(1)}) custom-call(f32[512,4096]{1,0:T(8,128)S(1)} %get-tuple-element.40.refs_1_.refs_0_, bf16[8192,128]{1,0:T(8,128)(2,1)S(1)} %copy-done.1, f32[512,128]{1,0:T(8,128)S(1)} %collective-permute-done.refs_0_.refs_2_.refs_4_, ...), custom_call_target="tpu_custom_call" | custom-call | flops 2147483648 | bytes 10752000 | tf_op jit(solution)/shard_map/squares/pallas_call | solution.py:298
  39.2 1.6 %collective-permute-done.6.refs_4_ = f32[1,4096]{1,0:T(1,128)S(1)} collective-permute-done((f32[1,4096]{1,0:T(1,128)S(1)}, f32[1,4096]{1,0:T(1,128)S(1)}, u32[]{:S(2)}, u32[]{:S(2)}) %collective-permute-start.6) | collective-permute-done | bytes 16416 | tf_op jit(solution)/shard_map/ppermute | solution.py:312
  40.8 1.9 %target.1 = (f32[2,512]{1,0:T(2,128)S(1)}, f32[1,4096]{1,0:T(1,128)S(1)}) custom-call(f32[512,4096]{1,0:T(8,128)S(1)} %get-tuple-element.36.refs_0_, f32[512,4096]{1,0:T(8,128)S(1)} %get-tuple-element.40.refs_1_.refs_0_, f32[1,4096]{1,0:T(1,128)S(1)} %sum_x.1.refs_2_, f32[1,4096]{1,0:T(1,128)S(1)} %collective-permute-done.5.refs_3_, ...), custom_call_target="tpu_custom_call" | custom-call | bytes 17399808 | tf_op jit(solution)/shard_map/target/pallas_call | solution.py:298
  45.4 2.6 %cubes.3.refs_6_ = f32[512,256]{1,0:T(8,128)S(1)} custom-call(f32[512,4096]{1,0:T(8,128)S(1)} %get-tuple-element.40.refs_1_.refs_0_, f32[1,4096]{1,0:T(1,128)S(1)} %get-tuple-element.46.refs_2_.refs_1_, bf16[8192,128]{1,0:T(8,128)(2,1)S(1)} %copy-done.1), custom_call_target="tpu_custom_call" | custom-call | flops 2147483648 | bytes 10502144 | tf_op jit(solution)/shard_map/cubes/pallas_call | solution.py:298
  49.2 2.1 %collective-permute-start.11 = (f32[2,512]{1,0:T(2,128)S(1)}, f32[2,512]{1,0:T(2,128)S(1)}, u32[]{:S(2)}, u32[]{:S(2)}) collective-permute-start(f32[2,512]{1,0:T(2,128)S(1)} %target_zl.1.refs_8_), channel_id=1, source_target_pairs={{0,3},{1,2},{2,1},{3,0},{4,7},{5,6},{6,5},{7,4},{8,11},{9,10},{10,... | collective-permute-start | bytes 12296 | tf_op jit(solution)/shard_map/ppermute | solution.py:312
  51.6 2.6 %cubes.2.refs_5_ = f32[512,256]{1,0:T(8,128)S(1)} custom-call(f32[512,4096]{1,0:T(8,128)S(1)} %get-tuple-element.36.refs_0_, f32[1,4096]{1,0:T(1,128)S(1)} %get-tuple-element.46.refs_2_.refs_1_, bf16[8192,128]{1,0:T(8,128)(2,1)S(1)} %copy-done.1), custom_call_target="tpu_custom_call" | custom-call | flops 2147483648 | bytes 10502144 | tf_op jit(solution)/shard_map/cubes/pallas_call | solution.py:298
  55.0 1.7 %grad_far.1 = (f32[64,1024]{1,0:T(8,128)S(1)}, f32[64,1024]{1,0:T(8,128)S(1)}, f32[2,512]{1,0:T(2,128)S(1)}) custom-call(f32[512,4096]{1,0:T(8,128)S(1)} %get-tuple-element.36.refs_0_, f32[512,4096]{1,0:T(8,128)S(1)} %get-tuple-element.40.refs_1_.refs_0_, f32[1,4096]{1,0:T(1,128)S(1)} %get-tuple-element.46.refs_2_.refs_1_, bf16[8192,128]{1,0:T(8,128)(2,1)S(1)} %copy-done.1, ...), custom_call_target="tpu_custom_call" | custom-call | bytes 19726336 | tf_op jit(solution)/shard_map/grad_far/pallas_call | solution.py:298
  57.7 2.1 %collective-permute-start.14 = (f32[64,1024]{1,0:T(8,128)S(1)}, f32[64,1024]{1,0:T(8,128)S(1)}, u32[]{:S(2)}, u32[]{:S(2)}) collective-permute-start(f32[64,1024]{1,0:T(8,128)S(1)} %get-tuple-element.56), channel_id=1, source_target_pairs={{0,192},{64,128},{128,64},{192,0},{1,193},{65,129},{129,65},{193,1... | collective-permute-start | bytes 786440 | tf_op jit(solution)/shard_map/ppermute | solution.py:312
  60.4 3.1 %grad_mid.1 = (f32[128,1024]{1,0:T(8,128)S(1)}, f32[128,1024]{1,0:T(8,128)S(1)}) custom-call(f32[512,4096]{1,0:T(8,128)S(1)} %get-tuple-element.36.refs_0_, f32[512,4096]{1,0:T(8,128)S(1)} %get-tuple-element.40.refs_1_.refs_0_, f32[1,4096]{1,0:T(1,128)S(1)} %get-tuple-element.46.refs_2_.refs_1_, bf16[8192,128]{1,0:T(8,128)(2,1)S(1)} %copy-done.1, ...), custom_call_target="tpu_custom_call" | custom-call | bytes 19714048 | tf_op jit(solution)/shard_map/grad_mid/pallas_call | solution.py:298
  63.5 1.8 %collective-permute-done.14.refs_12_.refs_3_ = f32[64,1024]{1,0:T(8,128)S(1)} collective-permute-done((f32[64,1024]{1,0:T(8,128)S(1)}, f32[64,1024]{1,0:T(8,128)S(1)}, u32[]{:S(2)}, u32[]{:S(2)}) %collective-permute-start.14) | collective-permute-done | bytes 262176 | tf_op jit(solution)/shard_map/ppermute | solution.py:312
  66.5 2.2 %collective-permute-start.18 = (f32[128,512]{1,0:T(8,128)S(1)}, f32[128,512]{1,0:T(8,128)S(1)}, u32[]{:S(2)}, u32[]{:S(2)}) collective-permute-start(f32[128,512]{1,0:T(8,128)S(1)} %get-tuple-element.62), channel_id=1, source_target_pairs={{0,192},{64,128},{128,64},{192,0},{1,193},{65,129},{129,65},{193,1... | collective-permute-start | bytes 786440 | tf_op jit(solution)/shard_map/ppermute | solution.py:312
  68.6 1.6 %second_b.1 = (f32[128,512]{1,0:T(8,128)S(1)}, f32[128,512]{1,0:T(8,128)S(1)}, f32[128,1024]{1,0:T(8,128)S(1)}) custom-call(f32[512,4096]{1,0:T(8,128)S(1)} %get-tuple-element.36.refs_0_, f32[512,4096]{1,0:T(8,128)S(1)} %get-tuple-element.40.refs_1_.refs_0_, f32[1,4096]{1,0:T(1,128)S(1)} %get-tuple-element.46.refs_2_.refs_1_, ...), custom_call_target="tpu_custom_call" | custom-call | flops 10000000000 | bytes 21549056 | tf_op jit(solution)/shard_map/second_b/pallas_call | solution.py:298
  72.9 1.6 %collective-permute-start.24 = (f32[512,128]{1,0:T(8,128)S(1)}, f32[512,128]{1,0:T(8,128)S(1)}, u32[]{:S(2)}, u32[]{:S(2)}) collective-permute-start(f32[512,128]{1,0:T(8,128)S(1)} %embed_zl.1.refs_0_), channel_id=1, source_target_pairs={{0,1},{1,0},{2,3},{3,2},{4,5},{5,4},{6,7},{7,6},{8,9},{9,8},{10,11... | collective-permute-start | bytes 786440 | tf_op jit(solution)/shard_map/ppermute | solution.py:312
  76.7 1.6 %collective-permute-start.19 = (f32[128,256]{1,0:T(8,128)S(1)}, f32[128,256]{1,0:T(8,128)S(1)}, u32[]{:S(2)}, u32[]{:S(2)}) collective-permute-start(f32[128,256]{1,0:T(8,128)S(1)} %get-tuple-element.65), channel_id=1, source_target_pairs={{0,16},{16,0},{32,48},{48,32},{1,17},{17,1},{33,49},{49,33},{2,18}... | collective-permute-start | bytes 393224 | tf_op jit(solution)/shard_map/ppermute | solution.py:312
  78.3 3.8 %collective-permute-start.20 = (f32[128,256]{1,0:T(8,128)S(1)}, f32[128,256]{1,0:T(8,128)S(1)}, u32[]{:S(2)}, u32[]{:S(2)}) collective-permute-start(f32[128,256]{1,0:T(8,128)S(1)} %get-tuple-element.63.refs_3_), channel_id=1, source_target_pairs={{0,32},{16,48},{32,0},{48,16},{1,33},{17,49},{33,1},{49,17},{2,34}... | collective-permute-start | bytes 393224 | tf_op jit(solution)/shard_map/ppermute | solution.py:312
  84.8 4.8 %collective-permute-done.20.refs_2_ = f32[128,256]{1,0:T(8,128)S(1)} collective-permute-done((f32[128,256]{1,0:T(8,128)S(1)}, f32[128,256]{1,0:T(8,128)S(1)}, u32[]{:S(2)}, u32[]{:S(2)}) %collective-permute-start.20) | collective-permute-done | bytes 131104 | tf_op jit(solution)/shard_map/ppermute | solution.py:312
  89.6 2.1 %collective-permute-done.21.refs_1_ = f32[128,256]{1,0:T(8,128)S(1)} collective-permute-done((f32[128,256]{1,0:T(8,128)S(1)}, f32[128,256]{1,0:T(8,128)S(1)}, u32[]{:S(2)}, u32[]{:S(2)}) %collective-permute-start.21) | collective-permute-done | bytes 131104 | tf_op jit(solution)/shard_map/ppermute | solution.py:312
  (60 shorter events, 23.6 us)
Async XLA Ops:
  1.6 3.7 %collective-permute-start = (f32[512,128]{1,0:T(8,128)S(1)}, f32[512,128]{1,0:T(8,128)S(1)}, u32[]{:S(2)}, u32[]{:S(2)}) collective-permute-start(f32[512,128]{1,0:T(8,128)S(1)} %convert_element_type.3.refs_0_.refs_2_.refs_3_), channel_id=1, source_target_pairs={{0,8},{8,0},{1,9},{9,1},{2,10},{10,2},{3,11},{11,3},{4,12},{12,4},... | collective-permute-start | bytes 786440 | tf_op jit(solution)/shard_map/ppermute | solution.py:312
  20.5 7.0 %collective-permute-start.4 = (f32[1,4096]{1,0:T(1,128)S(1)}, f32[1,4096]{1,0:T(1,128)S(1)}, u32[]{:S(2)}, u32[]{:S(2)}) collective-permute-start(f32[1,4096]{1,0:T(1,128)S(1)} %get-tuple-element.42.refs_0_), channel_id=1, source_target_pairs={{0,128},{64,192},{128,0},{192,64},{1,129},{65,193},{129,1},{193,65... | collective-permute-start | bytes 49160 | tf_op jit(solution)/shard_map/ppermute | solution.py:312
  23.6 4.9 %collective-permute-start.3 = (f32[1,4096]{1,0:T(1,128)S(1)}, f32[1,4096]{1,0:T(1,128)S(1)}, u32[]{:S(2)}, u32[]{:S(2)}) collective-permute-start(f32[1,4096]{1,0:T(1,128)S(1)} %get-tuple-element.42.refs_0_), channel_id=1, source_target_pairs={{0,192},{64,128},{128,64},{192,0},{1,193},{65,129},{129,65},{193,1... | collective-permute-start | bytes 49160 | tf_op jit(solution)/shard_map/ppermute | solution.py:312
  24.7 3.8 %collective-permute-start.2 = (f32[1,4096]{1,0:T(1,128)S(1)}, f32[1,4096]{1,0:T(1,128)S(1)}, u32[]{:S(2)}, u32[]{:S(2)}) collective-permute-start(f32[1,4096]{1,0:T(1,128)S(1)} %get-tuple-element.42.refs_0_), channel_id=1, source_target_pairs={{0,64},{64,0},{128,192},{192,128},{1,65},{65,1},{129,193},{193,129... | collective-permute-start | bytes 49160 | tf_op jit(solution)/shard_map/ppermute | solution.py:312
  28.5 10.6 %collective-permute-start.7 = (f32[1,4096]{1,0:T(1,128)S(1)}, f32[1,4096]{1,0:T(1,128)S(1)}, u32[]{:S(2)}, u32[]{:S(2)}) collective-permute-start(f32[1,4096]{1,0:T(1,128)S(1)} %sum_x.1.refs_2_), channel_id=1, source_target_pairs={{0,32},{16,48},{32,0},{48,16},{1,33},{17,49},{33,1},{49,17},{2,34}... | collective-permute-start | bytes 49160 | tf_op jit(solution)/shard_map/ppermute | solution.py:312
  34.9 5.8 %collective-permute-start.6 = (f32[1,4096]{1,0:T(1,128)S(1)}, f32[1,4096]{1,0:T(1,128)S(1)}, u32[]{:S(2)}, u32[]{:S(2)}) collective-permute-start(f32[1,4096]{1,0:T(1,128)S(1)} %sum_x.1.refs_2_), channel_id=1, source_target_pairs={{0,48},{16,32},{32,16},{48,0},{1,49},{17,33},{33,17},{49,1},{2,50}... | collective-permute-start | bytes 49160 | tf_op jit(solution)/shard_map/ppermute | solution.py:312
  35.5 5.3 %collective-permute-start.5 = (f32[1,4096]{1,0:T(1,128)S(1)}, f32[1,4096]{1,0:T(1,128)S(1)}, u32[]{:S(2)}, u32[]{:S(2)}) collective-permute-start(f32[1,4096]{1,0:T(1,128)S(1)} %sum_x.1.refs_2_), channel_id=1, source_target_pairs={{0,16},{16,0},{32,48},{48,32},{1,17},{17,1},{33,49},{49,33},{2,18}... | collective-permute-start | bytes 49160 | tf_op jit(solution)/shard_map/ppermute | solution.py:312
  44.0 4.1 %collective-permute-start.9 = (f32[2,512]{1,0:T(2,128)S(1)}, f32[2,512]{1,0:T(2,128)S(1)}, u32[]{:S(2)}, u32[]{:S(2)}) collective-permute-start(f32[2,512]{1,0:T(2,128)S(1)} %target_core.1.refs_0_), channel_id=1, source_target_pairs={{0,4},{4,0},{1,5},{5,1},{2,6},{6,2},{3,7},{7,3},{8,12},{12,8},{9,1... | collective-permute-start | bytes 12296 | tf_op jit(solution)/shard_map/ppermute | solution.py:312
  48.0 6.2 %collective-permute-start.12 = (f32[2,512]{1,0:T(2,128)S(1)}, f32[2,512]{1,0:T(2,128)S(1)}, u32[]{:S(2)}, u32[]{:S(2)}) collective-permute-start(f32[2,512]{1,0:T(2,128)S(1)} %target_zl.1.refs_8_), channel_id=1, source_target_pairs={{0,2},{1,3},{2,0},{3,1},{4,6},{5,7},{6,4},{7,5},{8,10},{9,11},{10,... | collective-permute-start | bytes 12296 | tf_op jit(solution)/shard_map/ppermute | solution.py:312
  49.2 5.0 %collective-permute-start.11 = (f32[2,512]{1,0:T(2,128)S(1)}, f32[2,512]{1,0:T(2,128)S(1)}, u32[]{:S(2)}, u32[]{:S(2)}) collective-permute-start(f32[2,512]{1,0:T(2,128)S(1)} %target_zl.1.refs_8_), channel_id=1, source_target_pairs={{0,3},{1,2},{2,1},{3,0},{4,7},{5,6},{6,5},{7,4},{8,11},{9,10},{10,... | collective-permute-start | bytes 12296 | tf_op jit(solution)/shard_map/ppermute | solution.py:312
  51.4 3.6 %collective-permute-start.10 = (f32[2,512]{1,0:T(2,128)S(1)}, f32[2,512]{1,0:T(2,128)S(1)}, u32[]{:S(2)}, u32[]{:S(2)}) collective-permute-start(f32[2,512]{1,0:T(2,128)S(1)} %target_zl.1.refs_8_), channel_id=1, source_target_pairs={{0,1},{1,0},{2,3},{3,2},{4,5},{5,4},{6,7},{7,6},{8,9},{9,8},{10,11... | collective-permute-start | bytes 12296 | tf_op jit(solution)/shard_map/ppermute | solution.py:312
  56.6 6.9 %collective-permute-start.13 = (f32[64,1024]{1,0:T(8,128)S(1)}, f32[64,1024]{1,0:T(8,128)S(1)}, u32[]{:S(2)}, u32[]{:S(2)}) collective-permute-start(f32[64,1024]{1,0:T(8,128)S(1)} %get-tuple-element.55), channel_id=1, source_target_pairs={{0,64},{64,0},{128,192},{192,128},{1,65},{65,1},{129,193},{193,129... | collective-permute-start | bytes 786440 | tf_op jit(solution)/shard_map/ppermute | solution.py:312
  57.7 7.6 %collective-permute-start.14 = (f32[64,1024]{1,0:T(8,128)S(1)}, f32[64,1024]{1,0:T(8,128)S(1)}, u32[]{:S(2)}, u32[]{:S(2)}) collective-permute-start(f32[64,1024]{1,0:T(8,128)S(1)} %get-tuple-element.56), channel_id=1, source_target_pairs={{0,192},{64,128},{128,64},{192,0},{1,193},{65,129},{129,65},{193,1... | collective-permute-start | bytes 786440 | tf_op jit(solution)/shard_map/ppermute | solution.py:312
  60.1 5.2 %collective-permute-start.22 = (f32[512,128]{1,0:T(8,128)S(1)}, f32[512,128]{1,0:T(8,128)S(1)}, u32[]{:S(2)}, u32[]{:S(2)}) collective-permute-start(f32[512,128]{1,0:T(8,128)S(1)} %get-tuple-element.67), channel_id=1, source_target_pairs={{0,8},{8,0},{1,9},{9,1},{2,10},{10,2},{3,11},{11,3},{4,12},{12,4},... | collective-permute-start | bytes 786440 | tf_op jit(solution)/shard_map/ppermute | solution.py:312
  65.3 7.5 %collective-permute-start.23 = (f32[512,128]{1,0:T(8,128)S(1)}, f32[512,128]{1,0:T(8,128)S(1)}, u32[]{:S(2)}, u32[]{:S(2)}) collective-permute-start(f32[512,128]{1,0:T(8,128)S(1)} %embed_core.1.refs_0_), channel_id=1, source_target_pairs={{0,4},{4,0},{1,5},{5,1},{2,6},{6,2},{3,7},{7,3},{8,12},{12,8},{9,1... | collective-permute-start | bytes 786440 | tf_op jit(solution)/shard_map/ppermute | solution.py:312
  66.4 9.3 %collective-permute-start.17 = (f32[128,512]{1,0:T(8,128)S(1)}, f32[128,512]{1,0:T(8,128)S(1)}, u32[]{:S(2)}, u32[]{:S(2)}) collective-permute-start(f32[128,512]{1,0:T(8,128)S(1)} %get-tuple-element.61), channel_id=1, source_target_pairs={{0,64},{64,0},{128,192},{192,128},{1,65},{65,1},{129,193},{193,129... | collective-permute-start | bytes 786440 | tf_op jit(solution)/shard_map/ppermute | solution.py:312
  66.5 10.2 %collective-permute-start.18 = (f32[128,512]{1,0:T(8,128)S(1)}, f32[128,512]{1,0:T(8,128)S(1)}, u32[]{:S(2)}, u32[]{:S(2)}) collective-permute-start(f32[128,512]{1,0:T(8,128)S(1)} %get-tuple-element.62), channel_id=1, source_target_pairs={{0,192},{64,128},{128,64},{192,0},{1,193},{65,129},{129,65},{193,1... | collective-permute-start | bytes 786440 | tf_op jit(solution)/shard_map/ppermute | solution.py:312
  70.3 11.8 %collective-permute-start.15 = (f32[128,512]{1,0:T(8,128)S(1)}, f32[128,512]{1,0:T(8,128)S(1)}, u32[]{:S(2)}, u32[]{:S(2)}) collective-permute-start(f32[128,512]{1,0:T(8,128)S(1)} %get-tuple-element.59), channel_id=1, source_target_pairs={{0,64},{64,0},{128,192},{192,128},{1,65},{65,1},{129,193},{193,129... | collective-permute-start | bytes 786440 | tf_op jit(solution)/shard_map/ppermute | solution.py:312
  71.7 10.4 %collective-permute-start.16 = (f32[128,512]{1,0:T(8,128)S(1)}, f32[128,512]{1,0:T(8,128)S(1)}, u32[]{:S(2)}, u32[]{:S(2)}) collective-permute-start(f32[128,512]{1,0:T(8,128)S(1)} %get-tuple-element.60), channel_id=1, source_target_pairs={{0,192},{64,128},{128,64},{192,0},{1,193},{65,129},{129,65},{193,1... | collective-permute-start | bytes 786440 | tf_op jit(solution)/shard_map/ppermute | solution.py:312
  72.9 10.6 %collective-permute-start.24 = (f32[512,128]{1,0:T(8,128)S(1)}, f32[512,128]{1,0:T(8,128)S(1)}, u32[]{:S(2)}, u32[]{:S(2)}) collective-permute-start(f32[512,128]{1,0:T(8,128)S(1)} %embed_zl.1.refs_0_), channel_id=1, source_target_pairs={{0,1},{1,0},{2,3},{3,2},{4,5},{5,4},{6,7},{7,6},{8,9},{9,8},{10,11... | collective-permute-start | bytes 786440 | tf_op jit(solution)/shard_map/ppermute | solution.py:312
  76.7 8.1 %collective-permute-start.19 = (f32[128,256]{1,0:T(8,128)S(1)}, f32[128,256]{1,0:T(8,128)S(1)}, u32[]{:S(2)}, u32[]{:S(2)}) collective-permute-start(f32[128,256]{1,0:T(8,128)S(1)} %get-tuple-element.65), channel_id=1, source_target_pairs={{0,16},{16,0},{32,48},{48,32},{1,17},{17,1},{33,49},{49,33},{2,18}... | collective-permute-start | bytes 393224 | tf_op jit(solution)/shard_map/ppermute | solution.py:312
  78.3 11.3 %collective-permute-start.20 = (f32[128,256]{1,0:T(8,128)S(1)}, f32[128,256]{1,0:T(8,128)S(1)}, u32[]{:S(2)}, u32[]{:S(2)}) collective-permute-start(f32[128,256]{1,0:T(8,128)S(1)} %get-tuple-element.63.refs_3_), channel_id=1, source_target_pairs={{0,32},{16,48},{32,0},{48,16},{1,33},{17,49},{33,1},{49,17},{2,34}... | collective-permute-start | bytes 393224 | tf_op jit(solution)/shard_map/ppermute | solution.py:312
  82.2 9.5 %collective-permute-start.21 = (f32[128,256]{1,0:T(8,128)S(1)}, f32[128,256]{1,0:T(8,128)S(1)}, u32[]{:S(2)}, u32[]{:S(2)}) collective-permute-start(f32[128,256]{1,0:T(8,128)S(1)} %get-tuple-element.66), channel_id=1, source_target_pairs={{0,48},{16,32},{32,16},{48,0},{1,49},{17,33},{33,17},{49,1},{2,50}... | collective-permute-start | bytes 393224 | tf_op jit(solution)/shard_map/ppermute | solution.py:312
  83.5 8.2 %collective-permute-start.25 = (f32[512,128]{1,0:T(8,128)S(1)}, f32[512,128]{1,0:T(8,128)S(1)}, u32[]{:S(2)}, u32[]{:S(2)}) collective-permute-start(f32[512,128]{1,0:T(8,128)S(1)} %embed_y.1.refs_2_), channel_id=1, source_target_pairs={{0,3},{1,2},{2,1},{3,0},{4,7},{5,6},{6,5},{7,4},{8,11},{9,10},{10,... | collective-permute-start | bytes 786440 | tf_op jit(solution)/shard_map/ppermute | solution.py:312
  (5 other events, 26.1 us)

commit v3 on v2

--- a/solution.py
+++ b/solution.py
@@ -34,6 +34,10 @@
 
 def block_rows(block, inner, core):
     return pl.ds(pl.multiple_of((block * CORES + core) * inner, inner), inner)
+
+
+def widen_body(z_ref, out):
+    out[...] = z_ref[...].astype(F32)
 
 
 def kern_block(za, zn, ct, norms):
@@ -174,11 +178,10 @@
     return sums[:LANES] + sums[LANES : LANES + 1] * c.astype(F32).T
 
 
-def embed_sums(kern_ref, c_ref, out, power):
+def embed_sums(kern_ref, c_ref, out, power, step):
     half, count = kern_ref.shape
     inner = count // (SIDE * SIDE)
     core = lax.axis_index("core")
-    step = 2 * SIDE
     out[...] = jnp.zeros_like(out)
 
     @pl.loop(0, count // (inner * step))
@@ -194,15 +197,26 @@
         out[...] = total
 
 
-def square_body(p, kern_ref, c_ref, z_ref, rinv_ref, out, zt, rs):
-    zt[:LANES] = (-SCALE * z_ref[...].T).astype(BF16)
-    zt[LANES:] = jnp.full((ONES, z_ref.shape[0]), SCALE, BF16)
-    rs[...] = spread(rinv_ref[p : p + 1])
-    embed_sums(kern_ref, c_ref, out, lambda kern, at: kern * kern)
+def square_body(kern_ref, c_ref, out):
+    embed_sums(kern_ref, c_ref, out, lambda kern, at: kern * kern, 2 * SIDE)
+
+
+def square_setup_body(kern_ref, c_ref, rinv_ref, z, zo, out, zt0, zt1, rs0, rs1):
+    for p, (points, zt, rs) in enumerate(((z, zt0, rs0), (zo, zt1, rs1))):
+        zt[:LANES] = (-SCALE * points[...].T).astype(BF16)
+        zt[LANES:] = jnp.full((ONES, points.shape[0]), SCALE, BF16)
+        rs[...] = spread(rinv_ref[p : p + 1])
+    square_body(kern_ref, c_ref, out)
 
 
 def cube_body(kern_ref, finv_ref, c_ref, out):
-    embed_sums(kern_ref, c_ref, out, lambda kern, at: kern * kern * (kern * finv_ref[:, at]))
+    embed_sums(
+        kern_ref,
+        c_ref,
+        out,
+        lambda kern, at: kern * kern * (kern * finv_ref[:, at]),
+        SIDE * SIDE,
+    )
 
 
 def embed_grads(sums, ts, rs, points, outs):
@@ -328,7 +342,7 @@
         v = call(swap_add_body, [(parts, *rows)], v, swap(v, "core", 1), name="sum_core")
         return lax.all_to_all(v, ("zl", "y"), 0, 0)
 
-    z_own = embeddings.astype(F32)
+    z_own = call(widen_body, [(half, width)], embeddings, name="widen", flops=HINT)
     z_other = swap(z_own, "core", 1)
     kern_scratch = [pltpu.VMEM((half, width), BF16), pltpu.VMEM((half, LANES), F32)]
     kern_own, row, ct, norms = call(
@@ -364,22 +378,24 @@
     kerns = (kern_own, kern_other)
     sums = (half, 2 * LANES)
     work = 4 * half * count * 2 * LANES
-    lanes = ((width + ONES, half), (half, LANES))
-    squares = [
-        call(
-            functools.partial(square_body, p),
-            [sums, jax.ShapeDtypeStruct(lanes[0], BF16), lanes[1]],
-            kern,
-            centres,
-            points,
-            rinv,
-            limit=20,
-            name="squares",
-            flops=work,
-        )
-        for p, (kern, points) in enumerate(zip(kerns, (z_own, z_other)))
-    ]
-    squares, zt, rs = zip(*squares)
+    zt_shape = jax.ShapeDtypeStruct((width + ONES, half), BF16)
+    squares = call(
+        square_body, [sums], kern_own, centres, limit=20, name="squares_own", flops=work
+    )
+    more, *data = call(
+        square_setup_body,
+        [sums, zt_shape, zt_shape, (half, LANES), (half, LANES)],
+        kern_other,
+        centres,
+        rinv,
+        z_own,
+        z_other,
+        limit=20,
+        name="squares_other",
+        flops=work,
+    )
+    squares = (squares, more)
+    rs = data[CORES:]
     freq = call(
         add_body, [freq.shape], *around([freq] * SIDE, "x"), name="sum_x", after=squares[:1]
     )
@@ -405,7 +421,7 @@
 
     setup = [pltpu.VMEM((CORES, half, LANES), F32)]
     piece, part, pair = (width, SIDE * inner), (width // 2, SIDE * inner), (width, 2 * inner)
-    base = (*kerns, finv, centres, *zt, *rs)
+    base = (*kerns, finv, centres, *data)
     low, high, tinv = call(
         far_body, [part, part, rows], *base, *target, scratch=setup, limit=24, name="grad_far"
     )

time: 92.7 us -> 91.1 us (0.983)
    pallas_call x24 -> x25, Pallas kernels: 25.7 us -> 25.2 us  [call(): pl.pallas_call(kernel, out_shape=shapes, in_specs=[VMEM] * used + [ANY] *...]
  transfers between devices with their start and end apart: 26 -> 26, of which waited for: 10 -> 11; matrix products, arithmetic and copies ran while one was open for 0% -> 0% of each run, Pallas kernels for 20% -> 20%
where the time goes in v3:
time: 91.1 us; the launch traced here: 90.5 us
  starting transfers between devices  35.9 us (39%)
  Pallas kernels  25.2 us (28%)
  waiting for transfers between devices  16.4 us (18%)
  blocking collectives  10.6 us (12%)
  local copies, waits for them, and re-layouts  1.52 us (2%)
    ppermute x26, starting transfers between devices, swap(): lax.ppermute(v, axis, [(i, i ^ s) for i in range(lax.axis_size(axis))])  35.9 us
    pallas_call x25, Pallas kernels, call(): pl.pallas_call(kernel, out_shape=shapes, in_specs=[VMEM] * used + [ANY] *...  25.2 us
    ppermute x26, waiting for transfers between devices, swap(): lax.ppermute(v, axis, [(i, i ^ s) for i in range(lax.axis_size(axis))])  16.4 us
    all_to_all x1, blocking collectives, over_ctr(): return lax.all_to_all(v, ('zl', 'y'), 0, 0)  10.6 us
  transfers between devices with their start and end apart: 26, of which 11 were waited for; matrix products, arithmetic and copies ran while one was open for 0% of the time, Pallas kernels for 20%

profile of v3, /device:TPU:32, one launch (start us, length us, event | category | flops | bytes accessed | tf_op | source)
XLA Modules:
  0.0 90.5 jit_solution(2141323595347768655)
XLA Ops:
  2.3 2.0 %kern_own.1 = (f32[512,4096]{1,0:T(8,128)S(1)}, f32[1,512]{1,0:T(1,128)S(1)}, bf16[128,4096]{1,0:T(8,128)(2,1)S(1)}, f32[1,4096]{1,0:T(1,128)S(1)}) custom-call(f32[512,128]{1,0:T(8,128)S(1)} %widen.1.refs_0_.refs_3_, bf16[8192,128]{1,0:T(8,128)(2,1)S(1)} %copy-done), custom_call_target="tpu_custom_call" | custom-call | bytes 2359296 | tf_op jit(solution)/shard_map/kern_own/pallas_call | solution.py:312
  4.3 1.7 %kern_other.1 = (f32[512,4096]{1,0:T(8,128)S(1)}, f32[2,512]{1,0:T(2,128)S(1)}) custom-call(f32[512,128]{1,0:T(8,128)S(1)} %collective-permute-done.refs_0_.refs_4_, bf16[128,4096]{1,0:T(8,128)(2,1)S(1)} %get-tuple-element.36.refs_1_, f32[1,4096]{1,0:T(1,128)S(1)} %get-tuple-element.37.refs_2_, f32[1,512]{1,0:T(1,128)S(1)} %get-tuple-element.38.refs_3_), custom_call_target="tpu_custom_call" | custom-call | bytes 1329152 | tf_op jit(solution)/shard_map/kern_other/pallas_call | solution.py:312
  7.2 10.6 %all_to_all.5.refs_2_ = f32[8,2,512]{2,1,0:T(2,128)S(1)} all-to-all(f32[8,2,512]{2,1,0:T(2,128)S(1)} %sum_core.1), channel_id=1, replica_groups=mesh['x'=4,'h'=4,'core'=2,'zl'=2,'y'=4] {'zl','y'}, dimensions={0} | all-to-all | bytes 65536 | tf_op jit(solution)/shard_map/all_to_all | solution.py:343
  17.8 1.6 %freq.1 = (f32[1,4096]{1,0:T(1,128)S(1)}, f32[2,512]{1,0:T(2,128)S(1)}) custom-call(f32[512,4096]{1,0:T(8,128)S(1)} %get-tuple-element.35.refs_0_, f32[512,4096]{1,0:T(8,128)S(1)} %get-tuple-element.39.refs_1_.refs_0_, f32[8,2,512]{2,1,0:T(2,128)S(1)} %all_to_all.5.refs_2_), custom_call_target="tpu_custom_call" | custom-call | bytes 16809984 | tf_op jit(solution)/shard_map/freq/pallas_call | solution.py:312
  19.4 3.1 %collective-permute-start.4 = (f32[1,4096]{1,0:T(1,128)S(1)}, f32[1,4096]{1,0:T(1,128)S(1)}, u32[]{:S(2)}, u32[]{:S(2)}) collective-permute-start(f32[1,4096]{1,0:T(1,128)S(1)} %get-tuple-element.41.refs_0_), channel_id=1, source_target_pairs={{0,128},{64,192},{128,0},{192,64},{1,129},{65,193},{129,1},{193,65... | collective-permute-start | bytes 49160 | tf_op jit(solution)/shard_map/ppermute | solution.py:326
  23.6 2.6 %squares_own.1.refs_4_.refs_7_ = f32[512,256]{1,0:T(8,128)S(1)} custom-call(f32[512,4096]{1,0:T(8,128)S(1)} %get-tuple-element.35.refs_0_, bf16[8192,128]{1,0:T(8,128)(2,1)S(1)} %copy-done), custom_call_target="tpu_custom_call" | custom-call | flops 2147483648 | bytes 10485760 | tf_op jit(solution)/shard_map/squares_own/pallas_call | solution.py:312
  27.4 6.4 %collective-permute-start.7 = (f32[1,4096]{1,0:T(1,128)S(1)}, f32[1,4096]{1,0:T(1,128)S(1)}, u32[]{:S(2)}, u32[]{:S(2)}) collective-permute-start(f32[1,4096]{1,0:T(1,128)S(1)} %sum_x.1.refs_2_), channel_id=1, source_target_pairs={{0,32},{16,48},{32,0},{48,16},{1,33},{17,49},{33,1},{49,17},{2,34}... | collective-permute-start | bytes 49160 | tf_op jit(solution)/shard_map/ppermute | solution.py:326
  35.3 2.9 %squares_other.1 = (f32[512,256]{1,0:T(8,128)S(1)}, bf16[144,512]{1,0:T(8,128)(2,1)S(1)}, bf16[144,512]{1,0:T(8,128)(2,1)S(1)}, f32[512,128]{1,0:T(8,128)S(1)}, f32[512,128]{1,0:T(8,128)S(1)}) custom-call(f32[512,4096]{1,0:T(8,128)S(1)} %get-tuple-element.39.refs_1_.refs_0_, bf16[8192,128]{1,0:T(8,128)(2,1)S(1)} %copy-done, ...), custom_call_target="tpu_custom_call" | custom-call | flops 2147483648 | bytes 11014144 | tf_op jit(solution)/shard_map/squares_other/pallas_call | solution.py:312
  38.2 1.4 %collective-permute-done.6.refs_4_ = f32[1,4096]{1,0:T(1,128)S(1)} collective-permute-done((f32[1,4096]{1,0:T(1,128)S(1)}, f32[1,4096]{1,0:T(1,128)S(1)}, u32[]{:S(2)}, u32[]{:S(2)}) %collective-permute-start.6) | collective-permute-done | bytes 16416 | tf_op jit(solution)/shard_map/ppermute | solution.py:326
  39.7 1.8 %target.1 = (f32[2,512]{1,0:T(2,128)S(1)}, f32[1,4096]{1,0:T(1,128)S(1)}) custom-call(f32[512,4096]{1,0:T(8,128)S(1)} %get-tuple-element.35.refs_0_, f32[512,4096]{1,0:T(8,128)S(1)} %get-tuple-element.39.refs_1_.refs_0_, f32[1,4096]{1,0:T(1,128)S(1)} %sum_x.1.refs_2_, f32[1,4096]{1,0:T(1,128)S(1)} %collective-permute-done.5.refs_3_, ...), custom_call_target="tpu_custom_call" | custom-call | bytes 17399808 | tf_op jit(solution)/shard_map/target/pallas_call | solution.py:312
  44.1 2.4 %cubes.3.refs_6_ = f32[512,256]{1,0:T(8,128)S(1)} custom-call(f32[512,4096]{1,0:T(8,128)S(1)} %get-tuple-element.39.refs_1_.refs_0_, f32[1,4096]{1,0:T(1,128)S(1)} %get-tuple-element.44.refs_2_.refs_1_, bf16[8192,128]{1,0:T(8,128)(2,1)S(1)} %copy-done), custom_call_target="tpu_custom_call" | custom-call | flops 2147483648 | bytes 10502144 | tf_op jit(solution)/shard_map/cubes/pallas_call | solution.py:312
  47.8 2.1 %collective-permute-start.11 = (f32[2,512]{1,0:T(2,128)S(1)}, f32[2,512]{1,0:T(2,128)S(1)}, u32[]{:S(2)}, u32[]{:S(2)}) collective-permute-start(f32[2,512]{1,0:T(2,128)S(1)} %target_zl.1.refs_8_), channel_id=1, source_target_pairs={{0,3},{1,2},{2,1},{3,0},{4,7},{5,6},{6,5},{7,4},{8,11},{9,10},{10,... | collective-permute-start | bytes 12296 | tf_op jit(solution)/shard_map/ppermute | solution.py:326
  50.2 2.4 %cubes.2.refs_5_ = f32[512,256]{1,0:T(8,128)S(1)} custom-call(f32[512,4096]{1,0:T(8,128)S(1)} %get-tuple-element.35.refs_0_, f32[1,4096]{1,0:T(1,128)S(1)} %get-tuple-element.44.refs_2_.refs_1_, bf16[8192,128]{1,0:T(8,128)(2,1)S(1)} %copy-done), custom_call_target="tpu_custom_call" | custom-call | flops 2147483648 | bytes 10502144 | tf_op jit(solution)/shard_map/cubes/pallas_call | solution.py:312
  53.5 1.7 %grad_far.1 = (f32[64,1024]{1,0:T(8,128)S(1)}, f32[64,1024]{1,0:T(8,128)S(1)}, f32[2,512]{1,0:T(2,128)S(1)}) custom-call(f32[512,4096]{1,0:T(8,128)S(1)} %get-tuple-element.35.refs_0_, f32[512,4096]{1,0:T(8,128)S(1)} %get-tuple-element.39.refs_1_.refs_0_, f32[1,4096]{1,0:T(1,128)S(1)} %get-tuple-element.44.refs_2_.refs_1_, bf16[8192,128]{1,0:T(8,128)(2,1)S(1)} %copy-done, ...), custom_call_target="tpu_custom_call" | custom-call | bytes 19726336 | tf_op jit(solution)/shard_map/grad_far/pallas_call | solution.py:312
  56.1 2.1 %collective-permute-start.14 = (f32[64,1024]{1,0:T(8,128)S(1)}, f32[64,1024]{1,0:T(8,128)S(1)}, u32[]{:S(2)}, u32[]{:S(2)}) collective-permute-start(f32[64,1024]{1,0:T(8,128)S(1)} %get-tuple-element.54), channel_id=1, source_target_pairs={{0,192},{64,128},{128,64},{192,0},{1,193},{65,129},{129,65},{193,1... | collective-permute-start | bytes 786440 | tf_op jit(solution)/shard_map/ppermute | solution.py:326
  58.6 3.1 %grad_mid.1 = (f32[128,1024]{1,0:T(8,128)S(1)}, f32[128,1024]{1,0:T(8,128)S(1)}) custom-call(f32[512,4096]{1,0:T(8,128)S(1)} %get-tuple-element.35.refs_0_, f32[512,4096]{1,0:T(8,128)S(1)} %get-tuple-element.39.refs_1_.refs_0_, f32[1,4096]{1,0:T(1,128)S(1)} %get-tuple-element.44.refs_2_.refs_1_, bf16[8192,128]{1,0:T(8,128)(2,1)S(1)} %copy-done, ...), custom_call_target="tpu_custom_call" | custom-call | bytes 19714048 | tf_op jit(solution)/shard_map/grad_mid/pallas_call | solution.py:312
  61.9 1.9 %collective-permute-done.14.refs_12_.refs_3_ = f32[64,1024]{1,0:T(8,128)S(1)} collective-permute-done((f32[64,1024]{1,0:T(8,128)S(1)}, f32[64,1024]{1,0:T(8,128)S(1)}, u32[]{:S(2)}, u32[]{:S(2)}) %collective-permute-start.14) | collective-permute-done | bytes 262176 | tf_op jit(solution)/shard_map/ppermute | solution.py:326
  65.1 2.2 %collective-permute-start.18 = (f32[128,512]{1,0:T(8,128)S(1)}, f32[128,512]{1,0:T(8,128)S(1)}, u32[]{:S(2)}, u32[]{:S(2)}) collective-permute-start(f32[128,512]{1,0:T(8,128)S(1)} %get-tuple-element.60), channel_id=1, source_target_pairs={{0,192},{64,128},{128,64},{192,0},{1,193},{65,129},{129,65},{193,1... | collective-permute-start | bytes 786440 | tf_op jit(solution)/shard_map/ppermute | solution.py:326
  67.3 1.7 %second_b.1 = (f32[128,512]{1,0:T(8,128)S(1)}, f32[128,512]{1,0:T(8,128)S(1)}, f32[128,1024]{1,0:T(8,128)S(1)}) custom-call(f32[512,4096]{1,0:T(8,128)S(1)} %get-tuple-element.35.refs_0_, f32[512,4096]{1,0:T(8,128)S(1)} %get-tuple-element.39.refs_1_.refs_0_, f32[1,4096]{1,0:T(1,128)S(1)} %get-tuple-element.44.refs_2_.refs_1_, bf16[8192,128]{1,0:T(8,128)(2,1)S(1)} %copy-done, ...), custom_call_target="tpu_custom_call" | custom-call | flops 10000000000 | bytes 21549056 | tf_op jit(solution)/shard_map/second_b/pallas_call | solution.py:312
  68.9 1.7 %collective-permute-start.15 = (f32[128,512]{1,0:T(8,128)S(1)}, f32[128,512]{1,0:T(8,128)S(1)}, u32[]{:S(2)}, u32[]{:S(2)}) collective-permute-start(f32[128,512]{1,0:T(8,128)S(1)} %get-tuple-element.57), channel_id=1, source_target_pairs={{0,64},{64,0},{128,192},{192,128},{1,65},{65,1},{129,193},{193,129... | collective-permute-start | bytes 786440 | tf_op jit(solution)/shard_map/ppermute | solution.py:326
  75.0 1.6 %collective-permute-start.19 = (f32[128,256]{1,0:T(8,128)S(1)}, f32[128,256]{1,0:T(8,128)S(1)}, u32[]{:S(2)}, u32[]{:S(2)}) collective-permute-start(f32[128,256]{1,0:T(8,128)S(1)} %get-tuple-element.63), channel_id=1, source_target_pairs={{0,16},{16,0},{32,48},{48,32},{1,17},{17,1},{33,49},{49,33},{2,18}... | collective-permute-start | bytes 393224 | tf_op jit(solution)/shard_map/ppermute | solution.py:326
  76.6 3.8 %collective-permute-start.20 = (f32[128,256]{1,0:T(8,128)S(1)}, f32[128,256]{1,0:T(8,128)S(1)}, u32[]{:S(2)}, u32[]{:S(2)}) collective-permute-start(f32[128,256]{1,0:T(8,128)S(1)} %get-tuple-element.61.refs_3_), channel_id=1, source_target_pairs={{0,32},{16,48},{32,0},{48,16},{1,33},{17,49},{33,1},{49,17},{2,34}... | collective-permute-start | bytes 393224 | tf_op jit(solution)/shard_map/ppermute | solution.py:326
  83.1 4.6 %collective-permute-done.20.refs_2_ = f32[128,256]{1,0:T(8,128)S(1)} collective-permute-done((f32[128,256]{1,0:T(8,128)S(1)}, f32[128,256]{1,0:T(8,128)S(1)}, u32[]{:S(2)}, u32[]{:S(2)}) %collective-permute-start.20) | collective-permute-done | bytes 131104 | tf_op jit(solution)/shard_map/ppermute | solution.py:326
  87.7 1.9 %collective-permute-done.21.refs_1_ = f32[128,256]{1,0:T(8,128)S(1)} collective-permute-done((f32[128,256]{1,0:T(8,128)S(1)}, f32[128,256]{1,0:T(8,128)S(1)}, u32[]{:S(2)}, u32[]{:S(2)}) %collective-permute-start.21) | collective-permute-done | bytes 131104 | tf_op jit(solution)/shard_map/ppermute | solution.py:326
  (60 shorter events, 22.5 us)
Async XLA Ops:
  1.7 2.6 %collective-permute-start = (f32[512,128]{1,0:T(8,128)S(1)}, f32[512,128]{1,0:T(8,128)S(1)}, u32[]{:S(2)}, u32[]{:S(2)}) collective-permute-start(f32[512,128]{1,0:T(8,128)S(1)} %widen.1.refs_0_.refs_3_), channel_id=1, source_target_pairs={{0,8},{8,0},{1,9},{9,1},{2,10},{10,2},{3,11},{11,3},{4,12},{12,4},... | collective-permute-start | bytes 786440 | tf_op jit(solution)/shard_map/ppermute | solution.py:326
  19.4 6.9 %collective-permute-start.4 = (f32[1,4096]{1,0:T(1,128)S(1)}, f32[1,4096]{1,0:T(1,128)S(1)}, u32[]{:S(2)}, u32[]{:S(2)}) collective-permute-start(f32[1,4096]{1,0:T(1,128)S(1)} %get-tuple-element.41.refs_0_), channel_id=1, source_target_pairs={{0,128},{64,192},{128,0},{192,64},{1,129},{65,193},{129,1},{193,65... | collective-permute-start | bytes 49160 | tf_op jit(solution)/shard_map/ppermute | solution.py:326
  22.5 4.9 %collective-permute-start.3 = (f32[1,4096]{1,0:T(1,128)S(1)}, f32[1,4096]{1,0:T(1,128)S(1)}, u32[]{:S(2)}, u32[]{:S(2)}) collective-permute-start(f32[1,4096]{1,0:T(1,128)S(1)} %get-tuple-element.41.refs_0_), channel_id=1, source_target_pairs={{0,192},{64,128},{128,64},{192,0},{1,193},{65,129},{129,65},{193,1... | collective-permute-start | bytes 49160 | tf_op jit(solution)/shard_map/ppermute | solution.py:326
  23.6 3.8 %collective-permute-start.2 = (f32[1,4096]{1,0:T(1,128)S(1)}, f32[1,4096]{1,0:T(1,128)S(1)}, u32[]{:S(2)}, u32[]{:S(2)}) collective-permute-start(f32[1,4096]{1,0:T(1,128)S(1)} %get-tuple-element.41.refs_0_), channel_id=1, source_target_pairs={{0,64},{64,0},{128,192},{192,128},{1,65},{65,1},{129,193},{193,129... | collective-permute-start | bytes 49160 | tf_op jit(solution)/shard_map/ppermute | solution.py:326
  27.4 10.8 %collective-permute-start.7 = (f32[1,4096]{1,0:T(1,128)S(1)}, f32[1,4096]{1,0:T(1,128)S(1)}, u32[]{:S(2)}, u32[]{:S(2)}) collective-permute-start(f32[1,4096]{1,0:T(1,128)S(1)} %sum_x.1.refs_2_), channel_id=1, source_target_pairs={{0,32},{16,48},{32,0},{48,16},{1,33},{17,49},{33,1},{49,17},{2,34}... | collective-permute-start | bytes 49160 | tf_op jit(solution)/shard_map/ppermute | solution.py:326
  33.8 5.8 %collective-permute-start.6 = (f32[1,4096]{1,0:T(1,128)S(1)}, f32[1,4096]{1,0:T(1,128)S(1)}, u32[]{:S(2)}, u32[]{:S(2)}) collective-permute-start(f32[1,4096]{1,0:T(1,128)S(1)} %sum_x.1.refs_2_), channel_id=1, source_target_pairs={{0,48},{16,32},{32,16},{48,0},{1,49},{17,33},{33,17},{49,1},{2,50}... | collective-permute-start | bytes 49160 | tf_op jit(solution)/shard_map/ppermute | solution.py:326
  34.4 5.3 %collective-permute-start.5 = (f32[1,4096]{1,0:T(1,128)S(1)}, f32[1,4096]{1,0:T(1,128)S(1)}, u32[]{:S(2)}, u32[]{:S(2)}) collective-permute-start(f32[1,4096]{1,0:T(1,128)S(1)} %sum_x.1.refs_2_), channel_id=1, source_target_pairs={{0,16},{16,0},{32,48},{48,32},{1,17},{17,1},{33,49},{49,33},{2,18}... | collective-permute-start | bytes 49160 | tf_op jit(solution)/shard_map/ppermute | solution.py:326
  42.7 3.9 %collective-permute-start.9 = (f32[2,512]{1,0:T(2,128)S(1)}, f32[2,512]{1,0:T(2,128)S(1)}, u32[]{:S(2)}, u32[]{:S(2)}) collective-permute-start(f32[2,512]{1,0:T(2,128)S(1)} %target_core.1.refs_0_), channel_id=1, source_target_pairs={{0,4},{4,0},{1,5},{5,1},{2,6},{6,2},{3,7},{7,3},{8,12},{12,8},{9,1... | collective-permute-start | bytes 12296 | tf_op jit(solution)/shard_map/ppermute | solution.py:326
  46.6 6.0 %collective-permute-start.12 = (f32[2,512]{1,0:T(2,128)S(1)}, f32[2,512]{1,0:T(2,128)S(1)}, u32[]{:S(2)}, u32[]{:S(2)}) collective-permute-start(f32[2,512]{1,0:T(2,128)S(1)} %target_zl.1.refs_8_), channel_id=1, source_target_pairs={{0,2},{1,3},{2,0},{3,1},{4,6},{5,7},{6,4},{7,5},{8,10},{9,11},{10,... | collective-permute-start | bytes 12296 | tf_op jit(solution)/shard_map/ppermute | solution.py:326
  47.8 4.8 %collective-permute-start.11 = (f32[2,512]{1,0:T(2,128)S(1)}, f32[2,512]{1,0:T(2,128)S(1)}, u32[]{:S(2)}, u32[]{:S(2)}) collective-permute-start(f32[2,512]{1,0:T(2,128)S(1)} %target_zl.1.refs_8_), channel_id=1, source_target_pairs={{0,3},{1,2},{2,1},{3,0},{4,7},{5,6},{6,5},{7,4},{8,11},{9,10},{10,... | collective-permute-start | bytes 12296 | tf_op jit(solution)/shard_map/ppermute | solution.py:326
  49.9 3.6 %collective-permute-start.10 = (f32[2,512]{1,0:T(2,128)S(1)}, f32[2,512]{1,0:T(2,128)S(1)}, u32[]{:S(2)}, u32[]{:S(2)}) collective-permute-start(f32[2,512]{1,0:T(2,128)S(1)} %target_zl.1.refs_8_), channel_id=1, source_target_pairs={{0,1},{1,0},{2,3},{3,2},{4,5},{5,4},{6,7},{7,6},{8,9},{9,8},{10,11... | collective-permute-start | bytes 12296 | tf_op jit(solution)/shard_map/ppermute | solution.py:326
  55.2 6.7 %collective-permute-start.13 = (f32[64,1024]{1,0:T(8,128)S(1)}, f32[64,1024]{1,0:T(8,128)S(1)}, u32[]{:S(2)}, u32[]{:S(2)}) collective-permute-start(f32[64,1024]{1,0:T(8,128)S(1)} %get-tuple-element.53), channel_id=1, source_target_pairs={{0,64},{64,0},{128,192},{192,128},{1,65},{65,1},{129,193},{193,129... | collective-permute-start | bytes 786440 | tf_op jit(solution)/shard_map/ppermute | solution.py:326
  56.1 7.6 %collective-permute-start.14 = (f32[64,1024]{1,0:T(8,128)S(1)}, f32[64,1024]{1,0:T(8,128)S(1)}, u32[]{:S(2)}, u32[]{:S(2)}) collective-permute-start(f32[64,1024]{1,0:T(8,128)S(1)} %get-tuple-element.54), channel_id=1, source_target_pairs={{0,192},{64,128},{128,64},{192,0},{1,193},{65,129},{129,65},{193,1... | collective-permute-start | bytes 786440 | tf_op jit(solution)/shard_map/ppermute | solution.py:326
  58.5 5.2 %collective-permute-start.22 = (f32[512,128]{1,0:T(8,128)S(1)}, f32[512,128]{1,0:T(8,128)S(1)}, u32[]{:S(2)}, u32[]{:S(2)}) collective-permute-start(f32[512,128]{1,0:T(8,128)S(1)} %get-tuple-element.65), channel_id=1, source_target_pairs={{0,8},{8,0},{1,9},{9,1},{2,10},{10,2},{3,11},{11,3},{4,12},{12,4},... | collective-permute-start | bytes 786440 | tf_op jit(solution)/shard_map/ppermute | solution.py:326
  63.8 8.0 %collective-permute-start.23 = (f32[512,128]{1,0:T(8,128)S(1)}, f32[512,128]{1,0:T(8,128)S(1)}, u32[]{:S(2)}, u32[]{:S(2)}) collective-permute-start(f32[512,128]{1,0:T(8,128)S(1)} %embed_core.1.refs_0_), channel_id=1, source_target_pairs={{0,4},{4,0},{1,5},{5,1},{2,6},{6,2},{3,7},{7,3},{8,12},{12,8},{9,1... | collective-permute-start | bytes 786440 | tf_op jit(solution)/shard_map/ppermute | solution.py:326
  65.0 9.0 %collective-permute-start.17 = (f32[128,512]{1,0:T(8,128)S(1)}, f32[128,512]{1,0:T(8,128)S(1)}, u32[]{:S(2)}, u32[]{:S(2)}) collective-permute-start(f32[128,512]{1,0:T(8,128)S(1)} %get-tuple-element.59), channel_id=1, source_target_pairs={{0,64},{64,0},{128,192},{192,128},{1,65},{65,1},{129,193},{193,129... | collective-permute-start | bytes 786440 | tf_op jit(solution)/shard_map/ppermute | solution.py:326
  65.1 9.8 %collective-permute-start.18 = (f32[128,512]{1,0:T(8,128)S(1)}, f32[128,512]{1,0:T(8,128)S(1)}, u32[]{:S(2)}, u32[]{:S(2)}) collective-permute-start(f32[128,512]{1,0:T(8,128)S(1)} %get-tuple-element.60), channel_id=1, source_target_pairs={{0,192},{64,128},{128,64},{192,0},{1,193},{65,129},{129,65},{193,1... | collective-permute-start | bytes 786440 | tf_op jit(solution)/shard_map/ppermute | solution.py:326
  68.9 11.4 %collective-permute-start.15 = (f32[128,512]{1,0:T(8,128)S(1)}, f32[128,512]{1,0:T(8,128)S(1)}, u32[]{:S(2)}, u32[]{:S(2)}) collective-permute-start(f32[128,512]{1,0:T(8,128)S(1)} %get-tuple-element.57), channel_id=1, source_target_pairs={{0,64},{64,0},{128,192},{192,128},{1,65},{65,1},{129,193},{193,129... | collective-permute-start | bytes 786440 | tf_op jit(solution)/shard_map/ppermute | solution.py:326
  70.6 9.8 %collective-permute-start.16 = (f32[128,512]{1,0:T(8,128)S(1)}, f32[128,512]{1,0:T(8,128)S(1)}, u32[]{:S(2)}, u32[]{:S(2)}) collective-permute-start(f32[128,512]{1,0:T(8,128)S(1)} %get-tuple-element.58), channel_id=1, source_target_pairs={{0,192},{64,128},{128,64},{192,0},{1,193},{65,129},{129,65},{193,1... | collective-permute-start | bytes 786440 | tf_op jit(solution)/shard_map/ppermute | solution.py:326
  71.8 10.0 %collective-permute-start.24 = (f32[512,128]{1,0:T(8,128)S(1)}, f32[512,128]{1,0:T(8,128)S(1)}, u32[]{:S(2)}, u32[]{:S(2)}) collective-permute-start(f32[512,128]{1,0:T(8,128)S(1)} %embed_zl.1.refs_0_), channel_id=1, source_target_pairs={{0,1},{1,0},{2,3},{3,2},{4,5},{5,4},{6,7},{7,6},{8,9},{9,8},{10,11... | collective-permute-start | bytes 786440 | tf_op jit(solution)/shard_map/ppermute | solution.py:326
  75.0 8.1 %collective-permute-start.19 = (f32[128,256]{1,0:T(8,128)S(1)}, f32[128,256]{1,0:T(8,128)S(1)}, u32[]{:S(2)}, u32[]{:S(2)}) collective-permute-start(f32[128,256]{1,0:T(8,128)S(1)} %get-tuple-element.63), channel_id=1, source_target_pairs={{0,16},{16,0},{32,48},{48,32},{1,17},{17,1},{33,49},{49,33},{2,18}... | collective-permute-start | bytes 393224 | tf_op jit(solution)/shard_map/ppermute | solution.py:326
  76.6 11.1 %collective-permute-start.20 = (f32[128,256]{1,0:T(8,128)S(1)}, f32[128,256]{1,0:T(8,128)S(1)}, u32[]{:S(2)}, u32[]{:S(2)}) collective-permute-start(f32[128,256]{1,0:T(8,128)S(1)} %get-tuple-element.61.refs_3_), channel_id=1, source_target_pairs={{0,32},{16,48},{32,0},{48,16},{1,33},{17,49},{33,1},{49,17},{2,34}... | collective-permute-start | bytes 393224 | tf_op jit(solution)/shard_map/ppermute | solution.py:326
  80.4 9.2 %collective-permute-start.21 = (f32[128,256]{1,0:T(8,128)S(1)}, f32[128,256]{1,0:T(8,128)S(1)}, u32[]{:S(2)}, u32[]{:S(2)}) collective-permute-start(f32[128,256]{1,0:T(8,128)S(1)} %get-tuple-element.64), channel_id=1, source_target_pairs={{0,48},{16,32},{32,16},{48,0},{1,49},{17,33},{33,17},{49,1},{2,50}... | collective-permute-start | bytes 393224 | tf_op jit(solution)/shard_map/ppermute | solution.py:326
  81.8 7.9 %collective-permute-start.25 = (f32[512,128]{1,0:T(8,128)S(1)}, f32[512,128]{1,0:T(8,128)S(1)}, u32[]{:S(2)}, u32[]{:S(2)}) collective-permute-start(f32[512,128]{1,0:T(8,128)S(1)} %embed_y.1.refs_2_), channel_id=1, source_target_pairs={{0,3},{1,2},{2,1},{3,0},{4,7},{5,6},{6,5},{7,4},{8,11},{9,10},{10,... | collective-permute-start | bytes 786440 | tf_op jit(solution)/shard_map/ppermute | solution.py:326
  (5 other events, 18.6 us)

commit v4 on v3

--- a/solution.py
+++ b/solution.py
@@ -40,14 +40,27 @@
     out[...] = z_ref[...].astype(F32)
 
 
-def kern_block(za, zn, ct, norms):
-    cross = jnp.dot(za[...], ct, preferred_element_type=F32)
-    return 1.0 / (cross + norms + tile_lanes(zn[...], ct.shape[1]))
-
-
-def kern_setup(part, za, zn):
-    zn[...] = jnp.broadcast_to(jnp.sum(part * part, axis=1, keepdims=True) + 1.0, zn.shape)
-    za[...] = (-2.0 * part).astype(BF16)
+def three_terms(value):
+    first = value.astype(BF16).astype(F32)
+    second = (value - first).astype(BF16).astype(F32)
+    return first, second, value - first - second
+
+
+def kern_block(za, ct):
+    depth = za.shape[1] - ct.shape[0]
+    ct = jnp.concatenate([ct, jnp.zeros((depth, ct.shape[1]), BF16)], axis=0)
+    return 1.0 / jnp.dot(za[...], ct, preferred_element_type=F32)
+
+
+def kern_setup(part, za):
+    n0, n1, n2 = three_terms(
+        jnp.broadcast_to(jnp.sum(part * part, axis=1, keepdims=True) + 1.0, part.shape)
+    )
+    lane = lax.broadcasted_iota(jnp.int32, part.shape, 1)
+    norms = jnp.where(lane == 0, n0, jnp.where(lane == 1, n1, n2))
+    ones = jnp.where(lane < 6, 1.0, 0.0)
+    za[:, :LANES] = (-2.0 * part).astype(BF16)
+    za[:, LANES:] = jnp.where(lane < 3, norms, ones).astype(BF16)
 
 
 def lane_sums(total, kern):
@@ -56,33 +69,36 @@
     return total
 
 
-def own_body(z_ref, c_ref, kern_ref, row_ref, ct_ref, norm_ref, za, zn):
+def own_body(z_ref, c_ref, kern_ref, row_ref, ct_ref, za):
     half, count = kern_ref.shape
     inner = count // (SIDE * SIDE)
     core = lax.axis_index("core")
-    kern_setup(z_ref[...], za, zn)
+    kern_setup(z_ref[...], za)
     total = jnp.zeros((half, LANES), F32)
+    row = lax.broadcasted_iota(jnp.int32, (ONES, inner), 0)
     for b in range(count // inner):
         at = slice(b * inner, (b + 1) * inner)
         ct = c_ref[block_rows(b, inner, core), :].T
         norms = jnp.sum(jnp.square(ct.astype(F32)), axis=0, keepdims=True)
+        n0, n1, n2 = (jnp.broadcast_to(n, row.shape) for n in three_terms(norms))
+        norms = jnp.where(row == 3, n0, jnp.where(row == 4, n1, jnp.where(row == 5, n2, 0.0)))
+        ct = jnp.concatenate([ct, jnp.where(row < 3, 1.0, norms).astype(BF16)], axis=0)
         ct_ref[:, at] = ct
-        norm_ref[:, at] = norms
-        kern = kern_block(za, zn, ct, norms)
+        kern = kern_block(za, ct)
         kern_ref[:, at] = kern
         total = lane_sums(total, kern)
     row_ref[...] = jnp.sum(total.T, axis=0, keepdims=True)
 
 
-def other_body(zo_ref, ct_ref, norm_ref, row_ref, kern_ref, rows_ref, za, zn):
+def other_body(zo_ref, ct_ref, row_ref, kern_ref, rows_ref, za):
     half, count = kern_ref.shape
     step = 256
     rows_ref[:1] = row_ref[...]
-    kern_setup(zo_ref[...], za, zn)
+    kern_setup(zo_ref[...], za)
     total = jnp.zeros((half, LANES), F32)
     for b in range(count // step):
         at = slice(b * step, (b + 1) * step)
-        kern = kern_block(za, zn, ct_ref[:, at], norm_ref[:, at])
+        kern = kern_block(za, ct_ref[:, at])
         kern_ref[:, at] = kern
         total = lane_sums(total, kern)
     rows_ref[1:] = jnp.sum(total.T, axis=0, keepdims=True)
@@ -344,10 +360,10 @@
 
     z_own = call(widen_body, [(half, width)], embeddings, name="widen", flops=HINT)
     z_other = swap(z_own, "core", 1)
-    kern_scratch = [pltpu.VMEM((half, width), BF16), pltpu.VMEM((half, LANES), F32)]
-    kern_own, row, ct, norms = call(
+    kern_scratch = [pltpu.VMEM((half, 2 * LANES), BF16)]
+    kern_own, row, ct = call(
         own_body,
-        [(half, count), (1, half), jax.ShapeDtypeStruct((width, count), BF16), (1, count)],
+        [(half, count), (1, half), jax.ShapeDtypeStruct((width + ONES, count), BF16)],
         z_own,
         centres,
         scratch=kern_scratch,
@@ -359,7 +375,6 @@
         [(half, count), rows],
         z_other,
         ct,
-        norms,
         row,
         scratch=kern_scratch,
         limit=16,

time: 91.1 us -> 90.4 us (level)
  transfers between devices with their start and end apart: 26 -> 26, of which waited for: 11 -> 11; matrix products, arithmetic and copies ran while one was open for 0% -> 0% of each run, Pallas kernels for 20% -> 19%
where the time goes in v4:
time: 90.4 us; the launch traced here: 89.9 us
  starting transfers between devices  35.9 us (40%)
  Pallas kernels  24.4 us (27%)
  waiting for transfers between devices  16.6 us (18%)
  blocking collectives  10.6 us (12%)
  local copies, waits for them, and re-layouts  1.52 us (2%)
    ppermute x26, starting transfers between devices, swap(): lax.ppermute(v, axis, [(i, i ^ s) for i in range(lax.axis_size(axis))])  35.9 us
    pallas_call x25, Pallas kernels, call(): pl.pallas_call(kernel, out_shape=shapes, in_specs=[VMEM] * used + [ANY] *...  24.4 us
    ppermute x26, waiting for transfers between devices, swap(): lax.ppermute(v, axis, [(i, i ^ s) for i in range(lax.axis_size(axis))])  16.6 us
    all_to_all x1, blocking collectives, over_ctr(): return lax.all_to_all(v, ('zl', 'y'), 0, 0)  10.6 us
  transfers between devices with their start and end apart: 26, of which 11 were waited for; matrix products, arithmetic and copies ran while one was open for 0% of the time, Pallas kernels for 19%

profile of v4, /device:TPU:32, one launch (start us, length us, event | category | flops | bytes accessed | tf_op | source)
XLA Modules:
  0.0 89.9 jit_solution(523423520987262678)
XLA Ops:
  2.3 1.5 %kern_own.1 = (f32[512,4096]{1,0:T(8,128)S(1)}, f32[1,512]{1,0:T(1,128)S(1)}, bf16[144,4096]{1,0:T(8,128)(2,1)S(1)}) custom-call(f32[512,128]{1,0:T(8,128)S(1)} %widen.1.refs_0_.refs_3_, bf16[8192,128]{1,0:T(8,128)(2,1)S(1)} %copy-done), custom_call_target="tpu_custom_call" | custom-call | bytes 2359296 | tf_op jit(solution)/shard_map/kern_own/pallas_call | solution.py:328
  3.8 1.4 %kern_other.1 = (f32[512,4096]{1,0:T(8,128)S(1)}, f32[2,512]{1,0:T(2,128)S(1)}) custom-call(f32[512,128]{1,0:T(8,128)S(1)} %collective-permute-done.refs_0_.refs_4_, bf16[144,4096]{1,0:T(8,128)(2,1)S(1)} %get-tuple-element.35.refs_1_, f32[1,512]{1,0:T(1,128)S(1)} %get-tuple-element.36.refs_2_), custom_call_target="tpu_custom_call" | custom-call | bytes 1443840 | tf_op jit(solution)/shard_map/kern_other/pallas_call | solution.py:328
  6.5 10.6 %all_to_all.5.refs_2_ = f32[8,2,512]{2,1,0:T(2,128)S(1)} all-to-all(f32[8,2,512]{2,1,0:T(2,128)S(1)} %sum_core.1), channel_id=1, replica_groups=mesh['x'=4,'h'=4,'core'=2,'zl'=2,'y'=4] {'zl','y'}, dimensions={0} | all-to-all | bytes 65536 | tf_op jit(solution)/shard_map/all_to_all | solution.py:359
  17.1 1.6 %freq.1 = (f32[1,4096]{1,0:T(1,128)S(1)}, f32[2,512]{1,0:T(2,128)S(1)}) custom-call(f32[512,4096]{1,0:T(8,128)S(1)} %get-tuple-element.34.refs_0_, f32[512,4096]{1,0:T(8,128)S(1)} %get-tuple-element.37.refs_1_.refs_0_, f32[8,2,512]{2,1,0:T(2,128)S(1)} %all_to_all.5.refs_2_), custom_call_target="tpu_custom_call" | custom-call | bytes 16809984 | tf_op jit(solution)/shard_map/freq/pallas_call | solution.py:328
  18.6 3.1 %collective-permute-start.4 = (f32[1,4096]{1,0:T(1,128)S(1)}, f32[1,4096]{1,0:T(1,128)S(1)}, u32[]{:S(2)}, u32[]{:S(2)}) collective-permute-start(f32[1,4096]{1,0:T(1,128)S(1)} %get-tuple-element.39.refs_0_), channel_id=1, source_target_pairs={{0,128},{64,192},{128,0},{192,64},{1,129},{65,193},{129,1},{193,65... | collective-permute-start | bytes 49160 | tf_op jit(solution)/shard_map/ppermute | solution.py:342
  22.9 2.6 %squares_own.1.refs_4_.refs_7_ = f32[512,256]{1,0:T(8,128)S(1)} custom-call(f32[512,4096]{1,0:T(8,128)S(1)} %get-tuple-element.34.refs_0_, bf16[8192,128]{1,0:T(8,128)(2,1)S(1)} %copy-done), custom_call_target="tpu_custom_call" | custom-call | flops 2147483648 | bytes 10485760 | tf_op jit(solution)/shard_map/squares_own/pallas_call | solution.py:328
  26.7 6.4 %collective-permute-start.7 = (f32[1,4096]{1,0:T(1,128)S(1)}, f32[1,4096]{1,0:T(1,128)S(1)}, u32[]{:S(2)}, u32[]{:S(2)}) collective-permute-start(f32[1,4096]{1,0:T(1,128)S(1)} %sum_x.1.refs_2_), channel_id=1, source_target_pairs={{0,32},{16,48},{32,0},{48,16},{1,33},{17,49},{33,1},{49,17},{2,34}... | collective-permute-start | bytes 49160 | tf_op jit(solution)/shard_map/ppermute | solution.py:342
  34.6 2.9 %squares_other.1 = (f32[512,256]{1,0:T(8,128)S(1)}, bf16[144,512]{1,0:T(8,128)(2,1)S(1)}, bf16[144,512]{1,0:T(8,128)(2,1)S(1)}, f32[512,128]{1,0:T(8,128)S(1)}, f32[512,128]{1,0:T(8,128)S(1)}) custom-call(f32[512,4096]{1,0:T(8,128)S(1)} %get-tuple-element.37.refs_1_.refs_0_, bf16[8192,128]{1,0:T(8,128)(2,1)S(1)} %copy-done, ...), custom_call_target="tpu_custom_call" | custom-call | flops 2147483648 | bytes 11014144 | tf_op jit(solution)/shard_map/squares_other/pallas_call | solution.py:328
  37.5 1.5 %collective-permute-done.6.refs_4_ = f32[1,4096]{1,0:T(1,128)S(1)} collective-permute-done((f32[1,4096]{1,0:T(1,128)S(1)}, f32[1,4096]{1,0:T(1,128)S(1)}, u32[]{:S(2)}, u32[]{:S(2)}) %collective-permute-start.6) | collective-permute-done | bytes 16416 | tf_op jit(solution)/shard_map/ppermute | solution.py:342
  38.9 1.8 %target.1 = (f32[2,512]{1,0:T(2,128)S(1)}, f32[1,4096]{1,0:T(1,128)S(1)}) custom-call(f32[512,4096]{1,0:T(8,128)S(1)} %get-tuple-element.34.refs_0_, f32[512,4096]{1,0:T(8,128)S(1)} %get-tuple-element.37.refs_1_.refs_0_, f32[1,4096]{1,0:T(1,128)S(1)} %sum_x.1.refs_2_, f32[1,4096]{1,0:T(1,128)S(1)} %collective-permute-done.5.refs_3_, ...), custom_call_target="tpu_custom_call" | custom-call | bytes 17399808 | tf_op jit(solution)/shard_map/target/pallas_call | solution.py:328
  43.4 2.4 %cubes.3.refs_6_ = f32[512,256]{1,0:T(8,128)S(1)} custom-call(f32[512,4096]{1,0:T(8,128)S(1)} %get-tuple-element.37.refs_1_.refs_0_, f32[1,4096]{1,0:T(1,128)S(1)} %get-tuple-element.42.refs_2_.refs_1_, bf16[8192,128]{1,0:T(8,128)(2,1)S(1)} %copy-done), custom_call_target="tpu_custom_call" | custom-call | flops 2147483648 | bytes 10502144 | tf_op jit(solution)/shard_map/cubes/pallas_call | solution.py:328
  47.1 2.1 %collective-permute-start.11 = (f32[2,512]{1,0:T(2,128)S(1)}, f32[2,512]{1,0:T(2,128)S(1)}, u32[]{:S(2)}, u32[]{:S(2)}) collective-permute-start(f32[2,512]{1,0:T(2,128)S(1)} %target_zl.1.refs_8_), channel_id=1, source_target_pairs={{0,3},{1,2},{2,1},{3,0},{4,7},{5,6},{6,5},{7,4},{8,11},{9,10},{10,... | collective-permute-start | bytes 12296 | tf_op jit(solution)/shard_map/ppermute | solution.py:342
  49.4 2.4 %cubes.2.refs_5_ = f32[512,256]{1,0:T(8,128)S(1)} custom-call(f32[512,4096]{1,0:T(8,128)S(1)} %get-tuple-element.34.refs_0_, f32[1,4096]{1,0:T(1,128)S(1)} %get-tuple-element.42.refs_2_.refs_1_, bf16[8192,128]{1,0:T(8,128)(2,1)S(1)} %copy-done), custom_call_target="tpu_custom_call" | custom-call | flops 2147483648 | bytes 10502144 | tf_op jit(solution)/shard_map/cubes/pallas_call | solution.py:328
  52.8 1.7 %grad_far.1 = (f32[64,1024]{1,0:T(8,128)S(1)}, f32[64,1024]{1,0:T(8,128)S(1)}, f32[2,512]{1,0:T(2,128)S(1)}) custom-call(f32[512,4096]{1,0:T(8,128)S(1)} %get-tuple-element.34.refs_0_, f32[512,4096]{1,0:T(8,128)S(1)} %get-tuple-element.37.refs_1_.refs_0_, f32[1,4096]{1,0:T(1,128)S(1)} %get-tuple-element.42.refs_2_.refs_1_, bf16[8192,128]{1,0:T(8,128)(2,1)S(1)} %copy-done, ...), custom_call_target="tpu_custom_call" | custom-call | bytes 19726336 | tf_op jit(solution)/shard_map/grad_far/pallas_call | solution.py:328
  55.4 2.1 %collective-permute-start.14 = (f32[64,1024]{1,0:T(8,128)S(1)}, f32[64,1024]{1,0:T(8,128)S(1)}, u32[]{:S(2)}, u32[]{:S(2)}) collective-permute-start(f32[64,1024]{1,0:T(8,128)S(1)} %get-tuple-element.52), channel_id=1, source_target_pairs={{0,192},{64,128},{128,64},{192,0},{1,193},{65,129},{129,65},{193,1... | collective-permute-start | bytes 786440 | tf_op jit(solution)/shard_map/ppermute | solution.py:342
  57.9 3.1 %grad_mid.1 = (f32[128,1024]{1,0:T(8,128)S(1)}, f32[128,1024]{1,0:T(8,128)S(1)}) custom-call(f32[512,4096]{1,0:T(8,128)S(1)} %get-tuple-element.34.refs_0_, f32[512,4096]{1,0:T(8,128)S(1)} %get-tuple-element.37.refs_1_.refs_0_, f32[1,4096]{1,0:T(1,128)S(1)} %get-tuple-element.42.refs_2_.refs_1_, bf16[8192,128]{1,0:T(8,128)(2,1)S(1)} %copy-done, ...), custom_call_target="tpu_custom_call" | custom-call | bytes 19714048 | tf_op jit(solution)/shard_map/grad_mid/pallas_call | solution.py:328
  61.1 1.9 %collective-permute-done.14.refs_12_.refs_3_ = f32[64,1024]{1,0:T(8,128)S(1)} collective-permute-done((f32[64,1024]{1,0:T(8,128)S(1)}, f32[64,1024]{1,0:T(8,128)S(1)}, u32[]{:S(2)}, u32[]{:S(2)}) %collective-permute-start.14) | collective-permute-done | bytes 262176 | tf_op jit(solution)/shard_map/ppermute | solution.py:342
  64.3 2.2 %collective-permute-start.18 = (f32[128,512]{1,0:T(8,128)S(1)}, f32[128,512]{1,0:T(8,128)S(1)}, u32[]{:S(2)}, u32[]{:S(2)}) collective-permute-start(f32[128,512]{1,0:T(8,128)S(1)} %get-tuple-element.58), channel_id=1, source_target_pairs={{0,192},{64,128},{128,64},{192,0},{1,193},{65,129},{129,65},{193,1... | collective-permute-start | bytes 786440 | tf_op jit(solution)/shard_map/ppermute | solution.py:342
  66.5 1.6 %second_b.1 = (f32[128,512]{1,0:T(8,128)S(1)}, f32[128,512]{1,0:T(8,128)S(1)}, f32[128,1024]{1,0:T(8,128)S(1)}) custom-call(f32[512,4096]{1,0:T(8,128)S(1)} %get-tuple-element.34.refs_0_, f32[512,4096]{1,0:T(8,128)S(1)} %get-tuple-element.37.refs_1_.refs_0_, f32[1,4096]{1,0:T(1,128)S(1)} %get-tuple-element.42.refs_2_.refs_1_, bf16[8192,128]{1,0:T(8,128)(2,1)S(1)} %copy-done, ...), custom_call_target="tpu_custom_call" | custom-call | flops 10000000000 | bytes 21549056 | tf_op jit(solution)/shard_map/second_b/pallas_call | solution.py:328
  68.2 1.7 %collective-permute-start.15 = (f32[128,512]{1,0:T(8,128)S(1)}, f32[128,512]{1,0:T(8,128)S(1)}, u32[]{:S(2)}, u32[]{:S(2)}) collective-permute-start(f32[128,512]{1,0:T(8,128)S(1)} %get-tuple-element.55), channel_id=1, source_target_pairs={{0,64},{64,0},{128,192},{192,128},{1,65},{65,1},{129,193},{193,129... | collective-permute-start | bytes 786440 | tf_op jit(solution)/shard_map/ppermute | solution.py:342
  74.3 1.5 %collective-permute-start.19 = (f32[128,256]{1,0:T(8,128)S(1)}, f32[128,256]{1,0:T(8,128)S(1)}, u32[]{:S(2)}, u32[]{:S(2)}) collective-permute-start(f32[128,256]{1,0:T(8,128)S(1)} %get-tuple-element.61), channel_id=1, source_target_pairs={{0,16},{16,0},{32,48},{48,32},{1,17},{17,1},{33,49},{49,33},{2,18}... | collective-permute-start | bytes 393224 | tf_op jit(solution)/shard_map/ppermute | solution.py:342
  75.8 3.8 %collective-permute-start.20 = (f32[128,256]{1,0:T(8,128)S(1)}, f32[128,256]{1,0:T(8,128)S(1)}, u32[]{:S(2)}, u32[]{:S(2)}) collective-permute-start(f32[128,256]{1,0:T(8,128)S(1)} %get-tuple-element.59.refs_3_), channel_id=1, source_target_pairs={{0,32},{16,48},{32,0},{48,16},{1,33},{17,49},{33,1},{49,17},{2,34}... | collective-permute-start | bytes 393224 | tf_op jit(solution)/shard_map/ppermute | solution.py:342
  82.4 4.6 %collective-permute-done.20.refs_2_ = f32[128,256]{1,0:T(8,128)S(1)} collective-permute-done((f32[128,256]{1,0:T(8,128)S(1)}, f32[128,256]{1,0:T(8,128)S(1)}, u32[]{:S(2)}, u32[]{:S(2)}) %collective-permute-start.20) | collective-permute-done | bytes 131104 | tf_op jit(solution)/shard_map/ppermute | solution.py:342
  87.0 2.2 %collective-permute-done.21.refs_1_ = f32[128,256]{1,0:T(8,128)S(1)} collective-permute-done((f32[128,256]{1,0:T(8,128)S(1)}, f32[128,256]{1,0:T(8,128)S(1)}, u32[]{:S(2)}, u32[]{:S(2)}) %collective-permute-start.21) | collective-permute-done | bytes 131104 | tf_op jit(solution)/shard_map/ppermute | solution.py:342
  (60 shorter events, 22.5 us)
Async XLA Ops:
  1.7 2.1 %collective-permute-start = (f32[512,128]{1,0:T(8,128)S(1)}, f32[512,128]{1,0:T(8,128)S(1)}, u32[]{:S(2)}, u32[]{:S(2)}) collective-permute-start(f32[512,128]{1,0:T(8,128)S(1)} %widen.1.refs_0_.refs_3_), channel_id=1, source_target_pairs={{0,8},{8,0},{1,9},{9,1},{2,10},{10,2},{3,11},{11,3},{4,12},{12,4},... | collective-permute-start | bytes 786440 | tf_op jit(solution)/shard_map/ppermute | solution.py:342
  18.6 6.9 %collective-permute-start.4 = (f32[1,4096]{1,0:T(1,128)S(1)}, f32[1,4096]{1,0:T(1,128)S(1)}, u32[]{:S(2)}, u32[]{:S(2)}) collective-permute-start(f32[1,4096]{1,0:T(1,128)S(1)} %get-tuple-element.39.refs_0_), channel_id=1, source_target_pairs={{0,128},{64,192},{128,0},{192,64},{1,129},{65,193},{129,1},{193,65... | collective-permute-start | bytes 49160 | tf_op jit(solution)/shard_map/ppermute | solution.py:342
  21.7 4.9 %collective-permute-start.3 = (f32[1,4096]{1,0:T(1,128)S(1)}, f32[1,4096]{1,0:T(1,128)S(1)}, u32[]{:S(2)}, u32[]{:S(2)}) collective-permute-start(f32[1,4096]{1,0:T(1,128)S(1)} %get-tuple-element.39.refs_0_), channel_id=1, source_target_pairs={{0,192},{64,128},{128,64},{192,0},{1,193},{65,129},{129,65},{193,1... | collective-permute-start | bytes 49160 | tf_op jit(solution)/shard_map/ppermute | solution.py:342
  22.9 3.8 %collective-permute-start.2 = (f32[1,4096]{1,0:T(1,128)S(1)}, f32[1,4096]{1,0:T(1,128)S(1)}, u32[]{:S(2)}, u32[]{:S(2)}) collective-permute-start(f32[1,4096]{1,0:T(1,128)S(1)} %get-tuple-element.39.refs_0_), channel_id=1, source_target_pairs={{0,64},{64,0},{128,192},{192,128},{1,65},{65,1},{129,193},{193,129... | collective-permute-start | bytes 49160 | tf_op jit(solution)/shard_map/ppermute | solution.py:342
  26.7 10.8 %collective-permute-start.7 = (f32[1,4096]{1,0:T(1,128)S(1)}, f32[1,4096]{1,0:T(1,128)S(1)}, u32[]{:S(2)}, u32[]{:S(2)}) collective-permute-start(f32[1,4096]{1,0:T(1,128)S(1)} %sum_x.1.refs_2_), channel_id=1, source_target_pairs={{0,32},{16,48},{32,0},{48,16},{1,33},{17,49},{33,1},{49,17},{2,34}... | collective-permute-start | bytes 49160 | tf_op jit(solution)/shard_map/ppermute | solution.py:342
  33.1 5.8 %collective-permute-start.6 = (f32[1,4096]{1,0:T(1,128)S(1)}, f32[1,4096]{1,0:T(1,128)S(1)}, u32[]{:S(2)}, u32[]{:S(2)}) collective-permute-start(f32[1,4096]{1,0:T(1,128)S(1)} %sum_x.1.refs_2_), channel_id=1, source_target_pairs={{0,48},{16,32},{32,16},{48,0},{1,49},{17,33},{33,17},{49,1},{2,50}... | collective-permute-start | bytes 49160 | tf_op jit(solution)/shard_map/ppermute | solution.py:342
  33.6 5.3 %collective-permute-start.5 = (f32[1,4096]{1,0:T(1,128)S(1)}, f32[1,4096]{1,0:T(1,128)S(1)}, u32[]{:S(2)}, u32[]{:S(2)}) collective-permute-start(f32[1,4096]{1,0:T(1,128)S(1)} %sum_x.1.refs_2_), channel_id=1, source_target_pairs={{0,16},{16,0},{32,48},{48,32},{1,17},{17,1},{33,49},{49,33},{2,18}... | collective-permute-start | bytes 49160 | tf_op jit(solution)/shard_map/ppermute | solution.py:342
  42.0 3.9 %collective-permute-start.9 = (f32[2,512]{1,0:T(2,128)S(1)}, f32[2,512]{1,0:T(2,128)S(1)}, u32[]{:S(2)}, u32[]{:S(2)}) collective-permute-start(f32[2,512]{1,0:T(2,128)S(1)} %target_core.1.refs_0_), channel_id=1, source_target_pairs={{0,4},{4,0},{1,5},{5,1},{2,6},{6,2},{3,7},{7,3},{8,12},{12,8},{9,1... | collective-permute-start | bytes 12296 | tf_op jit(solution)/shard_map/ppermute | solution.py:342
  45.9 6.0 %collective-permute-start.12 = (f32[2,512]{1,0:T(2,128)S(1)}, f32[2,512]{1,0:T(2,128)S(1)}, u32[]{:S(2)}, u32[]{:S(2)}) collective-permute-start(f32[2,512]{1,0:T(2,128)S(1)} %target_zl.1.refs_8_), channel_id=1, source_target_pairs={{0,2},{1,3},{2,0},{3,1},{4,6},{5,7},{6,4},{7,5},{8,10},{9,11},{10,... | collective-permute-start | bytes 12296 | tf_op jit(solution)/shard_map/ppermute | solution.py:342
  47.1 4.8 %collective-permute-start.11 = (f32[2,512]{1,0:T(2,128)S(1)}, f32[2,512]{1,0:T(2,128)S(1)}, u32[]{:S(2)}, u32[]{:S(2)}) collective-permute-start(f32[2,512]{1,0:T(2,128)S(1)} %target_zl.1.refs_8_), channel_id=1, source_target_pairs={{0,3},{1,2},{2,1},{3,0},{4,7},{5,6},{6,5},{7,4},{8,11},{9,10},{10,... | collective-permute-start | bytes 12296 | tf_op jit(solution)/shard_map/ppermute | solution.py:342
  49.2 3.6 %collective-permute-start.10 = (f32[2,512]{1,0:T(2,128)S(1)}, f32[2,512]{1,0:T(2,128)S(1)}, u32[]{:S(2)}, u32[]{:S(2)}) collective-permute-start(f32[2,512]{1,0:T(2,128)S(1)} %target_zl.1.refs_8_), channel_id=1, source_target_pairs={{0,1},{1,0},{2,3},{3,2},{4,5},{5,4},{6,7},{7,6},{8,9},{9,8},{10,11... | collective-permute-start | bytes 12296 | tf_op jit(solution)/shard_map/ppermute | solution.py:342
  54.5 6.7 %collective-permute-start.13 = (f32[64,1024]{1,0:T(8,128)S(1)}, f32[64,1024]{1,0:T(8,128)S(1)}, u32[]{:S(2)}, u32[]{:S(2)}) collective-permute-start(f32[64,1024]{1,0:T(8,128)S(1)} %get-tuple-element.51), channel_id=1, source_target_pairs={{0,64},{64,0},{128,192},{192,128},{1,65},{65,1},{129,193},{193,129... | collective-permute-start | bytes 786440 | tf_op jit(solution)/shard_map/ppermute | solution.py:342
  55.4 7.6 %collective-permute-start.14 = (f32[64,1024]{1,0:T(8,128)S(1)}, f32[64,1024]{1,0:T(8,128)S(1)}, u32[]{:S(2)}, u32[]{:S(2)}) collective-permute-start(f32[64,1024]{1,0:T(8,128)S(1)} %get-tuple-element.52), channel_id=1, source_target_pairs={{0,192},{64,128},{128,64},{192,0},{1,193},{65,129},{129,65},{193,1... | collective-permute-start | bytes 786440 | tf_op jit(solution)/shard_map/ppermute | solution.py:342
  57.8 5.2 %collective-permute-start.22 = (f32[512,128]{1,0:T(8,128)S(1)}, f32[512,128]{1,0:T(8,128)S(1)}, u32[]{:S(2)}, u32[]{:S(2)}) collective-permute-start(f32[512,128]{1,0:T(8,128)S(1)} %get-tuple-element.63), channel_id=1, source_target_pairs={{0,8},{8,0},{1,9},{9,1},{2,10},{10,2},{3,11},{11,3},{4,12},{12,4},... | collective-permute-start | bytes 786440 | tf_op jit(solution)/shard_map/ppermute | solution.py:342
  63.0 8.0 %collective-permute-start.23 = (f32[512,128]{1,0:T(8,128)S(1)}, f32[512,128]{1,0:T(8,128)S(1)}, u32[]{:S(2)}, u32[]{:S(2)}) collective-permute-start(f32[512,128]{1,0:T(8,128)S(1)} %embed_core.1.refs_0_), channel_id=1, source_target_pairs={{0,4},{4,0},{1,5},{5,1},{2,6},{6,2},{3,7},{7,3},{8,12},{12,8},{9,1... | collective-permute-start | bytes 786440 | tf_op jit(solution)/shard_map/ppermute | solution.py:342
  64.2 9.0 %collective-permute-start.17 = (f32[128,512]{1,0:T(8,128)S(1)}, f32[128,512]{1,0:T(8,128)S(1)}, u32[]{:S(2)}, u32[]{:S(2)}) collective-permute-start(f32[128,512]{1,0:T(8,128)S(1)} %get-tuple-element.57), channel_id=1, source_target_pairs={{0,64},{64,0},{128,192},{192,128},{1,65},{65,1},{129,193},{193,129... | collective-permute-start | bytes 786440 | tf_op jit(solution)/shard_map/ppermute | solution.py:342
  64.3 9.9 %collective-permute-start.18 = (f32[128,512]{1,0:T(8,128)S(1)}, f32[128,512]{1,0:T(8,128)S(1)}, u32[]{:S(2)}, u32[]{:S(2)}) collective-permute-start(f32[128,512]{1,0:T(8,128)S(1)} %get-tuple-element.58), channel_id=1, source_target_pairs={{0,192},{64,128},{128,64},{192,0},{1,193},{65,129},{129,65},{193,1... | collective-permute-start | bytes 786440 | tf_op jit(solution)/shard_map/ppermute | solution.py:342
  68.2 11.5 %collective-permute-start.15 = (f32[128,512]{1,0:T(8,128)S(1)}, f32[128,512]{1,0:T(8,128)S(1)}, u32[]{:S(2)}, u32[]{:S(2)}) collective-permute-start(f32[128,512]{1,0:T(8,128)S(1)} %get-tuple-element.55), channel_id=1, source_target_pairs={{0,64},{64,0},{128,192},{192,128},{1,65},{65,1},{129,193},{193,129... | collective-permute-start | bytes 786440 | tf_op jit(solution)/shard_map/ppermute | solution.py:342
  69.9 9.8 %collective-permute-start.16 = (f32[128,512]{1,0:T(8,128)S(1)}, f32[128,512]{1,0:T(8,128)S(1)}, u32[]{:S(2)}, u32[]{:S(2)}) collective-permute-start(f32[128,512]{1,0:T(8,128)S(1)} %get-tuple-element.56), channel_id=1, source_target_pairs={{0,192},{64,128},{128,64},{192,0},{1,193},{65,129},{129,65},{193,1... | collective-permute-start | bytes 786440 | tf_op jit(solution)/shard_map/ppermute | solution.py:342
  71.0 10.0 %collective-permute-start.24 = (f32[512,128]{1,0:T(8,128)S(1)}, f32[512,128]{1,0:T(8,128)S(1)}, u32[]{:S(2)}, u32[]{:S(2)}) collective-permute-start(f32[512,128]{1,0:T(8,128)S(1)} %embed_zl.1.refs_0_), channel_id=1, source_target_pairs={{0,1},{1,0},{2,3},{3,2},{4,5},{5,4},{6,7},{7,6},{8,9},{9,8},{10,11... | collective-permute-start | bytes 786440 | tf_op jit(solution)/shard_map/ppermute | solution.py:342
  74.3 8.1 %collective-permute-start.19 = (f32[128,256]{1,0:T(8,128)S(1)}, f32[128,256]{1,0:T(8,128)S(1)}, u32[]{:S(2)}, u32[]{:S(2)}) collective-permute-start(f32[128,256]{1,0:T(8,128)S(1)} %get-tuple-element.61), channel_id=1, source_target_pairs={{0,16},{16,0},{32,48},{48,32},{1,17},{17,1},{33,49},{49,33},{2,18}... | collective-permute-start | bytes 393224 | tf_op jit(solution)/shard_map/ppermute | solution.py:342
  75.8 11.1 %collective-permute-start.20 = (f32[128,256]{1,0:T(8,128)S(1)}, f32[128,256]{1,0:T(8,128)S(1)}, u32[]{:S(2)}, u32[]{:S(2)}) collective-permute-start(f32[128,256]{1,0:T(8,128)S(1)} %get-tuple-element.59.refs_3_), channel_id=1, source_target_pairs={{0,32},{16,48},{32,0},{48,16},{1,33},{17,49},{33,1},{49,17},{2,34}... | collective-permute-start | bytes 393224 | tf_op jit(solution)/shard_map/ppermute | solution.py:342
  79.7 9.4 %collective-permute-start.21 = (f32[128,256]{1,0:T(8,128)S(1)}, f32[128,256]{1,0:T(8,128)S(1)}, u32[]{:S(2)}, u32[]{:S(2)}) collective-permute-start(f32[128,256]{1,0:T(8,128)S(1)} %get-tuple-element.62), channel_id=1, source_target_pairs={{0,48},{16,32},{32,16},{48,0},{1,49},{17,33},{33,17},{49,1},{2,50}... | collective-permute-start | bytes 393224 | tf_op jit(solution)/shard_map/ppermute | solution.py:342
  81.1 8.1 %collective-permute-start.25 = (f32[512,128]{1,0:T(8,128)S(1)}, f32[512,128]{1,0:T(8,128)S(1)}, u32[]{:S(2)}, u32[]{:S(2)}) collective-permute-start(f32[512,128]{1,0:T(8,128)S(1)} %embed_y.1.refs_2_), channel_id=1, source_target_pairs={{0,3},{1,2},{2,1},{3,0},{4,7},{5,6},{6,5},{7,4},{8,11},{9,10},{10,... | collective-permute-start | bytes 786440 | tf_op jit(solution)/shard_map/ppermute | solution.py:342
  (5 other events, 18.7 us)

commit v5 on v4

--- a/solution.py
+++ b/solution.py
@@ -213,8 +213,8 @@
         out[...] = total
 
 
-def square_body(kern_ref, c_ref, out):
-    embed_sums(kern_ref, c_ref, out, lambda kern, at: kern * kern, 2 * SIDE)
+def square_body(step, kern_ref, c_ref, out):
+    embed_sums(kern_ref, c_ref, out, lambda kern, at: kern * kern, step)
 
 
 def square_setup_body(kern_ref, c_ref, rinv_ref, z, zo, out, zt0, zt1, rs0, rs1):
@@ -222,7 +222,7 @@
         zt[:LANES] = (-SCALE * points[...].T).astype(BF16)
         zt[LANES:] = jnp.full((ONES, points.shape[0]), SCALE, BF16)
         rs[...] = spread(rinv_ref[p : p + 1])
-    square_body(kern_ref, c_ref, out)
+    square_body(2 * SIDE, kern_ref, c_ref, out)
 
 
 def cube_body(kern_ref, finv_ref, c_ref, out):
@@ -395,7 +395,13 @@
     work = 4 * half * count * 2 * LANES
     zt_shape = jax.ShapeDtypeStruct((width + ONES, half), BF16)
     squares = call(
-        square_body, [sums], kern_own, centres, limit=20, name="squares_own", flops=work
+        functools.partial(square_body, SIDE * SIDE),
+        [sums],
+        kern_own,
+        centres,
+        limit=20,
+        name="squares_own",
+        flops=work,
     )
     more, *data = call(
         square_setup_body,
@@ -494,14 +500,14 @@
         )
 
     far2, far1 = split(0, (first_a, third_a), "split_a")
-    h2, h1 = swap(far2, "h", 2), swap(far1, "h", 1)
+    h2, h1 = swap(far2, "h", HOPS[0]), swap(far1, "h", HOPS[1])
     h3, h0 = split(2 * inner, (first_b, third_b), "split_b", after=[far2])
     most = call(three_body, [block], h0, h1, h2, name="most", flops=HINT)
     grad, embed = call(
         final_body,
         [(inner, width), (half, width)],
         most,
-        swap(h3, "h", 3),
+        swap(h3, "h", HOPS[2]),
         *embed,
         name="final",
         flops=HINT,

time: 90.4 us -> 90.1 us (level)
  no operation moved by 1% of the time
where the time goes in v5:
time: 90.1 us; the launch traced here: 89.9 us
  starting transfers between devices  35.7 us (40%)
  Pallas kernels  24.2 us (27%)
  waiting for transfers between devices  17.1 us (19%)
  blocking collectives  10.6 us (12%)
  local copies, waits for them, and re-layouts  1.52 us (2%)
    ppermute x26, starting transfers between devices, swap(): lax.ppermute(v, axis, [(i, i ^ s) for i in range(lax.axis_size(axis))])  35.7 us
    pallas_call x25, Pallas kernels, call(): pl.pallas_call(kernel, out_shape=shapes, in_specs=[VMEM] * used + [ANY] *...  24.2 us
    ppermute x26, waiting for transfers between devices, swap(): lax.ppermute(v, axis, [(i, i ^ s) for i in range(lax.axis_size(axis))])  17.1 us
    all_to_all x1, blocking collectives, over_ctr(): return lax.all_to_all(v, ('zl', 'y'), 0, 0)  10.6 us
  transfers between devices with their start and end apart: 26, of which 11 were waited for; matrix products, arithmetic and copies ran while one was open for 0% of the time, Pallas kernels for 19%

profile of v5, /device:TPU:32, one launch (start us, length us, event | category | flops | bytes accessed | tf_op | source)
XLA Modules:
  0.0 89.9 jit_solution(6583830123080186505)
XLA Ops:
  2.3 1.5 %kern_own.1 = (f32[512,4096]{1,0:T(8,128)S(1)}, f32[1,512]{1,0:T(1,128)S(1)}, bf16[144,4096]{1,0:T(8,128)(2,1)S(1)}) custom-call(f32[512,128]{1,0:T(8,128)S(1)} %widen.1.refs_0_.refs_3_, bf16[8192,128]{1,0:T(8,128)(2,1)S(1)} %copy-done), custom_call_target="tpu_custom_call" | custom-call | bytes 2359296 | tf_op jit(solution)/shard_map/kern_own/pallas_call | solution.py:328
  6.5 10.6 %all_to_all.5.refs_2_ = f32[8,2,512]{2,1,0:T(2,128)S(1)} all-to-all(f32[8,2,512]{2,1,0:T(2,128)S(1)} %sum_core.1), channel_id=1, replica_groups=mesh['x'=4,'h'=4,'core'=2,'zl'=2,'y'=4] {'zl','y'}, dimensions={0} | all-to-all | bytes 65536 | tf_op jit(solution)/shard_map/all_to_all | solution.py:359
  17.1 1.6 %freq.1 = (f32[1,4096]{1,0:T(1,128)S(1)}, f32[2,512]{1,0:T(2,128)S(1)}) custom-call(f32[512,4096]{1,0:T(8,128)S(1)} %get-tuple-element.34.refs_0_, f32[512,4096]{1,0:T(8,128)S(1)} %get-tuple-element.37.refs_1_.refs_0_, f32[8,2,512]{2,1,0:T(2,128)S(1)} %all_to_all.5.refs_2_), custom_call_target="tpu_custom_call" | custom-call | bytes 16809984 | tf_op jit(solution)/shard_map/freq/pallas_call | solution.py:328
  18.6 3.1 %collective-permute-start.4 = (f32[1,4096]{1,0:T(1,128)S(1)}, f32[1,4096]{1,0:T(1,128)S(1)}, u32[]{:S(2)}, u32[]{:S(2)}) collective-permute-start(f32[1,4096]{1,0:T(1,128)S(1)} %get-tuple-element.39.refs_0_), channel_id=1, source_target_pairs={{0,128},{64,192},{128,0},{192,64},{1,129},{65,193},{129,1},{193,65... | collective-permute-start | bytes 49160 | tf_op jit(solution)/shard_map/ppermute | solution.py:342
  22.9 2.4 %squares_own.1.refs_4_.refs_7_ = f32[512,256]{1,0:T(8,128)S(1)} custom-call(f32[512,4096]{1,0:T(8,128)S(1)} %get-tuple-element.34.refs_0_, bf16[8192,128]{1,0:T(8,128)(2,1)S(1)} %copy-done), custom_call_target="tpu_custom_call" | custom-call | flops 2147483648 | bytes 10485760 | tf_op jit(solution)/shard_map/squares_own/pallas_call | solution.py:328
  26.7 6.4 %collective-permute-start.7 = (f32[1,4096]{1,0:T(1,128)S(1)}, f32[1,4096]{1,0:T(1,128)S(1)}, u32[]{:S(2)}, u32[]{:S(2)}) collective-permute-start(f32[1,4096]{1,0:T(1,128)S(1)} %sum_x.1.refs_2_), channel_id=1, source_target_pairs={{0,32},{16,48},{32,0},{48,16},{1,33},{17,49},{33,1},{49,17},{2,34}... | collective-permute-start | bytes 49160 | tf_op jit(solution)/shard_map/ppermute | solution.py:342
  34.6 2.9 %squares_other.1 = (f32[512,256]{1,0:T(8,128)S(1)}, bf16[144,512]{1,0:T(8,128)(2,1)S(1)}, bf16[144,512]{1,0:T(8,128)(2,1)S(1)}, f32[512,128]{1,0:T(8,128)S(1)}, f32[512,128]{1,0:T(8,128)S(1)}) custom-call(f32[512,4096]{1,0:T(8,128)S(1)} %get-tuple-element.37.refs_1_.refs_0_, bf16[8192,128]{1,0:T(8,128)(2,1)S(1)} %copy-done, ...), custom_call_target="tpu_custom_call" | custom-call | flops 2147483648 | bytes 11014144 | tf_op jit(solution)/shard_map/squares_other/pallas_call | solution.py:328
  37.5 1.5 %collective-permute-done.6.refs_4_ = f32[1,4096]{1,0:T(1,128)S(1)} collective-permute-done((f32[1,4096]{1,0:T(1,128)S(1)}, f32[1,4096]{1,0:T(1,128)S(1)}, u32[]{:S(2)}, u32[]{:S(2)}) %collective-permute-start.6) | collective-permute-done | bytes 16416 | tf_op jit(solution)/shard_map/ppermute | solution.py:342
  38.9 1.8 %target.1 = (f32[2,512]{1,0:T(2,128)S(1)}, f32[1,4096]{1,0:T(1,128)S(1)}) custom-call(f32[512,4096]{1,0:T(8,128)S(1)} %get-tuple-element.34.refs_0_, f32[512,4096]{1,0:T(8,128)S(1)} %get-tuple-element.37.refs_1_.refs_0_, f32[1,4096]{1,0:T(1,128)S(1)} %sum_x.1.refs_2_, f32[1,4096]{1,0:T(1,128)S(1)} %collective-permute-done.5.refs_3_, ...), custom_call_target="tpu_custom_call" | custom-call | bytes 17399808 | tf_op jit(solution)/shard_map/target/pallas_call | solution.py:328
  43.4 2.4 %cubes.3.refs_6_ = f32[512,256]{1,0:T(8,128)S(1)} custom-call(f32[512,4096]{1,0:T(8,128)S(1)} %get-tuple-element.37.refs_1_.refs_0_, f32[1,4096]{1,0:T(1,128)S(1)} %get-tuple-element.42.refs_2_.refs_1_, bf16[8192,128]{1,0:T(8,128)(2,1)S(1)} %copy-done), custom_call_target="tpu_custom_call" | custom-call | flops 2147483648 | bytes 10502144 | tf_op jit(solution)/shard_map/cubes/pallas_call | solution.py:328
  47.1 2.1 %collective-permute-start.11 = (f32[2,512]{1,0:T(2,128)S(1)}, f32[2,512]{1,0:T(2,128)S(1)}, u32[]{:S(2)}, u32[]{:S(2)}) collective-permute-start(f32[2,512]{1,0:T(2,128)S(1)} %target_zl.1.refs_8_), channel_id=1, source_target_pairs={{0,3},{1,2},{2,1},{3,0},{4,7},{5,6},{6,5},{7,4},{8,11},{9,10},{10,... | collective-permute-start | bytes 12296 | tf_op jit(solution)/shard_map/ppermute | solution.py:342
  49.4 2.4 %cubes.2.refs_5_ = f32[512,256]{1,0:T(8,128)S(1)} custom-call(f32[512,4096]{1,0:T(8,128)S(1)} %get-tuple-element.34.refs_0_, f32[1,4096]{1,0:T(1,128)S(1)} %get-tuple-element.42.refs_2_.refs_1_, bf16[8192,128]{1,0:T(8,128)(2,1)S(1)} %copy-done), custom_call_target="tpu_custom_call" | custom-call | flops 2147483648 | bytes 10502144 | tf_op jit(solution)/shard_map/cubes/pallas_call | solution.py:328
  52.8 1.7 %grad_far.1 = (f32[64,1024]{1,0:T(8,128)S(1)}, f32[64,1024]{1,0:T(8,128)S(1)}, f32[2,512]{1,0:T(2,128)S(1)}) custom-call(f32[512,4096]{1,0:T(8,128)S(1)} %get-tuple-element.34.refs_0_, f32[512,4096]{1,0:T(8,128)S(1)} %get-tuple-element.37.refs_1_.refs_0_, f32[1,4096]{1,0:T(1,128)S(1)} %get-tuple-element.42.refs_2_.refs_1_, bf16[8192,128]{1,0:T(8,128)(2,1)S(1)} %copy-done, ...), custom_call_target="tpu_custom_call" | custom-call | bytes 19726336 | tf_op jit(solution)/shard_map/grad_far/pallas_call | solution.py:328
  55.2 2.1 %collective-permute-start.14 = (f32[64,1024]{1,0:T(8,128)S(1)}, f32[64,1024]{1,0:T(8,128)S(1)}, u32[]{:S(2)}, u32[]{:S(2)}) collective-permute-start(f32[64,1024]{1,0:T(8,128)S(1)} %get-tuple-element.52), channel_id=1, source_target_pairs={{0,192},{64,128},{128,64},{192,0},{1,193},{65,129},{129,65},{193,1... | collective-permute-start | bytes 786440 | tf_op jit(solution)/shard_map/ppermute | solution.py:342
  57.6 3.1 %grad_mid.1 = (f32[128,1024]{1,0:T(8,128)S(1)}, f32[128,1024]{1,0:T(8,128)S(1)}) custom-call(f32[512,4096]{1,0:T(8,128)S(1)} %get-tuple-element.34.refs_0_, f32[512,4096]{1,0:T(8,128)S(1)} %get-tuple-element.37.refs_1_.refs_0_, f32[1,4096]{1,0:T(1,128)S(1)} %get-tuple-element.42.refs_2_.refs_1_, bf16[8192,128]{1,0:T(8,128)(2,1)S(1)} %copy-done, ...), custom_call_target="tpu_custom_call" | custom-call | bytes 19714048 | tf_op jit(solution)/shard_map/grad_mid/pallas_call | solution.py:328
  61.1 1.6 %collective-permute-done.14.refs_12_.refs_3_ = f32[64,1024]{1,0:T(8,128)S(1)} collective-permute-done((f32[64,1024]{1,0:T(8,128)S(1)}, f32[64,1024]{1,0:T(8,128)S(1)}, u32[]{:S(2)}, u32[]{:S(2)}) %collective-permute-start.14) | collective-permute-done | bytes 262176 | tf_op jit(solution)/shard_map/ppermute | solution.py:342
  64.3 2.0 %collective-permute-start.18 = (f32[128,512]{1,0:T(8,128)S(1)}, f32[128,512]{1,0:T(8,128)S(1)}, u32[]{:S(2)}, u32[]{:S(2)}) collective-permute-start(f32[128,512]{1,0:T(8,128)S(1)} %get-tuple-element.58), channel_id=1, source_target_pairs={{0,192},{64,128},{128,64},{192,0},{1,193},{65,129},{129,65},{193,1... | collective-permute-start | bytes 786440 | tf_op jit(solution)/shard_map/ppermute | solution.py:342
  66.3 1.7 %second_b.1 = (f32[128,512]{1,0:T(8,128)S(1)}, f32[128,512]{1,0:T(8,128)S(1)}, f32[128,1024]{1,0:T(8,128)S(1)}) custom-call(f32[512,4096]{1,0:T(8,128)S(1)} %get-tuple-element.34.refs_0_, f32[512,4096]{1,0:T(8,128)S(1)} %get-tuple-element.37.refs_1_.refs_0_, f32[1,4096]{1,0:T(1,128)S(1)} %get-tuple-element.42.refs_2_.refs_1_, bf16[8192,128]{1,0:T(8,128)(2,1)S(1)} %copy-done, ...), custom_call_target="tpu_custom_call" | custom-call | flops 10000000000 | bytes 21549056 | tf_op jit(solution)/shard_map/second_b/pallas_call | solution.py:328
  68.0 1.7 %collective-permute-start.15 = (f32[128,512]{1,0:T(8,128)S(1)}, f32[128,512]{1,0:T(8,128)S(1)}, u32[]{:S(2)}, u32[]{:S(2)}) collective-permute-start(f32[128,512]{1,0:T(8,128)S(1)} %get-tuple-element.55), channel_id=1, source_target_pairs={{0,64},{64,0},{128,192},{192,128},{1,65},{65,1},{129,193},{193,129... | collective-permute-start | bytes 786440 | tf_op jit(solution)/shard_map/ppermute | solution.py:342
  72.8 1.6 %collective-permute-done.18.refs_2_ = f32[128,512]{1,0:T(8,128)S(1)} collective-permute-done((f32[128,512]{1,0:T(8,128)S(1)}, f32[128,512]{1,0:T(8,128)S(1)}, u32[]{:S(2)}, u32[]{:S(2)}) %collective-permute-start.18) | collective-permute-done | bytes 262176 | tf_op jit(solution)/shard_map/ppermute | solution.py:342
  74.5 1.5 %collective-permute-start.19 = (f32[128,256]{1,0:T(8,128)S(1)}, f32[128,256]{1,0:T(8,128)S(1)}, u32[]{:S(2)}, u32[]{:S(2)}) collective-permute-start(f32[128,256]{1,0:T(8,128)S(1)} %get-tuple-element.61), channel_id=1, source_target_pairs={{0,16},{16,0},{32,48},{48,32},{1,17},{17,1},{33,49},{49,33},{2,18}... | collective-permute-start | bytes 393224 | tf_op jit(solution)/shard_map/ppermute | solution.py:342
  76.1 3.8 %collective-permute-start.20 = (f32[128,256]{1,0:T(8,128)S(1)}, f32[128,256]{1,0:T(8,128)S(1)}, u32[]{:S(2)}, u32[]{:S(2)}) collective-permute-start(f32[128,256]{1,0:T(8,128)S(1)} %get-tuple-element.59.refs_3_), channel_id=1, source_target_pairs={{0,32},{16,48},{32,0},{48,16},{1,33},{17,49},{33,1},{49,17},{2,34}... | collective-permute-start | bytes 393224 | tf_op jit(solution)/shard_map/ppermute | solution.py:342
  82.6 4.5 %collective-permute-done.20.refs_2_ = f32[128,256]{1,0:T(8,128)S(1)} collective-permute-done((f32[128,256]{1,0:T(8,128)S(1)}, f32[128,256]{1,0:T(8,128)S(1)}, u32[]{:S(2)}, u32[]{:S(2)}) %collective-permute-start.20) | collective-permute-done | bytes 131104 | tf_op jit(solution)/shard_map/ppermute | solution.py:342
  87.2 2.0 %collective-permute-done.21.refs_1_ = f32[128,256]{1,0:T(8,128)S(1)} collective-permute-done((f32[128,256]{1,0:T(8,128)S(1)}, f32[128,256]{1,0:T(8,128)S(1)}, u32[]{:S(2)}, u32[]{:S(2)}) %collective-permute-start.21) | collective-permute-done | bytes 131104 | tf_op jit(solution)/shard_map/ppermute | solution.py:342
  (60 shorter events, 23.1 us)
Async XLA Ops:
  1.7 2.1 %collective-permute-start = (f32[512,128]{1,0:T(8,128)S(1)}, f32[512,128]{1,0:T(8,128)S(1)}, u32[]{:S(2)}, u32[]{:S(2)}) collective-permute-start(f32[512,128]{1,0:T(8,128)S(1)} %widen.1.refs_0_.refs_3_), channel_id=1, source_target_pairs={{0,8},{8,0},{1,9},{9,1},{2,10},{10,2},{3,11},{11,3},{4,12},{12,4},... | collective-permute-start | bytes 786440 | tf_op jit(solution)/shard_map/ppermute | solution.py:342
  18.6 6.7 %collective-permute-start.4 = (f32[1,4096]{1,0:T(1,128)S(1)}, f32[1,4096]{1,0:T(1,128)S(1)}, u32[]{:S(2)}, u32[]{:S(2)}) collective-permute-start(f32[1,4096]{1,0:T(1,128)S(1)} %get-tuple-element.39.refs_0_), channel_id=1, source_target_pairs={{0,128},{64,192},{128,0},{192,64},{1,129},{65,193},{129,1},{193,65... | collective-permute-start | bytes 49160 | tf_op jit(solution)/shard_map/ppermute | solution.py:342
  21.7 4.9 %collective-permute-start.3 = (f32[1,4096]{1,0:T(1,128)S(1)}, f32[1,4096]{1,0:T(1,128)S(1)}, u32[]{:S(2)}, u32[]{:S(2)}) collective-permute-start(f32[1,4096]{1,0:T(1,128)S(1)} %get-tuple-element.39.refs_0_), channel_id=1, source_target_pairs={{0,192},{64,128},{128,64},{192,0},{1,193},{65,129},{129,65},{193,1... | collective-permute-start | bytes 49160 | tf_op jit(solution)/shard_map/ppermute | solution.py:342
  22.9 3.8 %collective-permute-start.2 = (f32[1,4096]{1,0:T(1,128)S(1)}, f32[1,4096]{1,0:T(1,128)S(1)}, u32[]{:S(2)}, u32[]{:S(2)}) collective-permute-start(f32[1,4096]{1,0:T(1,128)S(1)} %get-tuple-element.39.refs_0_), channel_id=1, source_target_pairs={{0,64},{64,0},{128,192},{192,128},{1,65},{65,1},{129,193},{193,129... | collective-permute-start | bytes 49160 | tf_op jit(solution)/shard_map/ppermute | solution.py:342
  26.7 10.8 %collective-permute-start.7 = (f32[1,4096]{1,0:T(1,128)S(1)}, f32[1,4096]{1,0:T(1,128)S(1)}, u32[]{:S(2)}, u32[]{:S(2)}) collective-permute-start(f32[1,4096]{1,0:T(1,128)S(1)} %sum_x.1.refs_2_), channel_id=1, source_target_pairs={{0,32},{16,48},{32,0},{48,16},{1,33},{17,49},{33,1},{49,17},{2,34}... | collective-permute-start | bytes 49160 | tf_op jit(solution)/shard_map/ppermute | solution.py:342
  33.1 5.8 %collective-permute-start.6 = (f32[1,4096]{1,0:T(1,128)S(1)}, f32[1,4096]{1,0:T(1,128)S(1)}, u32[]{:S(2)}, u32[]{:S(2)}) collective-permute-start(f32[1,4096]{1,0:T(1,128)S(1)} %sum_x.1.refs_2_), channel_id=1, source_target_pairs={{0,48},{16,32},{32,16},{48,0},{1,49},{17,33},{33,17},{49,1},{2,50}... | collective-permute-start | bytes 49160 | tf_op jit(solution)/shard_map/ppermute | solution.py:342
  33.6 5.3 %collective-permute-start.5 = (f32[1,4096]{1,0:T(1,128)S(1)}, f32[1,4096]{1,0:T(1,128)S(1)}, u32[]{:S(2)}, u32[]{:S(2)}) collective-permute-start(f32[1,4096]{1,0:T(1,128)S(1)} %sum_x.1.refs_2_), channel_id=1, source_target_pairs={{0,16},{16,0},{32,48},{48,32},{1,17},{17,1},{33,49},{49,33},{2,18}... | collective-permute-start | bytes 49160 | tf_op jit(solution)/shard_map/ppermute | solution.py:342
  42.0 3.9 %collective-permute-start.9 = (f32[2,512]{1,0:T(2,128)S(1)}, f32[2,512]{1,0:T(2,128)S(1)}, u32[]{:S(2)}, u32[]{:S(2)}) collective-permute-start(f32[2,512]{1,0:T(2,128)S(1)} %target_core.1.refs_0_), channel_id=1, source_target_pairs={{0,4},{4,0},{1,5},{5,1},{2,6},{6,2},{3,7},{7,3},{8,12},{12,8},{9,1... | collective-permute-start | bytes 12296 | tf_op jit(solution)/shard_map/ppermute | solution.py:342
  45.9 6.0 %collective-permute-start.12 = (f32[2,512]{1,0:T(2,128)S(1)}, f32[2,512]{1,0:T(2,128)S(1)}, u32[]{:S(2)}, u32[]{:S(2)}) collective-permute-start(f32[2,512]{1,0:T(2,128)S(1)} %target_zl.1.refs_8_), channel_id=1, source_target_pairs={{0,2},{1,3},{2,0},{3,1},{4,6},{5,7},{6,4},{7,5},{8,10},{9,11},{10,... | collective-permute-start | bytes 12296 | tf_op jit(solution)/shard_map/ppermute | solution.py:342
  47.1 4.8 %collective-permute-start.11 = (f32[2,512]{1,0:T(2,128)S(1)}, f32[2,512]{1,0:T(2,128)S(1)}, u32[]{:S(2)}, u32[]{:S(2)}) collective-permute-start(f32[2,512]{1,0:T(2,128)S(1)} %target_zl.1.refs_8_), channel_id=1, source_target_pairs={{0,3},{1,2},{2,1},{3,0},{4,7},{5,6},{6,5},{7,4},{8,11},{9,10},{10,... | collective-permute-start | bytes 12296 | tf_op jit(solution)/shard_map/ppermute | solution.py:342
  49.2 3.6 %collective-permute-start.10 = (f32[2,512]{1,0:T(2,128)S(1)}, f32[2,512]{1,0:T(2,128)S(1)}, u32[]{:S(2)}, u32[]{:S(2)}) collective-permute-start(f32[2,512]{1,0:T(2,128)S(1)} %target_zl.1.refs_8_), channel_id=1, source_target_pairs={{0,1},{1,0},{2,3},{3,2},{4,5},{5,4},{6,7},{7,6},{8,9},{9,8},{10,11... | collective-permute-start | bytes 12296 | tf_op jit(solution)/shard_map/ppermute | solution.py:342
  54.5 6.7 %collective-permute-start.13 = (f32[64,1024]{1,0:T(8,128)S(1)}, f32[64,1024]{1,0:T(8,128)S(1)}, u32[]{:S(2)}, u32[]{:S(2)}) collective-permute-start(f32[64,1024]{1,0:T(8,128)S(1)} %get-tuple-element.51), channel_id=1, source_target_pairs={{0,64},{64,0},{128,192},{192,128},{1,65},{65,1},{129,193},{193,129... | collective-permute-start | bytes 786440 | tf_op jit(solution)/shard_map/ppermute | solution.py:342
  55.2 7.6 %collective-permute-start.14 = (f32[64,1024]{1,0:T(8,128)S(1)}, f32[64,1024]{1,0:T(8,128)S(1)}, u32[]{:S(2)}, u32[]{:S(2)}) collective-permute-start(f32[64,1024]{1,0:T(8,128)S(1)} %get-tuple-element.52), channel_id=1, source_target_pairs={{0,192},{64,128},{128,64},{192,0},{1,193},{65,129},{129,65},{193,1... | collective-permute-start | bytes 786440 | tf_op jit(solution)/shard_map/ppermute | solution.py:342
  57.5 5.2 %collective-permute-start.22 = (f32[512,128]{1,0:T(8,128)S(1)}, f32[512,128]{1,0:T(8,128)S(1)}, u32[]{:S(2)}, u32[]{:S(2)}) collective-permute-start(f32[512,128]{1,0:T(8,128)S(1)} %get-tuple-element.63), channel_id=1, source_target_pairs={{0,8},{8,0},{1,9},{9,1},{2,10},{10,2},{3,11},{11,3},{4,12},{12,4},... | collective-permute-start | bytes 786440 | tf_op jit(solution)/shard_map/ppermute | solution.py:342
  62.8 8.0 %collective-permute-start.23 = (f32[512,128]{1,0:T(8,128)S(1)}, f32[512,128]{1,0:T(8,128)S(1)}, u32[]{:S(2)}, u32[]{:S(2)}) collective-permute-start(f32[512,128]{1,0:T(8,128)S(1)} %embed_core.1.refs_0_), channel_id=1, source_target_pairs={{0,4},{4,0},{1,5},{5,1},{2,6},{6,2},{3,7},{7,3},{8,12},{12,8},{9,1... | collective-permute-start | bytes 786440 | tf_op jit(solution)/shard_map/ppermute | solution.py:342
  64.0 8.8 %collective-permute-start.17 = (f32[128,512]{1,0:T(8,128)S(1)}, f32[128,512]{1,0:T(8,128)S(1)}, u32[]{:S(2)}, u32[]{:S(2)}) collective-permute-start(f32[128,512]{1,0:T(8,128)S(1)} %get-tuple-element.57), channel_id=1, source_target_pairs={{0,64},{64,0},{128,192},{192,128},{1,65},{65,1},{129,193},{193,129... | collective-permute-start | bytes 786440 | tf_op jit(solution)/shard_map/ppermute | solution.py:342
  64.3 10.2 %collective-permute-start.18 = (f32[128,512]{1,0:T(8,128)S(1)}, f32[128,512]{1,0:T(8,128)S(1)}, u32[]{:S(2)}, u32[]{:S(2)}) collective-permute-start(f32[128,512]{1,0:T(8,128)S(1)} %get-tuple-element.58), channel_id=1, source_target_pairs={{0,192},{64,128},{128,64},{192,0},{1,193},{65,129},{129,65},{193,1... | collective-permute-start | bytes 786440 | tf_op jit(solution)/shard_map/ppermute | solution.py:342
  68.0 11.9 %collective-permute-start.15 = (f32[128,512]{1,0:T(8,128)S(1)}, f32[128,512]{1,0:T(8,128)S(1)}, u32[]{:S(2)}, u32[]{:S(2)}) collective-permute-start(f32[128,512]{1,0:T(8,128)S(1)} %get-tuple-element.55), channel_id=1, source_target_pairs={{0,64},{64,0},{128,192},{192,128},{1,65},{65,1},{129,193},{193,129... | collective-permute-start | bytes 786440 | tf_op jit(solution)/shard_map/ppermute | solution.py:342
  69.7 10.3 %collective-permute-start.16 = (f32[128,512]{1,0:T(8,128)S(1)}, f32[128,512]{1,0:T(8,128)S(1)}, u32[]{:S(2)}, u32[]{:S(2)}) collective-permute-start(f32[128,512]{1,0:T(8,128)S(1)} %get-tuple-element.56), channel_id=1, source_target_pairs={{0,192},{64,128},{128,64},{192,0},{1,193},{65,129},{129,65},{193,1... | collective-permute-start | bytes 786440 | tf_op jit(solution)/shard_map/ppermute | solution.py:342
  70.8 10.5 %collective-permute-start.24 = (f32[512,128]{1,0:T(8,128)S(1)}, f32[512,128]{1,0:T(8,128)S(1)}, u32[]{:S(2)}, u32[]{:S(2)}) collective-permute-start(f32[512,128]{1,0:T(8,128)S(1)} %embed_zl.1.refs_0_), channel_id=1, source_target_pairs={{0,1},{1,0},{2,3},{3,2},{4,5},{5,4},{6,7},{7,6},{8,9},{9,8},{10,11... | collective-permute-start | bytes 786440 | tf_op jit(solution)/shard_map/ppermute | solution.py:342
  74.5 8.1 %collective-permute-start.19 = (f32[128,256]{1,0:T(8,128)S(1)}, f32[128,256]{1,0:T(8,128)S(1)}, u32[]{:S(2)}, u32[]{:S(2)}) collective-permute-start(f32[128,256]{1,0:T(8,128)S(1)} %get-tuple-element.61), channel_id=1, source_target_pairs={{0,16},{16,0},{32,48},{48,32},{1,17},{17,1},{33,49},{49,33},{2,18}... | collective-permute-start | bytes 393224 | tf_op jit(solution)/shard_map/ppermute | solution.py:342
  76.1 11.1 %collective-permute-start.20 = (f32[128,256]{1,0:T(8,128)S(1)}, f32[128,256]{1,0:T(8,128)S(1)}, u32[]{:S(2)}, u32[]{:S(2)}) collective-permute-start(f32[128,256]{1,0:T(8,128)S(1)} %get-tuple-element.59.refs_3_), channel_id=1, source_target_pairs={{0,32},{16,48},{32,0},{48,16},{1,33},{17,49},{33,1},{49,17},{2,34}... | collective-permute-start | bytes 393224 | tf_op jit(solution)/shard_map/ppermute | solution.py:342
  80.0 9.2 %collective-permute-start.21 = (f32[128,256]{1,0:T(8,128)S(1)}, f32[128,256]{1,0:T(8,128)S(1)}, u32[]{:S(2)}, u32[]{:S(2)}) collective-permute-start(f32[128,256]{1,0:T(8,128)S(1)} %get-tuple-element.62), channel_id=1, source_target_pairs={{0,48},{16,32},{32,16},{48,0},{1,49},{17,33},{33,17},{49,1},{2,50}... | collective-permute-start | bytes 393224 | tf_op jit(solution)/shard_map/ppermute | solution.py:342
  81.3 7.8 %collective-permute-start.25 = (f32[512,128]{1,0:T(8,128)S(1)}, f32[512,128]{1,0:T(8,128)S(1)}, u32[]{:S(2)}, u32[]{:S(2)}) collective-permute-start(f32[512,128]{1,0:T(8,128)S(1)} %embed_y.1.refs_2_), channel_id=1, source_target_pairs={{0,3},{1,2},{2,1},{3,0},{4,7},{5,6},{6,5},{7,4},{8,11},{9,10},{10,... | collective-permute-start | bytes 786440 | tf_op jit(solution)/shard_map/ppermute | solution.py:342
  (5 other events, 18.9 us)

commit v6 on v5

--- a/solution.py
+++ b/solution.py
@@ -130,7 +130,7 @@
     half, count = own_ref.shape
     rinv = 1.0 / summed(rows_ref)
     rinv_ref[...] = rinv
-    step, rows = 2048, 64
+    step, rows = 2048, 128
     scales = [spread(rinv[p : p + 1]) for p in range(CORES)]
     for p in range(CORES):
         scale_ref[p] = scales[p]
@@ -164,9 +164,10 @@
                 at = slice(g * LANES, (g + 1) * LANES)
                 kern = kern_ref[i : i + step, at]
                 total = total + kern * kern * finv_ref[:, at]
-            acc[i : i + step] = total
-
-        t_ref[row : row + 1] = jnp.sum(acc[...].T, axis=0, keepdims=True)
+            acc[row, i : i + step] = total
+
+    for row in range(CORES):
+        t_ref[row : row + 1] = jnp.sum(acc[row].T, axis=0, keepdims=True)
 
 
 def two_terms(value):
@@ -427,7 +428,7 @@
         *kerns,
         *freq,
         prior,
-        scratch=[pltpu.VMEM((half, LANES), F32)],
+        scratch=[pltpu.VMEM((CORES, half, LANES), F32)],
         limit=20,
         name="target",
         after=squares[1:],

time: 90.1 us -> 90 us (level)
  no operation moved by 1% of the time
where the time goes in v6:
time: 90 us; the launch traced here: 89.9 us
  starting transfers between devices  35.7 us (40%)
  Pallas kernels  24.1 us (27%)
  waiting for transfers between devices  17.1 us (19%)
  blocking collectives  10.6 us (12%)
  local copies, waits for them, and re-layouts  1.52 us (2%)
    ppermute x26, starting transfers between devices, swap(): lax.ppermute(v, axis, [(i, i ^ s) for i in range(lax.axis_size(axis))])  35.7 us
    pallas_call x25, Pallas kernels, call(): pl.pallas_call(kernel, out_shape=shapes, in_specs=[VMEM] * used + [ANY] *...  24.1 us
    ppermute x26, waiting for transfers between devices, swap(): lax.ppermute(v, axis, [(i, i ^ s) for i in range(lax.axis_size(axis))])  17.1 us
    all_to_all x1, blocking collectives, over_ctr(): return lax.all_to_all(v, ('zl', 'y'), 0, 0)  10.6 us
  transfers between devices with their start and end apart: 26, of which 11 were waited for; matrix products, arithmetic and copies ran while one was open for 0% of the time, Pallas kernels for 19%

profile of v6, /device:TPU:32, one launch (start us, length us, event | category | flops | bytes accessed | tf_op | source)
XLA Modules:
  0.0 89.9 jit_solution(4927522744568927611)
XLA Ops:
  2.3 1.5 %kern_own.1 = (f32[512,4096]{1,0:T(8,128)S(1)}, f32[1,512]{1,0:T(1,128)S(1)}, bf16[144,4096]{1,0:T(8,128)(2,1)S(1)}) custom-call(f32[512,128]{1,0:T(8,128)S(1)} %widen.1.refs_0_.refs_3_, bf16[8192,128]{1,0:T(8,128)(2,1)S(1)} %copy-done), custom_call_target="tpu_custom_call" | custom-call | bytes 2359296 | tf_op jit(solution)/shard_map/kern_own/pallas_call | solution.py:329
  6.5 10.6 %all_to_all.5.refs_2_ = f32[8,2,512]{2,1,0:T(2,128)S(1)} all-to-all(f32[8,2,512]{2,1,0:T(2,128)S(1)} %sum_core.1), channel_id=1, replica_groups=mesh['x'=4,'h'=4,'core'=2,'zl'=2,'y'=4] {'zl','y'}, dimensions={0} | all-to-all | bytes 65536 | tf_op jit(solution)/shard_map/all_to_all | solution.py:360
  17.1 1.5 %freq.1 = (f32[1,4096]{1,0:T(1,128)S(1)}, f32[2,512]{1,0:T(2,128)S(1)}) custom-call(f32[512,4096]{1,0:T(8,128)S(1)} %get-tuple-element.34.refs_0_, f32[512,4096]{1,0:T(8,128)S(1)} %get-tuple-element.37.refs_1_.refs_0_, f32[8,2,512]{2,1,0:T(2,128)S(1)} %all_to_all.5.refs_2_), custom_call_target="tpu_custom_call" | custom-call | bytes 16809984 | tf_op jit(solution)/shard_map/freq/pallas_call | solution.py:329
  18.6 3.1 %collective-permute-start.4 = (f32[1,4096]{1,0:T(1,128)S(1)}, f32[1,4096]{1,0:T(1,128)S(1)}, u32[]{:S(2)}, u32[]{:S(2)}) collective-permute-start(f32[1,4096]{1,0:T(1,128)S(1)} %get-tuple-element.39.refs_0_), channel_id=1, source_target_pairs={{0,128},{64,192},{128,0},{192,64},{1,129},{65,193},{129,1},{193,65... | collective-permute-start | bytes 49160 | tf_op jit(solution)/shard_map/ppermute | solution.py:343
  22.8 2.4 %squares_own.1.refs_4_.refs_7_ = f32[512,256]{1,0:T(8,128)S(1)} custom-call(f32[512,4096]{1,0:T(8,128)S(1)} %get-tuple-element.34.refs_0_, bf16[8192,128]{1,0:T(8,128)(2,1)S(1)} %copy-done), custom_call_target="tpu_custom_call" | custom-call | flops 2147483648 | bytes 10485760 | tf_op jit(solution)/shard_map/squares_own/pallas_call | solution.py:329
  26.6 6.4 %collective-permute-start.7 = (f32[1,4096]{1,0:T(1,128)S(1)}, f32[1,4096]{1,0:T(1,128)S(1)}, u32[]{:S(2)}, u32[]{:S(2)}) collective-permute-start(f32[1,4096]{1,0:T(1,128)S(1)} %sum_x.1.refs_2_), channel_id=1, source_target_pairs={{0,32},{16,48},{32,0},{48,16},{1,33},{17,49},{33,1},{49,17},{2,34}... | collective-permute-start | bytes 49160 | tf_op jit(solution)/shard_map/ppermute | solution.py:343
  34.5 2.9 %squares_other.1 = (f32[512,256]{1,0:T(8,128)S(1)}, bf16[144,512]{1,0:T(8,128)(2,1)S(1)}, bf16[144,512]{1,0:T(8,128)(2,1)S(1)}, f32[512,128]{1,0:T(8,128)S(1)}, f32[512,128]{1,0:T(8,128)S(1)}) custom-call(f32[512,4096]{1,0:T(8,128)S(1)} %get-tuple-element.37.refs_1_.refs_0_, bf16[8192,128]{1,0:T(8,128)(2,1)S(1)} %copy-done, ...), custom_call_target="tpu_custom_call" | custom-call | flops 2147483648 | bytes 11014144 | tf_op jit(solution)/shard_map/squares_other/pallas_call | solution.py:329
  37.4 1.4 %collective-permute-done.6.refs_4_ = f32[1,4096]{1,0:T(1,128)S(1)} collective-permute-done((f32[1,4096]{1,0:T(1,128)S(1)}, f32[1,4096]{1,0:T(1,128)S(1)}, u32[]{:S(2)}, u32[]{:S(2)}) %collective-permute-start.6) | collective-permute-done | bytes 16416 | tf_op jit(solution)/shard_map/ppermute | solution.py:343
  38.9 1.8 %target.1 = (f32[2,512]{1,0:T(2,128)S(1)}, f32[1,4096]{1,0:T(1,128)S(1)}) custom-call(f32[512,4096]{1,0:T(8,128)S(1)} %get-tuple-element.34.refs_0_, f32[512,4096]{1,0:T(8,128)S(1)} %get-tuple-element.37.refs_1_.refs_0_, f32[1,4096]{1,0:T(1,128)S(1)} %sum_x.1.refs_2_, f32[1,4096]{1,0:T(1,128)S(1)} %collective-permute-done.5.refs_3_, ...), custom_call_target="tpu_custom_call" | custom-call | bytes 17399808 | tf_op jit(solution)/shard_map/target/pallas_call | solution.py:329
  43.3 2.4 %cubes.3.refs_6_ = f32[512,256]{1,0:T(8,128)S(1)} custom-call(f32[512,4096]{1,0:T(8,128)S(1)} %get-tuple-element.37.refs_1_.refs_0_, f32[1,4096]{1,0:T(1,128)S(1)} %get-tuple-element.42.refs_2_.refs_1_, bf16[8192,128]{1,0:T(8,128)(2,1)S(1)} %copy-done), custom_call_target="tpu_custom_call" | custom-call | flops 2147483648 | bytes 10502144 | tf_op jit(solution)/shard_map/cubes/pallas_call | solution.py:329
  47.0 2.1 %collective-permute-start.11 = (f32[2,512]{1,0:T(2,128)S(1)}, f32[2,512]{1,0:T(2,128)S(1)}, u32[]{:S(2)}, u32[]{:S(2)}) collective-permute-start(f32[2,512]{1,0:T(2,128)S(1)} %target_zl.1.refs_8_), channel_id=1, source_target_pairs={{0,3},{1,2},{2,1},{3,0},{4,7},{5,6},{6,5},{7,4},{8,11},{9,10},{10,... | collective-permute-start | bytes 12296 | tf_op jit(solution)/shard_map/ppermute | solution.py:343
  49.4 2.4 %cubes.2.refs_5_ = f32[512,256]{1,0:T(8,128)S(1)} custom-call(f32[512,4096]{1,0:T(8,128)S(1)} %get-tuple-element.34.refs_0_, f32[1,4096]{1,0:T(1,128)S(1)} %get-tuple-element.42.refs_2_.refs_1_, bf16[8192,128]{1,0:T(8,128)(2,1)S(1)} %copy-done), custom_call_target="tpu_custom_call" | custom-call | flops 2147483648 | bytes 10502144 | tf_op jit(solution)/shard_map/cubes/pallas_call | solution.py:329
  52.7 1.7 %grad_far.1 = (f32[64,1024]{1,0:T(8,128)S(1)}, f32[64,1024]{1,0:T(8,128)S(1)}, f32[2,512]{1,0:T(2,128)S(1)}) custom-call(f32[512,4096]{1,0:T(8,128)S(1)} %get-tuple-element.34.refs_0_, f32[512,4096]{1,0:T(8,128)S(1)} %get-tuple-element.37.refs_1_.refs_0_, f32[1,4096]{1,0:T(1,128)S(1)} %get-tuple-element.42.refs_2_.refs_1_, bf16[8192,128]{1,0:T(8,128)(2,1)S(1)} %copy-done, ...), custom_call_target="tpu_custom_call" | custom-call | bytes 19726336 | tf_op jit(solution)/shard_map/grad_far/pallas_call | solution.py:329
  55.1 2.1 %collective-permute-start.14 = (f32[64,1024]{1,0:T(8,128)S(1)}, f32[64,1024]{1,0:T(8,128)S(1)}, u32[]{:S(2)}, u32[]{:S(2)}) collective-permute-start(f32[64,1024]{1,0:T(8,128)S(1)} %get-tuple-element.52), channel_id=1, source_target_pairs={{0,192},{64,128},{128,64},{192,0},{1,193},{65,129},{129,65},{193,1... | collective-permute-start | bytes 786440 | tf_op jit(solution)/shard_map/ppermute | solution.py:343
  57.6 3.1 %grad_mid.1 = (f32[128,1024]{1,0:T(8,128)S(1)}, f32[128,1024]{1,0:T(8,128)S(1)}) custom-call(f32[512,4096]{1,0:T(8,128)S(1)} %get-tuple-element.34.refs_0_, f32[512,4096]{1,0:T(8,128)S(1)} %get-tuple-element.37.refs_1_.refs_0_, f32[1,4096]{1,0:T(1,128)S(1)} %get-tuple-element.42.refs_2_.refs_1_, bf16[8192,128]{1,0:T(8,128)(2,1)S(1)} %copy-done, ...), custom_call_target="tpu_custom_call" | custom-call | bytes 19714048 | tf_op jit(solution)/shard_map/grad_mid/pallas_call | solution.py:329
  61.1 1.6 %collective-permute-done.14.refs_12_.refs_3_ = f32[64,1024]{1,0:T(8,128)S(1)} collective-permute-done((f32[64,1024]{1,0:T(8,128)S(1)}, f32[64,1024]{1,0:T(8,128)S(1)}, u32[]{:S(2)}, u32[]{:S(2)}) %collective-permute-start.14) | collective-permute-done | bytes 262176 | tf_op jit(solution)/shard_map/ppermute | solution.py:343
  64.2 2.0 %collective-permute-start.18 = (f32[128,512]{1,0:T(8,128)S(1)}, f32[128,512]{1,0:T(8,128)S(1)}, u32[]{:S(2)}, u32[]{:S(2)}) collective-permute-start(f32[128,512]{1,0:T(8,128)S(1)} %get-tuple-element.58), channel_id=1, source_target_pairs={{0,192},{64,128},{128,64},{192,0},{1,193},{65,129},{129,65},{193,1... | collective-permute-start | bytes 786440 | tf_op jit(solution)/shard_map/ppermute | solution.py:343
  66.2 1.7 %second_b.1 = (f32[128,512]{1,0:T(8,128)S(1)}, f32[128,512]{1,0:T(8,128)S(1)}, f32[128,1024]{1,0:T(8,128)S(1)}) custom-call(f32[512,4096]{1,0:T(8,128)S(1)} %get-tuple-element.34.refs_0_, f32[512,4096]{1,0:T(8,128)S(1)} %get-tuple-element.37.refs_1_.refs_0_, f32[1,4096]{1,0:T(1,128)S(1)} %get-tuple-element.42.refs_2_.refs_1_, bf16[8192,128]{1,0:T(8,128)(2,1)S(1)} %copy-done, ...), custom_call_target="tpu_custom_call" | custom-call | flops 10000000000 | bytes 21549056 | tf_op jit(solution)/shard_map/second_b/pallas_call | solution.py:329
  67.9 1.7 %collective-permute-start.15 = (f32[128,512]{1,0:T(8,128)S(1)}, f32[128,512]{1,0:T(8,128)S(1)}, u32[]{:S(2)}, u32[]{:S(2)}) collective-permute-start(f32[128,512]{1,0:T(8,128)S(1)} %get-tuple-element.55), channel_id=1, source_target_pairs={{0,64},{64,0},{128,192},{192,128},{1,65},{65,1},{129,193},{193,129... | collective-permute-start | bytes 786440 | tf_op jit(solution)/shard_map/ppermute | solution.py:343
  72.8 1.6 %collective-permute-done.18.refs_2_ = f32[128,512]{1,0:T(8,128)S(1)} collective-permute-done((f32[128,512]{1,0:T(8,128)S(1)}, f32[128,512]{1,0:T(8,128)S(1)}, u32[]{:S(2)}, u32[]{:S(2)}) %collective-permute-start.18) | collective-permute-done | bytes 262176 | tf_op jit(solution)/shard_map/ppermute | solution.py:343
  74.5 1.6 %collective-permute-start.19 = (f32[128,256]{1,0:T(8,128)S(1)}, f32[128,256]{1,0:T(8,128)S(1)}, u32[]{:S(2)}, u32[]{:S(2)}) collective-permute-start(f32[128,256]{1,0:T(8,128)S(1)} %get-tuple-element.61), channel_id=1, source_target_pairs={{0,16},{16,0},{32,48},{48,32},{1,17},{17,1},{33,49},{49,33},{2,18}... | collective-permute-start | bytes 393224 | tf_op jit(solution)/shard_map/ppermute | solution.py:343
  76.0 3.8 %collective-permute-start.20 = (f32[128,256]{1,0:T(8,128)S(1)}, f32[128,256]{1,0:T(8,128)S(1)}, u32[]{:S(2)}, u32[]{:S(2)}) collective-permute-start(f32[128,256]{1,0:T(8,128)S(1)} %get-tuple-element.59.refs_3_), channel_id=1, source_target_pairs={{0,32},{16,48},{32,0},{48,16},{1,33},{17,49},{33,1},{49,17},{2,34}... | collective-permute-start | bytes 393224 | tf_op jit(solution)/shard_map/ppermute | solution.py:343
  82.5 4.5 %collective-permute-done.20.refs_2_ = f32[128,256]{1,0:T(8,128)S(1)} collective-permute-done((f32[128,256]{1,0:T(8,128)S(1)}, f32[128,256]{1,0:T(8,128)S(1)}, u32[]{:S(2)}, u32[]{:S(2)}) %collective-permute-start.20) | collective-permute-done | bytes 131104 | tf_op jit(solution)/shard_map/ppermute | solution.py:343
  87.1 2.0 %collective-permute-done.21.refs_1_ = f32[128,256]{1,0:T(8,128)S(1)} collective-permute-done((f32[128,256]{1,0:T(8,128)S(1)}, f32[128,256]{1,0:T(8,128)S(1)}, u32[]{:S(2)}, u32[]{:S(2)}) %collective-permute-start.21) | collective-permute-done | bytes 131104 | tf_op jit(solution)/shard_map/ppermute | solution.py:343
  (60 shorter events, 23.1 us)
Async XLA Ops:
  1.7 2.1 %collective-permute-start = (f32[512,128]{1,0:T(8,128)S(1)}, f32[512,128]{1,0:T(8,128)S(1)}, u32[]{:S(2)}, u32[]{:S(2)}) collective-permute-start(f32[512,128]{1,0:T(8,128)S(1)} %widen.1.refs_0_.refs_3_), channel_id=1, source_target_pairs={{0,8},{8,0},{1,9},{9,1},{2,10},{10,2},{3,11},{11,3},{4,12},{12,4},... | collective-permute-start | bytes 786440 | tf_op jit(solution)/shard_map/ppermute | solution.py:343
  18.6 6.7 %collective-permute-start.4 = (f32[1,4096]{1,0:T(1,128)S(1)}, f32[1,4096]{1,0:T(1,128)S(1)}, u32[]{:S(2)}, u32[]{:S(2)}) collective-permute-start(f32[1,4096]{1,0:T(1,128)S(1)} %get-tuple-element.39.refs_0_), channel_id=1, source_target_pairs={{0,128},{64,192},{128,0},{192,64},{1,129},{65,193},{129,1},{193,65... | collective-permute-start | bytes 49160 | tf_op jit(solution)/shard_map/ppermute | solution.py:343
  21.7 4.9 %collective-permute-start.3 = (f32[1,4096]{1,0:T(1,128)S(1)}, f32[1,4096]{1,0:T(1,128)S(1)}, u32[]{:S(2)}, u32[]{:S(2)}) collective-permute-start(f32[1,4096]{1,0:T(1,128)S(1)} %get-tuple-element.39.refs_0_), channel_id=1, source_target_pairs={{0,192},{64,128},{128,64},{192,0},{1,193},{65,129},{129,65},{193,1... | collective-permute-start | bytes 49160 | tf_op jit(solution)/shard_map/ppermute | solution.py:343
  22.8 3.8 %collective-permute-start.2 = (f32[1,4096]{1,0:T(1,128)S(1)}, f32[1,4096]{1,0:T(1,128)S(1)}, u32[]{:S(2)}, u32[]{:S(2)}) collective-permute-start(f32[1,4096]{1,0:T(1,128)S(1)} %get-tuple-element.39.refs_0_), channel_id=1, source_target_pairs={{0,64},{64,0},{128,192},{192,128},{1,65},{65,1},{129,193},{193,129... | collective-permute-start | bytes 49160 | tf_op jit(solution)/shard_map/ppermute | solution.py:343
  26.6 10.8 %collective-permute-start.7 = (f32[1,4096]{1,0:T(1,128)S(1)}, f32[1,4096]{1,0:T(1,128)S(1)}, u32[]{:S(2)}, u32[]{:S(2)}) collective-permute-start(f32[1,4096]{1,0:T(1,128)S(1)} %sum_x.1.refs_2_), channel_id=1, source_target_pairs={{0,32},{16,48},{32,0},{48,16},{1,33},{17,49},{33,1},{49,17},{2,34}... | collective-permute-start | bytes 49160 | tf_op jit(solution)/shard_map/ppermute | solution.py:343
  33.0 5.8 %collective-permute-start.6 = (f32[1,4096]{1,0:T(1,128)S(1)}, f32[1,4096]{1,0:T(1,128)S(1)}, u32[]{:S(2)}, u32[]{:S(2)}) collective-permute-start(f32[1,4096]{1,0:T(1,128)S(1)} %sum_x.1.refs_2_), channel_id=1, source_target_pairs={{0,48},{16,32},{32,16},{48,0},{1,49},{17,33},{33,17},{49,1},{2,50}... | collective-permute-start | bytes 49160 | tf_op jit(solution)/shard_map/ppermute | solution.py:343
  33.6 5.3 %collective-permute-start.5 = (f32[1,4096]{1,0:T(1,128)S(1)}, f32[1,4096]{1,0:T(1,128)S(1)}, u32[]{:S(2)}, u32[]{:S(2)}) collective-permute-start(f32[1,4096]{1,0:T(1,128)S(1)} %sum_x.1.refs_2_), channel_id=1, source_target_pairs={{0,16},{16,0},{32,48},{48,32},{1,17},{17,1},{33,49},{49,33},{2,18}... | collective-permute-start | bytes 49160 | tf_op jit(solution)/shard_map/ppermute | solution.py:343
  41.9 3.9 %collective-permute-start.9 = (f32[2,512]{1,0:T(2,128)S(1)}, f32[2,512]{1,0:T(2,128)S(1)}, u32[]{:S(2)}, u32[]{:S(2)}) collective-permute-start(f32[2,512]{1,0:T(2,128)S(1)} %target_core.1.refs_0_), channel_id=1, source_target_pairs={{0,4},{4,0},{1,5},{5,1},{2,6},{6,2},{3,7},{7,3},{8,12},{12,8},{9,1... | collective-permute-start | bytes 12296 | tf_op jit(solution)/shard_map/ppermute | solution.py:343
  45.8 6.0 %collective-permute-start.12 = (f32[2,512]{1,0:T(2,128)S(1)}, f32[2,512]{1,0:T(2,128)S(1)}, u32[]{:S(2)}, u32[]{:S(2)}) collective-permute-start(f32[2,512]{1,0:T(2,128)S(1)} %target_zl.1.refs_8_), channel_id=1, source_target_pairs={{0,2},{1,3},{2,0},{3,1},{4,6},{5,7},{6,4},{7,5},{8,10},{9,11},{10,... | collective-permute-start | bytes 12296 | tf_op jit(solution)/shard_map/ppermute | solution.py:343
  47.0 4.8 %collective-permute-start.11 = (f32[2,512]{1,0:T(2,128)S(1)}, f32[2,512]{1,0:T(2,128)S(1)}, u32[]{:S(2)}, u32[]{:S(2)}) collective-permute-start(f32[2,512]{1,0:T(2,128)S(1)} %target_zl.1.refs_8_), channel_id=1, source_target_pairs={{0,3},{1,2},{2,1},{3,0},{4,7},{5,6},{6,5},{7,4},{8,11},{9,10},{10,... | collective-permute-start | bytes 12296 | tf_op jit(solution)/shard_map/ppermute | solution.py:343
  49.1 3.6 %collective-permute-start.10 = (f32[2,512]{1,0:T(2,128)S(1)}, f32[2,512]{1,0:T(2,128)S(1)}, u32[]{:S(2)}, u32[]{:S(2)}) collective-permute-start(f32[2,512]{1,0:T(2,128)S(1)} %target_zl.1.refs_8_), channel_id=1, source_target_pairs={{0,1},{1,0},{2,3},{3,2},{4,5},{5,4},{6,7},{7,6},{8,9},{9,8},{10,11... | collective-permute-start | bytes 12296 | tf_op jit(solution)/shard_map/ppermute | solution.py:343
  54.4 6.7 %collective-permute-start.13 = (f32[64,1024]{1,0:T(8,128)S(1)}, f32[64,1024]{1,0:T(8,128)S(1)}, u32[]{:S(2)}, u32[]{:S(2)}) collective-permute-start(f32[64,1024]{1,0:T(8,128)S(1)} %get-tuple-element.51), channel_id=1, source_target_pairs={{0,64},{64,0},{128,192},{192,128},{1,65},{65,1},{129,193},{193,129... | collective-permute-start | bytes 786440 | tf_op jit(solution)/shard_map/ppermute | solution.py:343
  55.1 7.6 %collective-permute-start.14 = (f32[64,1024]{1,0:T(8,128)S(1)}, f32[64,1024]{1,0:T(8,128)S(1)}, u32[]{:S(2)}, u32[]{:S(2)}) collective-permute-start(f32[64,1024]{1,0:T(8,128)S(1)} %get-tuple-element.52), channel_id=1, source_target_pairs={{0,192},{64,128},{128,64},{192,0},{1,193},{65,129},{129,65},{193,1... | collective-permute-start | bytes 786440 | tf_op jit(solution)/shard_map/ppermute | solution.py:343
  57.5 5.2 %collective-permute-start.22 = (f32[512,128]{1,0:T(8,128)S(1)}, f32[512,128]{1,0:T(8,128)S(1)}, u32[]{:S(2)}, u32[]{:S(2)}) collective-permute-start(f32[512,128]{1,0:T(8,128)S(1)} %get-tuple-element.63), channel_id=1, source_target_pairs={{0,8},{8,0},{1,9},{9,1},{2,10},{10,2},{3,11},{11,3},{4,12},{12,4},... | collective-permute-start | bytes 786440 | tf_op jit(solution)/shard_map/ppermute | solution.py:343
  62.7 8.0 %collective-permute-start.23 = (f32[512,128]{1,0:T(8,128)S(1)}, f32[512,128]{1,0:T(8,128)S(1)}, u32[]{:S(2)}, u32[]{:S(2)}) collective-permute-start(f32[512,128]{1,0:T(8,128)S(1)} %embed_core.1.refs_0_), channel_id=1, source_target_pairs={{0,4},{4,0},{1,5},{5,1},{2,6},{6,2},{3,7},{7,3},{8,12},{12,8},{9,1... | collective-permute-start | bytes 786440 | tf_op jit(solution)/shard_map/ppermute | solution.py:343
  64.0 8.8 %collective-permute-start.17 = (f32[128,512]{1,0:T(8,128)S(1)}, f32[128,512]{1,0:T(8,128)S(1)}, u32[]{:S(2)}, u32[]{:S(2)}) collective-permute-start(f32[128,512]{1,0:T(8,128)S(1)} %get-tuple-element.57), channel_id=1, source_target_pairs={{0,64},{64,0},{128,192},{192,128},{1,65},{65,1},{129,193},{193,129... | collective-permute-start | bytes 786440 | tf_op jit(solution)/shard_map/ppermute | solution.py:343
  64.2 10.2 %collective-permute-start.18 = (f32[128,512]{1,0:T(8,128)S(1)}, f32[128,512]{1,0:T(8,128)S(1)}, u32[]{:S(2)}, u32[]{:S(2)}) collective-permute-start(f32[128,512]{1,0:T(8,128)S(1)} %get-tuple-element.58), channel_id=1, source_target_pairs={{0,192},{64,128},{128,64},{192,0},{1,193},{65,129},{129,65},{193,1... | collective-permute-start | bytes 786440 | tf_op jit(solution)/shard_map/ppermute | solution.py:343
  67.9 11.9 %collective-permute-start.15 = (f32[128,512]{1,0:T(8,128)S(1)}, f32[128,512]{1,0:T(8,128)S(1)}, u32[]{:S(2)}, u32[]{:S(2)}) collective-permute-start(f32[128,512]{1,0:T(8,128)S(1)} %get-tuple-element.55), channel_id=1, source_target_pairs={{0,64},{64,0},{128,192},{192,128},{1,65},{65,1},{129,193},{193,129... | collective-permute-start | bytes 786440 | tf_op jit(solution)/shard_map/ppermute | solution.py:343
  69.6 10.3 %collective-permute-start.16 = (f32[128,512]{1,0:T(8,128)S(1)}, f32[128,512]{1,0:T(8,128)S(1)}, u32[]{:S(2)}, u32[]{:S(2)}) collective-permute-start(f32[128,512]{1,0:T(8,128)S(1)} %get-tuple-element.56), channel_id=1, source_target_pairs={{0,192},{64,128},{128,64},{192,0},{1,193},{65,129},{129,65},{193,1... | collective-permute-start | bytes 786440 | tf_op jit(solution)/shard_map/ppermute | solution.py:343
  70.8 10.4 %collective-permute-start.24 = (f32[512,128]{1,0:T(8,128)S(1)}, f32[512,128]{1,0:T(8,128)S(1)}, u32[]{:S(2)}, u32[]{:S(2)}) collective-permute-start(f32[512,128]{1,0:T(8,128)S(1)} %embed_zl.1.refs_0_), channel_id=1, source_target_pairs={{0,1},{1,0},{2,3},{3,2},{4,5},{5,4},{6,7},{7,6},{8,9},{9,8},{10,11... | collective-permute-start | bytes 786440 | tf_op jit(solution)/shard_map/ppermute | solution.py:343
  74.5 8.1 %collective-permute-start.19 = (f32[128,256]{1,0:T(8,128)S(1)}, f32[128,256]{1,0:T(8,128)S(1)}, u32[]{:S(2)}, u32[]{:S(2)}) collective-permute-start(f32[128,256]{1,0:T(8,128)S(1)} %get-tuple-element.61), channel_id=1, source_target_pairs={{0,16},{16,0},{32,48},{48,32},{1,17},{17,1},{33,49},{49,33},{2,18}... | collective-permute-start | bytes 393224 | tf_op jit(solution)/shard_map/ppermute | solution.py:343
  76.0 11.1 %collective-permute-start.20 = (f32[128,256]{1,0:T(8,128)S(1)}, f32[128,256]{1,0:T(8,128)S(1)}, u32[]{:S(2)}, u32[]{:S(2)}) collective-permute-start(f32[128,256]{1,0:T(8,128)S(1)} %get-tuple-element.59.refs_3_), channel_id=1, source_target_pairs={{0,32},{16,48},{32,0},{48,16},{1,33},{17,49},{33,1},{49,17},{2,34}... | collective-permute-start | bytes 393224 | tf_op jit(solution)/shard_map/ppermute | solution.py:343
  79.9 9.2 %collective-permute-start.21 = (f32[128,256]{1,0:T(8,128)S(1)}, f32[128,256]{1,0:T(8,128)S(1)}, u32[]{:S(2)}, u32[]{:S(2)}) collective-permute-start(f32[128,256]{1,0:T(8,128)S(1)} %get-tuple-element.62), channel_id=1, source_target_pairs={{0,48},{16,32},{32,16},{48,0},{1,49},{17,33},{33,17},{49,1},{2,50}... | collective-permute-start | bytes 393224 | tf_op jit(solution)/shard_map/ppermute | solution.py:343
  81.2 7.9 %collective-permute-start.25 = (f32[512,128]{1,0:T(8,128)S(1)}, f32[512,128]{1,0:T(8,128)S(1)}, u32[]{:S(2)}, u32[]{:S(2)}) collective-permute-start(f32[512,128]{1,0:T(8,128)S(1)} %embed_y.1.refs_2_), channel_id=1, source_target_pairs={{0,3},{1,2},{2,1},{3,0},{4,7},{5,6},{6,5},{7,4},{8,11},{9,10},{10,... | collective-permute-start | bytes 786440 | tf_op jit(solution)/shard_map/ppermute | solution.py:343
  (5 other events, 18.9 us)
